TPU v7x, 32 devices: a whole 2x2x4 slice. The times are simulated.
32 devices in a mesh: batch: 4 (over y, x), seq: 2 (over core), tensor: 4 (over z).
Axes of the slice: x: 2, y: 2, z: 4, core: 2. Of those that a mesh axis runs over, the one named last changes fastest.
Arguments:
- layer_in: bfloat16 [4, 1024, 2304], P('batch', 'seq'), may hold values from -6 to 6
- cotangent: bfloat16 [4, 1024, 2304], P('batch', 'seq'), may hold values from -6 to 6
- qkv_weight: float32 [2304, 4, 1024], P(('batch', 'seq'), 'tensor')
- out_weight: float32 [2048, 2304], P('tensor', ('batch', 'seq')), may hold values from -0.125 to 0.125
- gate_up_weight: float32 [2304, 2, 9216], P(('batch', 'seq'), None, 'tensor'), may hold values from -0.125 to 0.125
- down_weight: float32 [9216, 2304], P('tensor', ('batch', 'seq')), may hold values from -0.0625 to 0.0625
- norm_gains: float32 [4, 2304], P(None, ('batch', 'seq')), may hold values from -0.1 to 0.1
- qkv_first: float32 [2304, 4, 1024], P(('batch', 'seq'), 'tensor'), may hold values from -40 to 40
- out_first: float32 [2048, 2304], P('tensor', ('batch', 'seq')), may hold values from -112 to 112
- gate_up_first: float32 [2304, 2, 9216], P(('batch', 'seq'), None, 'tensor'), may hold values from -40 to 40
- down_first: float32 [9216, 2304], P('tensor', ('batch', 'seq')), may hold values from -80 to 80
- gains_first: float32 [4, 2304], P(None, ('batch', 'seq')), may hold values from -80 to 80
- qkv_second: float32 [2304, 4, 1024], P(('batch', 'seq'), 'tensor'), may hold values from 51.2 to 204.8
- out_second: float32 [2048, 2304], P('tensor', ('batch', 'seq')), may hold values from 409.6 to 1638.4
- gate_up_second: float32 [2304, 2, 9216], P(('batch', 'seq'), None, 'tensor'), may hold values from 51.2 to 204.8
- down_second: float32 [9216, 2304], P('tensor', ('batch', 'seq')), may hold values from 204.8 to 819.2
- gains_second: float32 [4, 2304], P(None, ('batch', 'seq')), may hold values from 102.4 to 409.6
Outputs:
- layer_out: bfloat16 [4, 1024, 2304], P('batch', 'seq')
- input_grad: float32 [4, 1024, 2304], P('batch', 'seq')
- qkv_grad: float32 [2304, 4, 1024], P(('batch', 'seq'), 'tensor')
- out_grad: float32 [2048, 2304], P('tensor', ('batch', 'seq'))
- gate_up_grad: float32 [2304, 2, 9216], P(('batch', 'seq'), None, 'tensor')
- down_grad: float32 [9216, 2304], P('tensor', ('batch', 'seq'))
- gains_grad: float32 [4, 2304], P(None, ('batch', 'seq'))
- qkv_weight_new: float32 [2304, 4, 1024], P(('batch', 'seq'), 'tensor')
- out_weight_new: float32 [2048, 2304], P('tensor', ('batch', 'seq'))
- gate_up_weight_new: float32 [2304, 2, 9216], P(('batch', 'seq'), None, 'tensor')
- down_weight_new: float32 [9216, 2304], P('tensor', ('batch', 'seq'))
- norm_gains_new: float32 [4, 2304], P(None, ('batch', 'seq'))
- qkv_first_new: float32 [2304, 4, 1024], P(('batch', 'seq'), 'tensor')
- out_first_new: float32 [2048, 2304], P('tensor', ('batch', 'seq'))
- gate_up_first_new: float32 [2304, 2, 9216], P(('batch', 'seq'), None, 'tensor')
- down_first_new: float32 [9216, 2304], P('tensor', ('batch', 'seq'))
- gains_first_new: float32 [4, 2304], P(None, ('batch', 'seq'))
- qkv_second_new: float32 [2304, 4, 1024], P(('batch', 'seq'), 'tensor')
- out_second_new: float32 [2048, 2304], P('tensor', ('batch', 'seq'))
- gate_up_second_new: float32 [2304, 2, 9216], P(('batch', 'seq'), None, 'tensor')
- down_second_new: float32 [9216, 2304], P('tensor', ('batch', 'seq'))
- gains_second_new: float32 [4, 2304], P(None, ('batch', 'seq'))
All inputs are finite; a program needn't handle non-finite values.
Results may differ from a plain program's by a relative error of at most 0.025.
Values may be sent and summed in bfloat16 or wider, within the bound.
No kernel may reach another device: no remote copies, remote signals or barrier semaphores. Data moves between devices by JAX's collectives and lax.ppermute only.
A program may use at most 320 MiB of HBM per device.

v0:
```python
import jax
import jax.numpy as jnp
from jax import lax
from jax.sharding import PartitionSpec as P

HEAD_DIM = 256
WIN_BLOCKS = 4
STEP = 10
GROUP = 2


norm_eps = 1e-06
soft_cap = 50.0
learn_rate = 0.02
decay_rate = 0.1
beta_first = 0.9
beta_second = 0.95
adam_eps = 1e-08
gelu_coef = 0.7978845608028654


def from_behind(value, axis, steps):
    count = lax.axis_size(axis)
    initial, last = (max(0, -steps), min(count, count - steps))
    return lax.ppermute(value, axis, [(source, source + steps) for source in range(initial, last)])


def rms_norm(values, gain):
    scale = lax.rsqrt(jnp.mean(values * values, axis=-1, keepdims=True) + norm_eps)
    return values * scale * (1.0 + gain)


def norm_back(values, gain, upstream):
    _, pullback = jax.vjp(rms_norm, values, gain)
    return pullback(upstream)


def gelu_tanh(values):
    inner = gelu_coef * (values + 0.044715 * values * values * values)
    return 0.5 * values * (1.0 + jnp.tanh(inner))


def geglu(gate, up_part):
    return gelu_tanh(gate) * up_part


def rope_tables(positions, head_size):
    half = head_size // 2
    exponent = jnp.arange(half, dtype=jnp.float32) * (2.0 / head_size)
    freqs = 10000.0 ** (-exponent)
    angles = positions.astype(jnp.float32)[:, None] * freqs[None, :]
    return (jnp.cos(angles), jnp.sin(angles))


def rotate(values, cosine, sine):
    half = values.shape[-1] // 2
    first = values[..., :half]
    second = values[..., half:]
    cosine = cosine[:, None, :]
    sine = sine[:, None, :]
    return jnp.concatenate(
        [first * cosine - second * sine, second * cosine + first * sine], axis=-1
    )


def adam_step(weight, grad, first, second, decay):
    first_new = beta_first * first + (1.0 - beta_first) * grad
    second_new = beta_second * second + (1.0 - beta_second) * grad * grad
    first_hat = first_new / (1.0 - beta_first**STEP)
    second_hat = second_new / (1.0 - beta_second**STEP)
    weight_new = weight - learn_rate * (
        first_hat / (jnp.sqrt(second_hat) + adam_eps) + decay * weight
    )
    return (weight_new, first_new, second_new)


def rows_product(left, right):
    return lax.dot_general(
        left, right, (((0,), (0,)), ((), ())), preferred_element_type=jnp.float32
    )


def cols_product(left, right):
    return lax.dot_general(
        left, right, (((1,), (1,)), ((), ())), preferred_element_type=jnp.float32
    )


def capped_scores(query_groups, ext_keys):
    raw = jnp.einsum(
        "icgd,jcd->cgij", query_groups, ext_keys, preferred_element_type=jnp.float32
    ) * query_groups.shape[-1] ** (-0.5)
    return soft_cap * jnp.tanh(raw / soft_cap)


def on_device(
    layer_in,
    cotangent,
    qkv_weight,
    out_weight,
    gate_up_weight,
    down_weight,
    norm_gains,
    qkv_first,
    out_first,
    gate_up_first,
    down_first,
    gains_first,
    qkv_second,
    out_second,
    gate_up_second,
    down_second,
    gains_second,
):
    tok_rows = layer_in.shape[1]
    seq_index = lax.axis_index("seq")
    collected = (
        lax.all_gather(qkv_weight.astype(jnp.bfloat16), ("batch", "seq"), axis=0, tiled=True),
        lax.all_gather(out_weight.astype(jnp.bfloat16), ("batch", "seq"), axis=1, tiled=True),
        lax.all_gather(gate_up_weight.astype(jnp.bfloat16), ("batch", "seq"), axis=0, tiled=True),
        lax.all_gather(down_weight.astype(jnp.bfloat16), ("batch", "seq"), axis=1, tiled=True),
        lax.all_gather(norm_gains.astype(jnp.bfloat16), ("batch", "seq"), axis=1, tiled=True),
    )
    qkv_full, out_full, gate_up_full, down_full, gains_full = collected
    model_width = qkv_full.shape[0]
    kv_local = qkv_full.shape[1]
    heads_local = kv_local * GROUP
    ffn_local = gate_up_full.shape[2]
    qkv_flat = qkv_full.reshape(model_width, kv_local * (GROUP + 2) * HEAD_DIM)
    gate_up_flat = gate_up_full.reshape(model_width, 2 * ffn_local)
    gains_float = gains_full.astype(jnp.float32)
    positions = seq_index * tok_rows + jnp.arange(tok_rows, dtype=jnp.int32)
    cosine, sine = rope_tables(positions, HEAD_DIM)
    key_positions = (seq_index - WIN_BLOCKS) * tok_rows + jnp.arange(
        (WIN_BLOCKS + 1) * tok_rows, dtype=jnp.int32
    )
    spread = positions[:, None] - key_positions[None, :]
    allowed = (spread >= 0) & (spread < WIN_BLOCKS * tok_rows) & (key_positions >= 0)[None, :]
    mask = allowed[None, None]
    stream = layer_in[0].astype(jnp.float32)
    attn_in = rms_norm(stream, gains_float[0]).astype(jnp.bfloat16)
    projected = jnp.dot(attn_in, qkv_flat, preferred_element_type=jnp.float32).reshape(
        tok_rows, kv_local, GROUP + 2, HEAD_DIM
    )
    queries = rotate(
        projected[:, :, :GROUP].reshape(tok_rows, heads_local, HEAD_DIM), cosine, sine
    ).astype(jnp.bfloat16)
    keys = rotate(projected[:, :, GROUP], cosine, sine).astype(jnp.bfloat16)
    values = projected[:, :, GROUP + 1].astype(jnp.bfloat16)
    kv_pair = jnp.stack([keys, values], axis=0)
    reach = min(WIN_BLOCKS, lax.axis_size("seq") - 1)
    pieces = []
    for distance in range(WIN_BLOCKS, 0, -1):
        if distance <= reach:
            pieces.append(from_behind(kv_pair, "seq", distance))
        else:
            pieces.append(jnp.zeros_like(kv_pair))
    pieces.append(kv_pair)
    extended = jnp.concatenate(pieces, axis=1)
    ext_keys = extended[0]
    ext_values = extended[1]
    query_groups = queries.reshape(tok_rows, kv_local, GROUP, HEAD_DIM)
    capped = capped_scores(query_groups, ext_keys)
    log_sums = jnp.log(jnp.sum(jnp.where(mask, jnp.exp(capped), 0.0), axis=-1))
    probs = jnp.where(mask, jnp.exp(capped - log_sums[..., None]), 0.0).astype(jnp.bfloat16)
    attended = jnp.einsum(
        "cgij,jcd->icgd", probs, ext_values, preferred_element_type=jnp.float32
    ).astype(jnp.bfloat16)
    att_flat = attended.reshape(tok_rows, heads_local * HEAD_DIM)
    attn_out = lax.psum(jnp.dot(att_flat, out_full, preferred_element_type=jnp.float32), "tensor")
    mid_stream = stream + rms_norm(attn_out, gains_float[1])
    ffn_in = rms_norm(mid_stream, gains_float[2]).astype(jnp.bfloat16)
    gate_up = jnp.dot(ffn_in, gate_up_flat, preferred_element_type=jnp.float32).reshape(
        tok_rows, 2, ffn_local
    )
    hidden = geglu(gate_up[:, 0], gate_up[:, 1]).astype(jnp.bfloat16)
    ffn_out = lax.psum(jnp.dot(hidden, down_full, preferred_element_type=jnp.float32), "tensor")
    layer_out = (mid_stream + rms_norm(ffn_out, gains_float[3])).astype(jnp.bfloat16)
    grad_top = cotangent[0].astype(jnp.float32)
    grad_ffn_out, gain_three = norm_back(ffn_out, gains_float[3], grad_top)
    grad_ffn = grad_ffn_out.astype(jnp.bfloat16)
    grad_hidden = cols_product(grad_ffn, down_full)
    _, geglu_pull = jax.vjp(geglu, gate_up[:, 0], gate_up[:, 1])
    grad_gate, grad_up = geglu_pull(grad_hidden)
    grad_gate_up = (
        jnp.stack([grad_gate, grad_up], axis=1)
        .reshape(tok_rows, 2 * ffn_local)
        .astype(jnp.bfloat16)
    )
    grad_ffn_in = lax.psum(cols_product(grad_gate_up, gate_up_flat), "tensor")
    grad_mid_norm, gain_two = norm_back(mid_stream, gains_float[2], grad_ffn_in)
    grad_mid = grad_top + grad_mid_norm
    grad_attn_out, gain_one = norm_back(attn_out, gains_float[1], grad_mid)
    grad_attn = grad_attn_out.astype(jnp.bfloat16)
    grad_att = (
        cols_product(grad_attn, out_full)
        .astype(jnp.bfloat16)
        .reshape(tok_rows, kv_local, GROUP, HEAD_DIM)
    )
    capped_again = capped_scores(query_groups, ext_keys)
    probs_float = jnp.where(mask, jnp.exp(capped_again - log_sums[..., None]), 0.0)
    probs_again = probs_float.astype(jnp.bfloat16)
    delta = jnp.einsum("icgd,icgd->cgi", grad_att, attended, preferred_element_type=jnp.float32)
    grad_probs = jnp.einsum(
        "icgd,jcd->cgij", grad_att, ext_values, preferred_element_type=jnp.float32
    )
    grad_scores = (
        probs_float * (grad_probs - delta[..., None]) * (1.0 - (capped_again / soft_cap) ** 2)
    ).astype(jnp.bfloat16)
    score_scale = HEAD_DIM ** (-0.5)
    grad_values_ext = jnp.einsum(
        "cgij,icgd->jcd", probs_again, grad_att, preferred_element_type=jnp.float32
    )
    grad_keys_ext = (
        jnp.einsum("cgij,icgd->jcd", grad_scores, query_groups, preferred_element_type=jnp.float32)
        * score_scale
    )
    grad_queries = (
        jnp.einsum("cgij,jcd->icgd", grad_scores, ext_keys, preferred_element_type=jnp.float32)
        * score_scale
    )
    grad_pair_ext = jnp.stack([grad_keys_ext, grad_values_ext], axis=0)
    grad_pair = grad_pair_ext[:, WIN_BLOCKS * tok_rows :]
    for distance in range(1, reach + 1):
        start = (WIN_BLOCKS - distance) * tok_rows
        piece = grad_pair_ext[:, start : start + tok_rows]
        grad_pair = grad_pair + from_behind(piece.astype(jnp.bfloat16), "seq", -distance).astype(
            piece.dtype
        )
    grad_queries = rotate(
        grad_queries.reshape(tok_rows, heads_local, HEAD_DIM), cosine, -sine
    ).reshape(tok_rows, kv_local, GROUP, HEAD_DIM)
    grad_keys = rotate(grad_pair[0], cosine, -sine)
    grad_values = grad_pair[1]
    grad_proj = (
        jnp.concatenate([grad_queries, grad_keys[:, :, None], grad_values[:, :, None]], axis=2)
        .reshape(tok_rows, kv_local * (GROUP + 2) * HEAD_DIM)
        .astype(jnp.bfloat16)
    )
    grad_attn_in = lax.psum(
        cols_product(grad_proj, qkv_flat).astype(jnp.bfloat16), "tensor"
    ).astype(jnp.float32)
    grad_stream_norm, gain_zero = norm_back(stream, gains_float[0], grad_attn_in)
    input_grad = grad_mid + grad_stream_norm
    qkv_local = rows_product(attn_in, grad_proj).reshape(
        model_width, kv_local, (GROUP + 2) * HEAD_DIM
    )
    out_local = rows_product(att_flat, grad_attn)
    gate_up_local = rows_product(ffn_in, grad_gate_up).reshape(model_width, 2, ffn_local)
    down_local = rows_product(hidden, grad_ffn)
    gains_local = jnp.stack([gain_zero, gain_one, gain_two, gain_three])
    summed = (
        lax.psum_scatter(
            qkv_local.astype(jnp.bfloat16), ("batch", "seq"), scatter_dimension=0, tiled=True
        ).astype(jnp.float32),
        lax.psum_scatter(
            out_local.astype(jnp.bfloat16), ("batch", "seq"), scatter_dimension=1, tiled=True
        ).astype(jnp.float32),
        lax.psum_scatter(
            gate_up_local.astype(jnp.bfloat16), ("batch", "seq"), scatter_dimension=0, tiled=True
        ).astype(jnp.float32),
        lax.psum_scatter(
            down_local.astype(jnp.bfloat16), ("batch", "seq"), scatter_dimension=1, tiled=True
        ).astype(jnp.float32),
        lax.psum_scatter(
            gains_local.astype(jnp.bfloat16), ("batch", "seq"), scatter_dimension=1, tiled=True
        ).astype(jnp.float32),
    )
    qkv_grad, out_grad, gate_up_grad, down_grad, gains_grad = summed
    qkv_new, qkv_first_new, qkv_second_new = adam_step(
        qkv_weight, qkv_grad, qkv_first, qkv_second, decay_rate
    )
    out_new, out_first_new, out_second_new = adam_step(
        out_weight, out_grad, out_first, out_second, decay_rate
    )
    gate_up_new, gate_up_first_new, gate_up_second_new = adam_step(
        gate_up_weight, gate_up_grad, gate_up_first, gate_up_second, decay_rate
    )
    down_new, down_first_new, down_second_new = adam_step(
        down_weight, down_grad, down_first, down_second, decay_rate
    )
    gains_new, gains_first_new, gains_second_new = adam_step(
        norm_gains, gains_grad, gains_first, gains_second, 0.0
    )
    return (
        layer_out[None],
        input_grad[None],
        qkv_grad,
        out_grad,
        gate_up_grad,
        down_grad,
        gains_grad,
        qkv_new,
        out_new,
        gate_up_new,
        down_new,
        gains_new,
        qkv_first_new,
        out_first_new,
        gate_up_first_new,
        down_first_new,
        gains_first_new,
        qkv_second_new,
        out_second_new,
        gate_up_second_new,
        down_second_new,
        gains_second_new,
    )


def solution(mesh):
    in_specs = (
        P("batch", "seq", None),
        P("batch", "seq", None),
        P(("batch", "seq"), "tensor", None),
        P("tensor", ("batch", "seq")),
        P(("batch", "seq"), None, "tensor"),
        P("tensor", ("batch", "seq")),
        P(None, ("batch", "seq")),
        P(("batch", "seq"), "tensor", None),
        P("tensor", ("batch", "seq")),
        P(("batch", "seq"), None, "tensor"),
        P("tensor", ("batch", "seq")),
        P(None, ("batch", "seq")),
        P(("batch", "seq"), "tensor", None),
        P("tensor", ("batch", "seq")),
        P(("batch", "seq"), None, "tensor"),
        P("tensor", ("batch", "seq")),
        P(None, ("batch", "seq")),
    )
    out_specs = (
        P("batch", "seq", None),
        P("batch", "seq", None),
        P(("batch", "seq"), "tensor", None),
        P("tensor", ("batch", "seq")),
        P(("batch", "seq"), None, "tensor"),
        P("tensor", ("batch", "seq")),
        P(None, ("batch", "seq")),
        P(("batch", "seq"), "tensor", None),
        P("tensor", ("batch", "seq")),
        P(("batch", "seq"), None, "tensor"),
        P("tensor", ("batch", "seq")),
        P(None, ("batch", "seq")),
        P(("batch", "seq"), "tensor", None),
        P("tensor", ("batch", "seq")),
        P(("batch", "seq"), None, "tensor"),
        P("tensor", ("batch", "seq")),
        P(None, ("batch", "seq")),
        P(("batch", "seq"), "tensor", None),
        P("tensor", ("batch", "seq")),
        P(("batch", "seq"), None, "tensor"),
        P("tensor", ("batch", "seq")),
        P(None, ("batch", "seq")),
    )
    return jax.shard_map(
        on_device, mesh=mesh, in_specs=in_specs, out_specs=out_specs, check_vma=False
    )
```

profile of v0, /device:TPU:0, one launch (start us, length us, event | category | flops | bytes accessed | tf_op | source)
XLA Modules:
  0.0 1394.6 jit_solution(9745958846151239119)
XLA Ops:
  12.4 10.5 all-gather
  29.0 23.1 %all-gather.6.cloned.1.call-done = bf16[2304,1,1024]{2,0,1:T(8,128)(2,1)} async-done(((bf16[288,1,1024]{2,0,1:T(8,128)(2,1)}), bf16[2304,1,1024]{2,0,1:T(8,128)(2,1)}) %all-gather.6.cloned.1.call-update) | async-done | bytes 4718608 | tf_op jit(solution)/shard_map/all_gather | solution.py:118
  52.1 6.6 copy.135
  75.1 5.9 fusion.5
  102.6 163.7 %all-reduce.5.cloned.1.call-done = f32[512,2304]{1,0:T(8,128)} async-done(((f32[512,2304]{1,0:T(8,128)}), f32[512,2304]{1,0:T(8,128)}) %all-reduce.5.cloned.1.call-update) | async-done | bytes 4718608 | tf_op jit(solution)/shard_map/psum | solution.py:170
  273.4 103.1 %all-gather.10.cloned.1.call-done = bf16[2304,2,2304]{2,0,1:T(8,128)(2,1)} async-done(((bf16[288,2,2304]{2,0,1:T(8,128)(2,1)}), bf16[2304,2,2304]{2,0,1:T(8,128)(2,1)}) %all-gather.10.cloned.1.call-update) | async-done | bytes 21233680 | tf_op jit(solution)/shard_map/all_gather | solution.py:120
  376.5 28.9 %copy.142 = bf16[2304,2,2304]{0,2,1:T(8,128)(2,1)} copy(bf16[2304,2,2304]{2,0,1:T(8,128)(2,1)} %all-gather.10.cloned.1.call-done) | data formatting | bytes 42467328 | tf_op jit(solution)/shard_map/all_gather | solution.py:120
  405.3 19.6 %fusion = f32[512,2,2304]{2,0,1:T(8,128)} fusion(bf16[2304,2,2304]{0,2,1:T(8,128)(2,1)} %copy.142, f32[512,2304]{1,0:T(8,128)} %get-tuple-element.142, f32[2304]{0:T(1024)S(1)} %get-tuple-element.119, f32[512]{0:T(512)S(1)} %fusion.116), kind=kOutput, calls=%fused_computation.1 | convolution fusion | flops 10875174912 | bytes 35400704 | tf_op jit(solution)/shard_map/dot_general | solution.py:173
  424.9 5.7 multiply_convert_fusion
  430.6 12.0 all-gather.12.cloned.1.call-done
  442.6 11.7 fusion.132
  454.8 171.6 %all-reduce.7.cloned.1.call-done = f32[512,2304]{1,0:T(8,128)} async-done(((f32[512,2304]{1,0:T(8,128)}), f32[512,2304]{1,0:T(8,128)}) %all-reduce.7.cloned.1.call-update) | async-done | bytes 4718608 | tf_op jit(solution)/shard_map/psum | solution.py:177
  638.8 13.2 fusion.37
  654.3 15.7 %convolution_bitcast_fusion = f32[512,2304]{1,0:T(8,128)} fusion(bf16[2304,2,2304]{2,0,1:T(8,128)(2,1)} %all-gather.10.cloned.1.call-done, bf16[512,1,2304]{2,0,1:T(8,128)(2,1)S(1)} %get-tuple-element.144, bf16[512,1,2304]{2,0,1:T(8,128)(2,1)S(1)} %get-tuple-element.143), kind=kOutput, calls=%fused_computation.60 | convolution fusion | flops 10873995264 | bytes 30670848 | tf_op jit(solution)/shard_map/dot_general | solution.py:84
  670.2 170.9 %all-reduce.9.cloned.1.call-done = f32[512,2304]{1,0:T(8,128)} async-done(((f32[512,2304]{1,0:T(8,128)}), f32[512,2304]{1,0:T(8,128)}) %all-reduce.9.cloned.1.call-update) | async-done | bytes 4718608 | tf_op jit(solution)/shard_map/psum | solution.py:190
  846.3 6.7 multiply_reduce_fusion.1
  858.6 6.6 convolution_bitcast_fusion.1
  865.3 7.9 fusion.2
  884.9 95.5 %all-reduce.11.cloned.1.call-done = bf16[512,2304]{1,0:T(8,128)(2,1)} async-done(((bf16[512,2304]{1,0:T(8,128)(2,1)}), bf16[512,2304]{1,0:T(8,128)(2,1)}) %all-reduce.11.cloned.1.call-update) | async-done | bytes 2359312 | tf_op jit(solution)/shard_map/psum | solution.py:240
  994.8 10.4 convolution_convert_fusion.1
  1010.4 6.6 copy.148
  1017.1 19.1 %convolution_convert_fusion = bf16[2304,2,2304]{2,0,1:T(8,128)(2,1)} fusion(bf16[512,2,2304]{0,2,1:T(8,128)(2,1)} %copy.148, f32[512,2304]{1,0:T(8,128)} %get-tuple-element.142, f32[2304]{0:T(1024)S(1)} %get-tuple-element.119, f32[512]{0:T(512)S(1)} %fusion.116), kind=kOutput, calls=%fused_computation | convolution fusion | flops 10885791744 | bytes 30682112 | tf_op jit(solution)/shard_map/dot_general | solution.py:78
  1036.8 6.7 fusion.43
  1046.0 19.1 %reduce-scatter.10.cloned.1.call-done = bf16[512,288]{0,1:T(8,128)(2,1)} async-done(((bf16[512,2304]{0,1:T(8,128)(2,1)}), bf16[512,288]{0,1:T(8,128)(2,1)}) %reduce-scatter.10.cloned.1.call-update) | async-done | bytes 294928 | tf_op jit(solution)/shard_map/reduce_scatter | solution.py:256
  1067.8 55.6 %reduce-scatter.8.cloned.1.call-done = bf16[288,1,1024]{2,0,1:T(8,128)(2,1)} async-done(((bf16[2304,1,1024]{2,0,1:T(8,128)(2,1)}), bf16[288,1,1024]{2,0,1:T(8,128)(2,1)}) %reduce-scatter.8.cloned.1.call-update) | async-done | bytes 589840 | tf_op jit(solution)/shard_map/reduce_scatter | solution.py:253
  1134.7 74.3 %reduce-scatter.14.cloned.1.call-done = bf16[2304,288]{0,1:T(8,128)(2,1)} async-done(((bf16[2304,2304]{0,1:T(8,128)(2,1)}), bf16[2304,288]{0,1:T(8,128)(2,1)}) %reduce-scatter.14.cloned.1.call-update) | async-done | bytes 1327120 | tf_op jit(solution)/shard_map/reduce_scatter | solution.py:262
  1209.1 7.5 multiply_subtract_fusion.1
  1216.5 133.3 %reduce-scatter.12.cloned.1.call-done = bf16[288,2,2304]{2,0,1:T(8,128)(2,1)} async-done(((bf16[2304,2,2304]{2,0,1:T(8,128)(2,1)}), bf16[288,2,2304]{2,0,1:T(8,128)(2,1)}) %reduce-scatter.12.cloned.1.call-update) | async-done | bytes 2654224 | tf_op jit(solution)/shard_map/reduce_scatter | solution.py:259
  1349.9 10.4 multiply_subtract_fusion
  1360.3 9.0 copy.161
  1369.3 6.5 copy.163
  1375.8 6.7 copy.165
  (212 shorter events, 135.2 us)
Async XLA Ops:
  7.2 15.9 %copy-start.3 = (bf16[1,512,2304]{2,1,0:T(8,128)(2,1)S(1)}, bf16[1,512,2304]{2,1,0:T(8,128)(2,1)}, u32[]{:S(2)}) copy-start(bf16[1,512,2304]{2,1,0:T(8,128)(2,1)} %param.17) | copy-start | bytes 7077892
  7.2 44.9 %all-gather.6.cloned.1.call-start = ((), (), s32[]{:S(2)}) async-start(), calls=%async_computation.5 | async-start | bytes 5308416 | tf_op jit(solution)/shard_map/all_gather | solution.py:118
  9.7 79.1 %all-gather.8.cloned.1.call-start = ((), (), s32[]{:S(2)}) async-start(), calls=%async_computation.6 | async-start | bytes 2654208 | tf_op jit(solution)/shard_map/all_gather | solution.py:119
  11.6 254.8 %all-reduce.5.cloned.1.call-start = ((), (), s32[]{:S(2)}) async-start(), calls=%async_computation.7 | async-start | bytes 9437184 | tf_op jit(solution)/shard_map/psum | solution.py:170
  11.6 51.9 %copy-start.39 = (f32[128]{0:T(128)}, f32[128]{0:T(128)S(1)}, u32[]{:S(2)}) copy-start(f32[128]{0:T(128)S(1)} %negate_power_fusion) | copy-start | bytes 1540
  11.7 51.8 %copy-start.33 = (f32[512]{0:T(512)}, f32[512]{0:T(512)S(1)}, u32[]{:S(2)}) copy-start(f32[512]{0:T(512)S(1)} %fusion.118) | copy-start | bytes 6148
  23.1 35.6 %copy-start.31 = (f32[2304]{0:T(1024)}, f32[2304]{0:T(1024)S(1)}, u32[]{:S(2)}) copy-start(f32[2304]{0:T(1024)S(1)} %get-tuple-element.121) | copy-start | bytes 27652
  23.7 35.1 %copy-start.35 = (f32[512]{0:T(512)}, f32[512]{0:T(512)S(1)}, u32[]{:S(2)}) copy-start(f32[512]{0:T(512)S(1)} %fusion.114) | copy-start | bytes 6148
  26.0 44.3 %copy-start.18 = (f32[512,128]{0,1:T(8,128)}, f32[512,128]{0,1:T(8,128)S(1)}, u32[]{:S(2)}) copy-start(f32[512,128]{0,1:T(8,128)S(1)} %get-tuple-element.157) | copy-start | bytes 786436
  64.8 6.5 collective-permute-start
  75.1 9.8 copy-start.21
  88.7 765.3 %copy-start.26 = (bf16[256,2,512]{2,0,1:T(8,128)(2,1)}, bf16[256,2,512]{2,0,1:T(8,128)(2,1)S(1)}, u32[]{:S(2)}) copy-start(bf16[256,2,512]{2,0,1:T(8,128)(2,1)S(1)} %convolution_convert_fusion.4) | copy-start | bytes 1572868
  94.3 282.2 %all-gather.10.cloned.1.call-start = ((), (), s32[]{:S(2)}) async-start(), calls=%async_computation.8 | async-start | bytes 23887872 | tf_op jit(solution)/shard_map/all_gather | solution.py:120
  98.6 344.0 %all-gather.12.cloned.1.call-start = ((), (), s32[]{:S(2)}) async-start(), calls=%async_computation.9 | async-start | bytes 11943936 | tf_op jit(solution)/shard_map/all_gather | solution.py:121
  102.3 524.1 %all-reduce.7.cloned.1.call-start = ((), (), s32[]{:S(2)}) async-start(), calls=%async_computation.10 | async-start | bytes 9437184 | tf_op jit(solution)/shard_map/psum | solution.py:177
  454.3 386.8 %all-reduce.9.cloned.1.call-start = ((), (), s32[]{:S(2)}) async-start(), calls=%async_computation.11 | async-start | bytes 9437184 | tf_op jit(solution)/shard_map/psum | solution.py:190
  638.8 13.3 copy-start.11
  670.0 310.4 %all-reduce.11.cloned.1.call-start = ((), (), s32[]{:S(2)}) async-start(), calls=%async_computation.12 | async-start | bytes 4718592 | tf_op jit(solution)/shard_map/psum | solution.py:240
  841.1 11.9 slice-start
  874.9 3.9 collective-permute-start.1
  880.8 99.6 %copy-start.32 = (f32[2304]{0:T(1024)S(1)}, f32[2304]{0:T(1024)}, u32[]{:S(2)}) copy-start(f32[2304]{0:T(1024)} %copy-done.31) | copy-start | bytes 27652
  880.8 99.6 %copy-start.36 = (f32[512]{0:T(512)S(1)}, f32[512]{0:T(512)}, u32[]{:S(2)}) copy-start(f32[512]{0:T(512)} %copy-done.35) | copy-start | bytes 6148
  884.8 158.7 %reduce-scatter.16.cloned.1.call-start = ((), (), s32[]{:S(2)}) async-start(), calls=%async_computation.17 | async-start | bytes 663552
  985.2 79.9 %reduce-scatter.10.cloned.1.call-start = ((), (), s32[]{:S(2)}) async-start(), calls=%async_computation.14 | async-start | bytes 2654208 | tf_op jit(solution)/shard_map/reduce_scatter | solution.py:256
  990.0 133.5 %reduce-scatter.8.cloned.1.call-start = ((), (), s32[]{:S(2)}) async-start(), calls=%async_computation.13 | async-start | bytes 5308416 | tf_op jit(solution)/shard_map/reduce_scatter | solution.py:253
  994.7 214.3 %reduce-scatter.14.cloned.1.call-start = ((), (), s32[]{:S(2)}) async-start(), calls=%async_computation.16 | async-start | bytes 11943936 | tf_op jit(solution)/shard_map/reduce_scatter | solution.py:262
  1005.2 344.7 %reduce-scatter.12.cloned.1.call-start = ((), (), s32[]{:S(2)}) async-start(), calls=%async_computation.15 | async-start | bytes 23887872 | tf_op jit(solution)/shard_map/reduce_scatter | solution.py:259
  1036.8 28.3 %copy-start.12 = (f32[512,288]{0,1:T(8,128)S(1)}, f32[512,288]{0,1:T(8,128)}, u32[]{:S(2)}) copy-start(f32[512,288]{0,1:T(8,128)} %param.20) | copy-start | bytes 1769476
  1036.8 28.3 %copy-start.25 = (f32[512,288]{0,1:T(8,128)S(1)}, f32[512,288]{0,1:T(8,128)}, u32[]{:S(2)}) copy-start(f32[512,288]{0,1:T(8,128)} %param.25) | copy-start | bytes 1769476
  1043.5 79.9 %copy-start.10 = (f32[288,1,1024]{2,1,0:T(1,128)S(1)}, f32[288,1,1024]{2,1,0:T(1,128)}, u32[]{:S(2)}) copy-start(f32[288,1,1024]{2,1,0:T(1,128)} %param.19) | copy-start | bytes 3538948
  1043.5 79.9 %copy-start.23 = (f32[288,1,1024]{2,1,0:T(1,128)S(1)}, f32[288,1,1024]{2,1,0:T(1,128)}, u32[]{:S(2)}) copy-start(f32[288,1,1024]{2,1,0:T(1,128)} %param.24) | copy-start | bytes 3538948
  1126.1 83.0 %copy-start.7 = (f32[2304,288]{0,1:T(8,128)S(1)}, f32[2304,288]{0,1:T(8,128)}, u32[]{:S(2)}) copy-start(f32[2304,288]{0,1:T(8,128)} %param.22) | copy-start | bytes 7962628
  (32 other events, 124.2 us)
Sparse Core Ops, SparseCore 0:
  10.5 41.6 all-gather.5
  54.6 29.0 all-gather.7
  94.4 171.9 all-reduce.4
  268.7 107.6 all-gather.9
  378.8 63.8 all-gather.11
  454.4 171.9 all-reduce.6
  670.1 170.9 all-reduce.8
  884.9 95.3 all-reduce.10
  985.3 33.4 reduce-scatter.15
  1022.6 42.4 reduce-scatter.9
  1069.5 53.8 reduce-scatter.7
  1126.8 82.2 reduce-scatter.13
  1212.7 137.1 reduce-scatter.11
where the time goes:
time: 1400 us; the launch traced here: 1390 us
  waiting for transfers between devices  1020 us (73%)
  matrix products  142 us (10%)
  local copies, waits for them, and re-layouts  104 us (7%)
  other arithmetic  94.1 us (7%)
  between operations  15.2 us (1%)
    psum x1, waiting for transfers between devices, on_device(): lax.psum(jnp.dot(hidden, down_full, preferred_element_type=jnp.float32),...  172 us
    psum x1, waiting for transfers between devices, on_device(): grad_ffn_in = lax.psum(cols_product(grad_gate_up, gate_up_flat), 'tensor')  171 us
    psum x1, waiting for transfers between devices, on_device(): lax.psum(jnp.dot(att_flat, out_full, preferred_element_type=jnp.float32),...  164 us
    reduce_scatter x1, waiting for transfers between devices, on_device(): lax.psum_scatter(gate_up_local.astype(jnp.bfloat16), ('batch', 'seq'), sc...  133 us
    all_gather x1, waiting for transfers between devices, on_device(): lax.all_gather(gate_up_weight.astype(jnp.bfloat16), ('batch', 'seq'), axi...  103 us
    psum x1, waiting for transfers between devices, on_device(): lax.psum(cols_product(grad_proj, qkv_flat).astype(jnp.bfloat16), 'tensor')  95.5 us
    reduce_scatter x1, waiting for transfers between devices, on_device(): lax.psum_scatter(down_local.astype(jnp.bfloat16), ('batch', 'seq'), scatt...  74.3 us
    unnamed x110, local copies, waits for them, and re-layouts  57.6 us
  transfers between devices with their start and end apart: 15, of which 12 were waited for; matrix products, arithmetic and copies ran while one was open for 14% of the time, Pallas kernels for 0%

commit v1 on v0

--- a/solution.py
+++ b/solution.py
@@ -1,6 +1,8 @@
 import jax
 import jax.numpy as jnp
 from jax import lax
+from jax.experimental import pallas as pl
+from jax.experimental.pallas import tpu as pltpu
 from jax.sharding import PartitionSpec as P
 
 HEAD_DIM = 256
@@ -91,6 +93,766 @@
         "icgd,jcd->cgij", query_groups, ext_keys, preferred_element_type=jnp.float32
     ) * query_groups.shape[-1] ** (-0.5)
     return soft_cap * jnp.tanh(raw / soft_cap)
+
+
+def tensor_sum(part):
+    return lax.psum(part, "tensor")
+
+
+def swap(value, axis, bit):
+    count = lax.axis_size(axis)
+    return lax.ppermute(value, axis, [(source, source ^ bit) for source in range(count)])
+
+
+def gather_begin(shard):
+    half = shard.shape[0] // 2
+    low, high = shard[:half], shard[half:]
+    return low, high, swap(low, "batch", 1), swap(high, "batch", 2)
+
+
+def gather_end(state):
+    low, high, low_one, high_two = state
+    low_far = swap(jnp.stack([low, low_one]), "batch", 2)
+    high_far = swap(jnp.stack([high, high_two]), "batch", 1)
+    near = jnp.stack(
+        [
+            jnp.concatenate([low, high]),
+            jnp.concatenate([low_one, high_far[0]]),
+            jnp.concatenate([low_far[0], high_two]),
+            jnp.concatenate([low_far[1], high_far[1]]),
+        ]
+    )
+    return near, swap(near, "seq", 1)
+
+
+def own_blocks(wide):
+    tokens, width = wide.shape
+    chip, core = lax.axis_index("batch"), lax.axis_index("seq")
+    split = wide.reshape(tokens, 8, width // 8)
+    halves = []
+    for owner in (core, 1 - core):
+        parts = [
+            lax.dynamic_index_in_dim(split, (chip ^ k) * 2 + owner, 1, keepdims=False)
+            for k in range(4)
+        ]
+        halves.append(jnp.concatenate(parts, axis=1))
+    return halves
+
+
+def both_cores(wide):
+    mine, theirs = own_blocks(wide)
+    return jnp.concatenate([mine, swap(theirs, "seq", 1)], axis=0)
+
+
+def weight_local(wide, narrow):
+    local = rows_product(wide, narrow).astype(jnp.bfloat16)
+    return local.reshape(4, -1, local.shape[1])
+
+
+def scatter_begin(local):
+    half = local.shape[1] // 2
+    state = []
+    for part, first, second in ((local[:, :half], 1, 2), (local[:, half:], 2, 1)):
+        got = swap(jnp.stack([part[first], part[3]]), "batch", first)
+        far = part[second].astype(jnp.float32) + got[1].astype(jnp.float32)
+        state.append((part[0], got[0], far.astype(jnp.bfloat16)))
+    return state
+
+
+def scatter_end(state):
+    total = []
+    for (own, got, far), second in zip(state, (2, 1)):
+        got_far = swap(far, "batch", second)
+        near = own.astype(jnp.float32) + got.astype(jnp.float32)
+        total.append(near + got_far.astype(jnp.float32))
+    return jnp.concatenate(total, axis=0)
+
+
+def everywhere_sum(value):
+    for axis, bit in (("seq", 1), ("batch", 1), ("batch", 2), ("tensor", 1), ("tensor", 2)):
+        value = value + swap(value, axis, bit)
+    return value
+
+
+def spec_any():
+    return pl.BlockSpec(memory_space=pl.ANY)
+
+
+def spec_vmem():
+    return pl.BlockSpec(memory_space=pltpu.VMEM)
+
+
+def spec_smem():
+    return pl.BlockSpec(memory_space=pltpu.SMEM)
+
+
+def kernel_params():
+    return pltpu.CompilerParams(vmem_limit_bytes=56 * 1024 * 1024)
+
+
+def cost(flops, moved):
+    return pl.CostEstimate(flops=flops, bytes_accessed=moved, transcendentals=0)
+
+
+def shaped(shape, kind):
+    return jax.ShapeDtypeStruct(shape, kind)
+
+
+def dot_nn(left, right):
+    return lax.dot_general(
+        left, right, (((1,), (0,)), ((), ())), preferred_element_type=jnp.float32
+    )
+
+
+def dot_nt(left, right):
+    return lax.dot_general(
+        left, right, (((1,), (1,)), ((), ())), preferred_element_type=jnp.float32
+    )
+
+
+def dot_tn(left, right):
+    return lax.dot_general(
+        left, right, (((0,), (0,)), ((), ())), preferred_element_type=jnp.float32
+    )
+
+
+def row_scale(values):
+    return lax.rsqrt(jnp.mean(values * values, axis=-1, keepdims=True) + norm_eps)
+
+
+def norm_pull(values, scale, gain, upstream):
+    normed = values * scale
+    inner = upstream * (1.0 + gain)
+    pulled = scale * (inner - normed * jnp.mean(normed * inner, axis=-1, keepdims=True))
+    return pulled, upstream * normed
+
+
+def fetch_rows(place, near, far, target, sems, column, columns):
+    chip, core = place[0], place[1]
+    rows = near.shape[1]
+    copies = []
+    for k in range(4):
+        for which, source in enumerate((near, far)):
+            row = ((k ^ chip) * 2 + (which ^ core)) * rows
+            copies.append(
+                pltpu.make_async_copy(
+                    source.at[k, :, pl.ds(column, columns)],
+                    target.at[pl.ds(pl.multiple_of(row, 16), rows), :],
+                    sems.at[k * 2 + which],
+                )
+            )
+    for copy in copies:
+        copy.start()
+    return copies
+
+
+def rope(values, cosine, sine):
+    half = HEAD_DIM // 2
+    first, second = values[:, :half], values[:, half:]
+    return jnp.concatenate(
+        [first * cosine - second * sine, second * cosine + first * sine], axis=1
+    )
+
+
+def arrange_kernel(place, near, far, result, sems):
+    for copy in fetch_rows(place, near, far, result, sems, 0, result.shape[1]):
+        copy.wait()
+
+
+def arrange(place, near, far):
+    return pl.pallas_call(
+        arrange_kernel,
+        in_specs=[spec_smem(), spec_any(), spec_any()],
+        out_specs=spec_vmem(),
+        out_shape=shaped((8 * near.shape[1], near.shape[2]), jnp.bfloat16),
+        scratch_shapes=[pltpu.SemaphoreType.DMA((8,))],
+        compiler_params=kernel_params(),
+        cost_estimate=cost(0, 4 * near.size * 4),
+        name="arrange",
+    )(place, near, far)
+
+
+def project_kernel(place, x, near, far, cosine, sine, *rest):
+    queries, pair, attn_in, gains, weight, sems = rest[-6:]
+    copies = fetch_rows(place, near, far, weight, sems, 0, weight.shape[1])
+    for copy in copies:
+        copy.wait()
+    width = (GROUP + 2) * HEAD_DIM
+    tail = weight[:, width + GROUP * HEAD_DIM :].astype(jnp.float32)
+    gains[...] = jnp.transpose(tail)[:8]
+    gain = 1.0 + gains[0:1, :]
+    chunk = 16
+
+    @pl.loop(0, x.shape[0] // chunk, unroll=2)
+    def _(step):
+        rows = pl.ds(pl.multiple_of(step * chunk, chunk), chunk)
+        stream = x[rows, :].astype(jnp.float32)
+        attn_in[rows, :] = (stream * row_scale(stream) * gain).astype(jnp.bfloat16)
+
+    for member in range(GROUP + 2):
+        columns = slice(member * HEAD_DIM, (member + 1) * HEAD_DIM)
+        part = dot_nn(attn_in[...], weight[:, columns])
+        if member < GROUP:
+            queries[:, columns] = rope(part, cosine[...], sine[...]).astype(jnp.bfloat16)
+        elif member == GROUP:
+            pair[0] = rope(part, cosine[...], sine[...]).astype(jnp.bfloat16)
+        else:
+            pair[1] = part.astype(jnp.bfloat16)
+
+
+def project(place, x, near, far, cosine, sine, *earlier):
+    tokens, width = x.shape
+    bf16 = jnp.bfloat16
+    return pl.pallas_call(
+        project_kernel,
+        in_specs=[spec_smem(), spec_vmem(), spec_any(), spec_any(), spec_vmem(), spec_vmem()]
+        + [spec_any()] * len(earlier),
+        out_specs=[spec_vmem()] * 4,
+        out_shape=[
+            shaped((tokens, GROUP * HEAD_DIM), bf16),
+            shaped((2, tokens, HEAD_DIM), bf16),
+            shaped((tokens, width), bf16),
+            shaped((8, width), jnp.float32),
+        ],
+        scratch_shapes=[pltpu.VMEM((width, near.shape[2]), bf16), pltpu.SemaphoreType.DMA((8,))],
+        compiler_params=kernel_params(),
+        cost_estimate=cost(2 * tokens * width * 1024, 12_000_000),
+        name="project",
+    )(place, x, near, far, cosine, sine, *earlier)
+
+
+def chunk_scores(query, key, behind, row, core):
+    raw = dot_nt(query, key) * (HEAD_DIM**-0.5 / soft_cap)
+    bent = jnp.tanh(raw)
+    powers = jnp.exp(soft_cap * bent)
+    if behind:
+        powers = jnp.where(core > 0, powers, 0.0)
+    else:
+        at = row + lax.broadcasted_iota(jnp.int32, powers.shape, 0)
+        powers = jnp.where(at >= lax.broadcasted_iota(jnp.int32, powers.shape, 1), powers, 0.0)
+    return bent, powers
+
+
+def attend_kernel(place, queries, pair, behind, near, far, attended, result, weight, sems):
+    width = (GROUP + 2) * HEAD_DIM
+    copies = fetch_rows(place, near, far, weight, sems, width, GROUP * HEAD_DIM)
+    core = place[1]
+    chunk = 128
+    tokens = queries.shape[0]
+    for start in range(0, tokens, chunk):
+        rows = slice(start, start + chunk)
+        keys = start + chunk
+        for head in range(GROUP):
+            columns = slice(head * HEAD_DIM, (head + 1) * HEAD_DIM)
+            query = queries[rows, columns]
+            _, old = chunk_scores(query, behind[0], True, start, core)
+            _, new = chunk_scores(query, pair[0, :keys], False, start, core)
+            total = jnp.sum(old, axis=-1, keepdims=True) + jnp.sum(new, axis=-1, keepdims=True)
+            share = 1.0 / total
+            value = dot_nn((old * share).astype(jnp.bfloat16), behind[1])
+            value += dot_nn((new * share).astype(jnp.bfloat16), pair[1, :keys])
+            attended[rows, columns] = value.astype(jnp.bfloat16)
+    for copy in copies:
+        copy.wait()
+    tile = 768
+    for column in range(0, result.shape[1], tile):
+        part = dot_nt(attended[...], weight[column : column + tile, :])
+        result[:, column : column + tile] = part.astype(jnp.bfloat16)
+
+
+def attend(place, queries, pair, behind, near, far, width):
+    tokens = queries.shape[0]
+    bf16 = jnp.bfloat16
+    return pl.pallas_call(
+        attend_kernel,
+        in_specs=[spec_smem(), spec_vmem(), spec_vmem(), spec_vmem(), spec_any(), spec_any()],
+        out_specs=[spec_vmem()] * 2,
+        out_shape=[shaped((tokens, GROUP * HEAD_DIM), bf16), shaped((tokens, width), bf16)],
+        scratch_shapes=[
+            pltpu.VMEM((width, GROUP * HEAD_DIM), bf16),
+            pltpu.SemaphoreType.DMA((8,)),
+        ],
+        compiler_params=kernel_params(),
+        cost_estimate=cost(4 * tokens * width * 1024, 8_000_000),
+        name="attend",
+    )(place, queries, pair, behind, near, far)
+
+
+def widen_kernel(attn_out, x, gains, ffn, *rest):
+    ffn_in, hidden, by_gate, by_up = rest[-4:]
+    chunk = 16
+
+    @pl.when(pl.program_id(0) == 0)
+    def _():
+        @pl.loop(0, x.shape[0] // chunk, unroll=2)
+        def _(step):
+            rows = pl.ds(pl.multiple_of(step * chunk, chunk), chunk)
+            out = attn_out[rows, :].astype(jnp.float32)
+            mid = x[rows, :].astype(jnp.float32) + out * row_scale(out) * (1.0 + gains[1:2, :])
+            ffn_in[rows, :] = (mid * row_scale(mid) * (1.0 + gains[2:3, :])).astype(jnp.bfloat16)
+
+    value = ffn_in[...]
+    gate = dot_nn(value, ffn[0])
+    up = dot_nn(value, ffn[1])
+    square_of = gate * gate
+    bent = jnp.tanh(gate * (gelu_coef + gelu_coef * 0.044715 * square_of))
+    half = 0.5 + 0.5 * bent
+    curve = gate * half
+    slope = half + curve * (1.0 - bent) * (gelu_coef + 3.0 * gelu_coef * 0.044715 * square_of)
+    hidden[...] = (curve * up).astype(jnp.bfloat16)
+    by_gate[...] = (slope * up).astype(jnp.bfloat16)
+    by_up[...] = curve.astype(jnp.bfloat16)
+
+
+def whole(shape):
+    return pl.BlockSpec(shape, lambda *_: (0,) * len(shape))
+
+
+def widen(attn_out, x, gains, ffn, *earlier):
+    tokens, width = x.shape
+    units = ffn.shape[2]
+    tile = 256
+    bf16 = jnp.bfloat16
+    columns = pl.BlockSpec((tokens, tile), lambda i: (0, i))
+    return pl.pallas_call(
+        widen_kernel,
+        grid=(units // tile,),
+        in_specs=[
+            whole((tokens, width)),
+            whole((tokens, width)),
+            whole((8, width)),
+            pl.BlockSpec((2, width, tile), lambda i: (0, 0, i)),
+        ]
+        + [spec_any()] * len(earlier),
+        out_specs=[whole((tokens, width)), columns, columns, columns],
+        out_shape=[shaped((tokens, width), bf16)] + [shaped((tokens, units), bf16)] * 3,
+        compiler_params=kernel_params(),
+        cost_estimate=cost(4 * tokens * width * units, 36_000_000),
+        name="widen",
+    )(attn_out, x, gains, ffn, *earlier)
+
+
+def narrow_kernel(hidden, down, result):
+    result[...] = dot_nt(hidden[...], down[...]).astype(jnp.bfloat16)
+
+
+def narrow(hidden, down):
+    tokens, units = hidden.shape
+    width = down.shape[0]
+    tile = 256
+    return pl.pallas_call(
+        narrow_kernel,
+        grid=(width // tile,),
+        in_specs=[whole((tokens, units)), pl.BlockSpec((tile, units), lambda i: (i, 0))],
+        out_specs=pl.BlockSpec((tokens, tile), lambda i: (0, i)),
+        out_shape=shaped((tokens, width), jnp.bfloat16),
+        compiler_params=kernel_params(),
+        cost_estimate=cost(2 * tokens * width * units, 16_000_000),
+        name="narrow",
+    )(hidden, down)
+
+
+def top_back_kernel(ffn_out, top, gains, grad_ffn, gain_out):
+    chunk = 16
+    gain_out[...] = jnp.zeros_like(gain_out)
+
+    @pl.loop(0, ffn_out.shape[0] // chunk, unroll=2)
+    def _(step):
+        rows = pl.ds(pl.multiple_of(step * chunk, chunk), chunk)
+        out = ffn_out[rows, :].astype(jnp.float32)
+        upstream = top[rows, :].astype(jnp.float32)
+        pulled, product = norm_pull(out, row_scale(out), gains[3:4, :], upstream)
+        grad_ffn[rows, :] = pulled.astype(jnp.bfloat16)
+        gain_out[...] += product[:8] + product[8:]
+
+
+def top_back(ffn_out, top, gains):
+    tokens, width = top.shape
+    return pl.pallas_call(
+        top_back_kernel,
+        in_specs=[spec_vmem()] * 3,
+        out_specs=[spec_vmem()] * 2,
+        out_shape=[shaped((tokens, width), jnp.bfloat16), shaped((8, width), jnp.float32)],
+        compiler_params=kernel_params(),
+        cost_estimate=cost(20 * tokens * width, 8_000_000),
+        name="top_back",
+    )(ffn_out, top, gains)
+
+
+def ffn_back_kernel(grad_ffn, down, gate_up, by_gate, by_up, *rest):
+    grad_gate, grad_up, result, total = rest[-4:]
+
+    @pl.when(pl.program_id(0) == 0)
+    def _():
+        total[...] = jnp.zeros_like(total)
+
+    grad_hidden = dot_nn(grad_ffn[...], down[...])
+    one = (grad_hidden * by_gate[...].astype(jnp.float32)).astype(jnp.bfloat16)
+    two = (grad_hidden * by_up[...].astype(jnp.float32)).astype(jnp.bfloat16)
+    grad_gate[...] = one
+    grad_up[...] = two
+    total[...] += dot_nt(one, gate_up[0]) + dot_nt(two, gate_up[1])
+
+    @pl.when(pl.program_id(0) == pl.num_programs(0) - 1)
+    def _():
+        result[...] = total[...].astype(jnp.bfloat16)
+
+
+def ffn_back(grad_ffn, down, gate_up, by_gate, by_up, *earlier):
+    tokens, width = grad_ffn.shape
+    units = by_up.shape[1]
+    tile = 256
+    bf16 = jnp.bfloat16
+    columns = pl.BlockSpec((tokens, tile), lambda i: (0, i))
+    return pl.pallas_call(
+        ffn_back_kernel,
+        grid=(units // tile,),
+        in_specs=[
+            whole((tokens, width)),
+            pl.BlockSpec((width, tile), lambda i: (0, i)),
+            pl.BlockSpec((2, width, tile), lambda i: (0, 0, i)),
+            columns,
+            columns,
+        ]
+        + [spec_any()] * len(earlier),
+        out_specs=[columns, columns, whole((tokens, width))],
+        out_shape=[
+            shaped((tokens, units), bf16),
+            shaped((tokens, units), bf16),
+            shaped((tokens, width), bf16),
+        ],
+        scratch_shapes=[pltpu.VMEM((tokens, width), jnp.float32)],
+        compiler_params=kernel_params(),
+        cost_estimate=cost(6 * tokens * width * units, 52_000_000),
+        name="ffn_back",
+    )(grad_ffn, down, gate_up, by_gate, by_up, *earlier)
+
+
+def mid_back_kernel(place, grad_in, x, attn_out, top, gains, near, far, *rest):
+    grad_mid, grad_attn, grad_att, gain_out, weight, sems = rest[-6:]
+    width = (GROUP + 2) * HEAD_DIM
+    copies = fetch_rows(place, near, far, weight, sems, width, GROUP * HEAD_DIM)
+    gain_out[...] = jnp.zeros_like(gain_out)
+    chunk = 16
+    tokens = x.shape[0]
+
+    @pl.loop(0, tokens // chunk, unroll=2)
+    def _(step):
+        rows = pl.ds(pl.multiple_of(step * chunk, chunk), chunk)
+        out = attn_out[rows, :].astype(jnp.float32)
+        out_scale = row_scale(out)
+        mid = x[rows, :].astype(jnp.float32) + out * out_scale * (1.0 + gains[1:2, :])
+        upstream = grad_in[rows, :].astype(jnp.float32)
+        pulled, product = norm_pull(mid, row_scale(mid), gains[2:3, :], upstream)
+        gain_out[1] += product[:8] + product[8:]
+        at_mid = top[rows, :].astype(jnp.float32) + pulled
+        grad_mid[rows, :] = at_mid
+        pulled, product = norm_pull(out, out_scale, gains[1:2, :], at_mid)
+        gain_out[0] += product[:8] + product[8:]
+        grad_attn[rows, :] = pulled.astype(jnp.bfloat16)
+
+    for copy in copies:
+        copy.wait()
+    grad_att[...] = dot_nn(grad_attn[...], weight[...]).astype(jnp.bfloat16)
+
+
+def mid_back(place, grad_in, x, attn_out, top, gains, near, far, *earlier):
+    tokens, width = x.shape
+    heads = GROUP * HEAD_DIM
+    bf16 = jnp.bfloat16
+    return pl.pallas_call(
+        mid_back_kernel,
+        in_specs=[spec_smem()]
+        + [spec_vmem()] * 5
+        + [spec_any()] * 2
+        + [spec_any()] * len(earlier),
+        out_specs=[spec_vmem()] * 4,
+        out_shape=[
+            shaped((tokens, width), jnp.float32),
+            shaped((tokens, width), bf16),
+            shaped((tokens, heads), bf16),
+            shaped((2, 8, width), jnp.float32),
+        ],
+        scratch_shapes=[pltpu.VMEM((width, heads), bf16), pltpu.SemaphoreType.DMA((8,))],
+        compiler_params=kernel_params(),
+        cost_estimate=cost(2 * tokens * width * heads, 24_000_000),
+        name="mid_back",
+    )(place, grad_in, x, attn_out, top, gains, near, far, *earlier)
+
+
+def attend_back_kernel(
+    place, queries, pair, behind, attended, grad_att, cosine, sine, grad_q, grad_own, grad_old, sums
+):
+    core = place[1]
+    chunk = 128
+    tokens = queries.shape[0]
+    scale = HEAD_DIM**-0.5
+    sums[...] = jnp.zeros_like(sums)
+    for start in range(0, tokens, chunk):
+        rows = slice(start, start + chunk)
+        keys = start + chunk
+        cos, sin = cosine[rows, :], sine[rows, :]
+        for head in range(GROUP):
+            columns = slice(head * HEAD_DIM, (head + 1) * HEAD_DIM)
+            query, upstream = queries[rows, columns], grad_att[rows, columns]
+            delta = jnp.sum(
+                upstream.astype(jnp.float32) * attended[rows, columns].astype(jnp.float32),
+                axis=-1,
+                keepdims=True,
+            )
+            bent_old, old = chunk_scores(query, behind[0], True, start, core)
+            bent_new, new = chunk_scores(query, pair[0, :keys], False, start, core)
+            share = 1.0 / (
+                jnp.sum(old, axis=-1, keepdims=True) + jnp.sum(new, axis=-1, keepdims=True)
+            )
+            total = jnp.zeros((chunk, HEAD_DIM), jnp.float32)
+            for bent, powers, block, end, base in (
+                (bent_old, old, behind, tokens, 0),
+                (bent_new, new, pair, keys, 2),
+            ):
+                prob = powers * share
+                grad_p = dot_nt(upstream, block[1, :end])
+                grad_s = (prob * (grad_p - delta) * (1.0 - bent * bent)).astype(jnp.bfloat16)
+                total += dot_nn(grad_s, block[0, :end])
+                sums[base, :end, :] += dot_tn(grad_s, query)
+                sums[base + 1, :end, :] += dot_tn(prob.astype(jnp.bfloat16), upstream)
+            grad_q[rows, columns] = rope(total * scale, cos, -sin).astype(jnp.bfloat16)
+    grad_old[0] = (sums[0] * scale).astype(jnp.bfloat16)
+    grad_old[1] = sums[1].astype(jnp.bfloat16)
+    grad_own[0] = sums[2] * scale
+    grad_own[1] = sums[3]
+
+
+def attend_back(place, queries, pair, behind, attended, grad_att, cosine, sine):
+    tokens, heads = queries.shape
+    bf16 = jnp.bfloat16
+    return pl.pallas_call(
+        attend_back_kernel,
+        in_specs=[spec_smem()] + [spec_vmem()] * 7,
+        out_specs=[spec_vmem()] * 3,
+        out_shape=[
+            shaped((tokens, heads), bf16),
+            shaped((2, tokens, HEAD_DIM), jnp.float32),
+            shaped((2, tokens, HEAD_DIM), bf16),
+        ],
+        scratch_shapes=[pltpu.VMEM((4, tokens, HEAD_DIM), jnp.float32)],
+        compiler_params=kernel_params(),
+        cost_estimate=cost(20 * tokens * 1024 * heads, 5_000_000),
+        name="attend_back",
+    )(place, queries, pair, behind, attended, grad_att, cosine, sine)
+
+
+def project_back_kernel(
+    place, grad_q, grad_own, grad_ahead, cosine, sine, x, near, far, *rest
+):
+    proj, result, gain_out, weight, sems = rest[-5:]
+    width = (GROUP + 2) * HEAD_DIM
+    copies = fetch_rows(place, near, far, weight, sems, 0, width)
+    heads = GROUP * HEAD_DIM
+    proj[:, :heads] = grad_q[...]
+    grad_key = grad_own[0] + grad_ahead[0].astype(jnp.float32)
+    proj[:, heads : heads + HEAD_DIM] = rope(grad_key, cosine[...], -sine[...]).astype(jnp.bfloat16)
+    proj[:, heads + HEAD_DIM :] = (grad_own[1] + grad_ahead[1].astype(jnp.float32)).astype(
+        jnp.bfloat16
+    )
+    gain_out[...] = jnp.zeros_like(gain_out)
+    for copy in copies:
+        copy.wait()
+    tile = 768
+    for column in range(0, result.shape[1], tile):
+        part = dot_nt(proj[...], weight[column : column + tile, :])
+        result[:, column : column + tile] = part.astype(jnp.bfloat16)
+    chunk = 16
+
+    @pl.loop(0, x.shape[0] // chunk, unroll=2)
+    def _(step):
+        rows = pl.ds(pl.multiple_of(step * chunk, chunk), chunk)
+        stream = x[rows, :].astype(jnp.float32)
+        product = result[rows, :].astype(jnp.float32) * (stream * row_scale(stream))
+        gain_out[...] += product[:8] + product[8:]
+
+
+def project_back(place, grad_q, grad_own, grad_ahead, cosine, sine, x, near, far, *earlier):
+    tokens, width = x.shape
+    proj_width = (GROUP + 2) * HEAD_DIM
+    bf16 = jnp.bfloat16
+    return pl.pallas_call(
+        project_back_kernel,
+        in_specs=[spec_smem()]
+        + [spec_vmem()] * 6
+        + [spec_any()] * 2
+        + [spec_any()] * len(earlier),
+        out_specs=[spec_vmem()] * 3,
+        out_shape=[
+            shaped((tokens, proj_width), bf16),
+            shaped((tokens, width), bf16),
+            shaped((8, width), jnp.float32),
+        ],
+        scratch_shapes=[pltpu.VMEM((width, proj_width), bf16), pltpu.SemaphoreType.DMA((8,))],
+        compiler_params=kernel_params(),
+        cost_estimate=cost(2 * tokens * width * proj_width, 14_000_000),
+        name="project_back",
+    )(place, grad_q, grad_own, grad_ahead, cosine, sine, x, near, far, *earlier)
+
+
+def stream_back_kernel(grad_in, x, gains, grad_mid, *rest):
+    result = rest[-1]
+    stream = x[...].astype(jnp.float32)
+    pulled, _ = norm_pull(
+        stream, row_scale(stream), gains[0:1, :], grad_in[...].astype(jnp.float32)
+    )
+    result[...] = grad_mid[...] + pulled
+
+
+def stream_back(grad_in, x, gains, grad_mid, *earlier):
+    tokens, width = x.shape
+    tile = 64
+    rows = pl.BlockSpec((tile, width), lambda i: (i, 0))
+    return pl.pallas_call(
+        stream_back_kernel,
+        grid=(tokens // tile,),
+        in_specs=[rows, rows, whole((8, width)), rows] + [spec_any()] * len(earlier),
+        out_specs=rows,
+        out_shape=shaped((tokens, width), jnp.float32),
+        compiler_params=kernel_params(),
+        cost_estimate=cost(20 * tokens * width, 14_000_000),
+        name="stream_back",
+    )(grad_in, x, gains, grad_mid, *earlier)
+
+
+def on_square(
+    layer_in,
+    cotangent,
+    qkv_weight,
+    out_weight,
+    gate_up_weight,
+    down_weight,
+    norm_gains,
+    qkv_first,
+    out_first,
+    gate_up_first,
+    down_first,
+    gains_first,
+    qkv_second,
+    out_second,
+    gate_up_second,
+    down_second,
+    gains_second,
+):
+    tok_rows = layer_in.shape[1]
+    chip, core = lax.axis_index("batch"), lax.axis_index("seq")
+    place = jnp.stack([chip, core]).astype(jnp.int32)
+    plane = ("batch", "seq")
+    stream, top = layer_in[0], cotangent[0]
+    gains_cast = jnp.pad(norm_gains.T, ((0, 0), (0, 128 - norm_gains.shape[0])))
+    attn_cast = jnp.concatenate([qkv_weight[:, 0], out_weight.T, gains_cast], axis=1)
+    gate_up_cast = gate_up_weight.astype(jnp.bfloat16).transpose(1, 0, 2)
+    down_cast = down_weight.T.astype(jnp.bfloat16)
+    state, down_cast, gate_up_cast = lax.optimization_barrier(
+        (gather_begin(attn_cast.astype(jnp.bfloat16)), down_cast, gate_up_cast)
+    )
+    near, far = gather_end(state)
+    down_state = gather_begin(down_cast)
+    near, far, down_state = lax.optimization_barrier((near, far, down_state))
+    down = arrange(place, *gather_end(down_state))
+    gate_up = lax.all_gather(gate_up_cast, plane, axis=1, tiled=True)
+    positions = core * tok_rows + jnp.arange(tok_rows, dtype=jnp.int32)
+    cosine, sine = rope_tables(positions, HEAD_DIM)
+
+    queries, pair, attn_in, gains = project(
+        place, stream, near, far, cosine, sine, gate_up_cast
+    )
+    behind = from_behind(pair, "seq", 1)
+    attended, attn_part = attend(place, queries, pair, behind, near, far, stream.shape[1])
+    attn_out = tensor_sum(attn_part)
+    ffn_in, hidden, by_gate, by_up = widen(attn_out, stream, gains, gate_up)
+    ffn_out = tensor_sum(narrow(hidden, down))
+
+    grad_ffn, gain_ffn = top_back(ffn_out, top, gains)
+    grad_gate, grad_up, grad_ffn_part = ffn_back(grad_ffn, down, gate_up, by_gate, by_up)
+    grad_ffn_in = tensor_sum(grad_ffn_part)
+    ffn_in_both = both_cores(ffn_in)
+    hidden_both = jnp.concatenate([hidden, swap(hidden, "seq", 1)], axis=0)
+    grad_gate_both = jnp.concatenate([grad_gate, swap(grad_gate, "seq", 1)], axis=0)
+    grad_up_both = jnp.concatenate([grad_up, swap(grad_up, "seq", 1)], axis=0)
+    down_grad = scatter_end(scatter_begin(weight_local(both_cores(grad_ffn), hidden_both)))
+    gate_state = scatter_begin(weight_local(ffn_in_both, grad_gate_both))
+    up_local = weight_local(ffn_in_both, grad_up_both)
+
+    grad_mid, grad_attn, grad_att, gain_mid = mid_back(
+        place, grad_ffn_in, stream, attn_out, top, gains, near, far, down_grad, gate_state[0][2],
+        gate_state[1][2], up_local
+    )
+    gate_grad = scatter_end(gate_state)
+    up_state = scatter_begin(up_local)
+    grad_q, grad_own, grad_old = attend_back(
+        place, queries, pair, behind, attended, grad_att, cosine, sine
+    )
+    grad_ahead = from_behind(grad_old, "seq", -1)
+    grad_proj, grad_attn_part, gain_attn = project_back(
+        place, grad_q, grad_own, grad_ahead, cosine, sine, stream, near, far, gate_grad,
+        up_state[0][2], up_state[1][2]
+    )
+    grad_attn_in = tensor_sum(grad_attn_part)
+    up_grad = scatter_end(up_state)
+    gate_up_grad = jnp.stack([gate_grad, up_grad], axis=1)
+
+    att_both = jnp.concatenate([attended, swap(attended, "seq", 1)], axis=0)
+    out_grad = scatter_end(scatter_begin(weight_local(both_cores(grad_attn), att_both)))
+    proj_both = jnp.concatenate([grad_proj, swap(grad_proj, "seq", 1)], axis=0)
+    qkv_grad = scatter_end(scatter_begin(weight_local(both_cores(attn_in), proj_both)))[:, None]
+    gains_rest = jnp.concatenate([gain_mid, gain_ffn[None]], axis=0).sum(axis=1)
+    gains_rest = jnp.where(lax.axis_index("tensor") == 0, gains_rest, 0.0)
+    gains_total = everywhere_sum(jnp.concatenate([gain_attn.sum(axis=0)[None], gains_rest], axis=0))
+    own_columns = norm_gains.shape[1]
+    gains_grad = lax.dynamic_slice_in_dim(
+        gains_total, (chip * 2 + core) * own_columns, own_columns, axis=1
+    )
+    attn_float = attn_out.astype(jnp.float32)
+    mid_stream = stream.astype(jnp.float32) + rms_norm(attn_float, gains[1])
+    layer_out = (mid_stream + rms_norm(ffn_out.astype(jnp.float32), gains[3])).astype(jnp.bfloat16)
+    qkv_new, qkv_first_new, qkv_second_new = adam_step(
+        qkv_weight, qkv_grad, qkv_first, qkv_second, decay_rate
+    )
+    out_new, out_first_new, out_second_new = adam_step(
+        out_weight.T, out_grad, out_first.T, out_second.T, decay_rate
+    )
+    gate_up_new, gate_up_first_new, gate_up_second_new = adam_step(
+        gate_up_weight, gate_up_grad, gate_up_first, gate_up_second, decay_rate
+    )
+    down_new, down_first_new, down_second_new = adam_step(
+        down_weight.T, down_grad, down_first.T, down_second.T, decay_rate
+    )
+    gains_new, gains_first_new, gains_second_new = adam_step(
+        norm_gains, gains_grad, gains_first, gains_second, 0.0
+    )
+    input_grad = stream_back(
+        grad_attn_in, stream, gains, grad_mid, qkv_new, out_new, gate_up_new, down_new, gains_new
+    )
+    return (
+        layer_out[None],
+        input_grad[None],
+        qkv_grad,
+        out_grad.T,
+        gate_up_grad,
+        down_grad.T,
+        gains_grad,
+        qkv_new,
+        out_new.T,
+        gate_up_new,
+        down_new.T,
+        gains_new,
+        qkv_first_new,
+        out_first_new.T,
+        gate_up_first_new,
+        down_first_new.T,
+        gains_first_new,
+        qkv_second_new,
+        out_second_new.T,
+        gate_up_second_new,
+        down_second_new.T,
+        gains_second_new,
+    )
 
 
 def on_device(
@@ -352,6 +1114,8 @@
         P("tensor", ("batch", "seq")),
         P(None, ("batch", "seq")),
     )
+    sizes = tuple(mesh.shape[axis] for axis in ("batch", "seq", "tensor"))
+    body = on_square if sizes == (4, 2, 4) else on_device
     return jax.shard_map(
-        on_device, mesh=mesh, in_specs=in_specs, out_specs=out_specs, check_vma=False
-    )
+        body, mesh=mesh, in_specs=in_specs, out_specs=out_specs, check_vma=False
+    )

time: 1400 us -> 730 us (0.52)
  waiting for transfers between devices: 1020 us -> 330 us
  Pallas kernels: 0 us -> 156 us
  matrix products: 142 us -> 31.9 us
  local copies, waits for them, and re-layouts: 104 us -> 48.5 us
  starting transfers between devices: 6.62 us -> 44.5 us
    psum x4, waiting for transfers between devices: 602 us -> 99.5 us  [tensor_sum(): return lax.psum(part, 'tensor')]
    reduce_scatter x4 -> x0, waiting for transfers between devices: 282 us -> none  [the longest x1 133 us: on_device(): lax.psum_scatter(gate_up_local.astype(jnp.bfloat16), ('batch', 'seq'), sc...]
    ppermute x0 -> x44, waiting for transfers between devices: none -> 192 us  [swap(): lax.ppermute(value, axis, [(source, source ^ bit) for source in range(cou...]
    pallas_call x0 -> x11, Pallas kernels: none -> 156 us  [the longest x1 34.7 us: ffn_back(): pl.pallas_call(ffn_back_kernel, grid=(units // tile,), in_specs=[whole((t...]
    dot_general x14 -> x0, matrix products: 103 us -> none  [the longest x4 34.4 us: cols_product(): lax.dot_general(left, right, (((1,), (1,)), ((), ())), preferred_element_...]
    all_gather x4 -> x1, waiting for transfers between devices: 138 us -> 36.1 us  [on_square(): gate_up = lax.all_gather(gate_up_cast, plane, axis=1, tiled=True)]
    unnamed x110 -> x102, local copies, waits for them, and re-layouts: 57.6 us -> 12.2 us
    ppermute x0 -> x44, starting transfers between devices: none -> 41 us  [swap(): lax.ppermute(value, axis, [(source, source ^ bit) for source in range(cou...]
  transfers between devices with their start and end apart: 15 -> 51, of which waited for: 12 -> 24; matrix products, arithmetic and copies ran while one was open for 14% -> 22% of each run, Pallas kernels for 0% -> 13%
where the time goes in v1:
time: 730 us; the launch traced here: 721 us
  waiting for transfers between devices  330 us (45%)
  Pallas kernels  156 us (21%)
  other arithmetic  93.6 us (13%)
  local copies, waits for them, and re-layouts  48.5 us (7%)
  starting transfers between devices  44.5 us (6%)
  matrix products  31.9 us (4%)
  between operations  16.5 us (2%)
    ppermute x44, waiting for transfers between devices, swap(): lax.ppermute(value, axis, [(source, source ^ bit) for source in range(cou...  192 us
    psum x4, waiting for transfers between devices, tensor_sum(): return lax.psum(part, 'tensor')  99.5 us
    ppermute x44, starting transfers between devices, swap(): lax.ppermute(value, axis, [(source, source ^ bit) for source in range(cou...  41 us
    sub x3, other arithmetic, adam_step(): weight - learn_rate * (first_hat / (jnp.sqrt(second_hat) + adam_eps) + de...  38.3 us
    all_gather x1, waiting for transfers between devices, on_square(): gate_up = lax.all_gather(gate_up_cast, plane, axis=1, tiled=True)  36.1 us
    pallas_call x1, Pallas kernels, ffn_back(): pl.pallas_call(ffn_back_kernel, grid=(units // tile,), in_specs=[whole((t...  34.7 us
    dot_general x5, matrix products, rows_product(): lax.dot_general(left, right, (((0,), (0,)), ((), ())), preferred_element_...  31.9 us
    pallas_call x1, Pallas kernels, widen(): pl.pallas_call(widen_kernel, grid=(units // tile,), in_specs=[whole((toke...  24.2 us
  transfers between devices with their start and end apart: 51, of which 24 were waited for; matrix products, arithmetic and copies ran while one was open for 22% of the time, Pallas kernels for 13%

profile of v1, /device:TPU:0, one launch (start us, length us, event | category | flops | bytes accessed | tf_op | source)
XLA Modules:
  0.0 721.3 jit_solution(4216254107672894562)
XLA Ops:
  19.3 6.4 collective-permute-done
  33.3 17.9 %collective-permute-done.3 = bf16[2,144,1664]{2,1,0:T(8,128)(2,1)S(1)} collective-permute-done((bf16[2,144,1664]{2,1,0:T(8,128)(2,1)S(1)}, bf16[2,144,1664]{2,1,0:T(8,128)(2,1)S(1)}, u32[]{:S(2)}, u32[]{:S(2)}) %collective-permute-start.3) | collective-permute-done | bytes 958496 | tf_op jit(solution)/shard_map/ppermute | solution.py:104
  61.3 13.3 %collective-permute-done.5 = bf16[144,2304]{1,0:T(8,128)(2,1)} collective-permute-done((bf16[144,2304]{1,0:T(8,128)(2,1)}, bf16[144,2304]{1,0:T(8,128)(2,1)}, u32[]{:S(2)}, u32[]{:S(2)}) %collective-permute-start.5) | collective-permute-done | bytes 663584 | tf_op jit(solution)/shard_map/ppermute | solution.py:104
  75.5 11.6 %project.1 = (bf16[512,512]{1,0:T(8,128)(2,1)}, bf16[2,512,256]{2,1,0:T(8,128)(2,1)}, bf16[512,2304]{1,0:T(8,128)(2,1)}, f32[8,2304]{1,0:T(8,128)}) custom-call(s32[2]{0:T(128)} %pad_add_fusion.place, bf16[512,2304]{1,0:T(8,128)(2,1)} %bitcast.230, bf16[4,288,1664]{2,1,0:T(8,128)(2,1)} %pad_maximum_fusion.2.near, ...), custom_call_target="tpu_custom_call" | custom-call | flops 2415919104 | bytes 12000000 | tf_op jit(solution)/shard_map/project/pallas_call | solution.py:306
  91.0 7.7 %attend.1 = (bf16[512,512]{1,0:T(8,128)(2,1)}, bf16[512,2304]{1,0:T(8,128)(2,1)}) custom-call(s32[2]{0:T(128)} %pad_add_fusion.place, bf16[512,512]{1,0:T(8,128)(2,1)} %get-tuple-element.67.queries, bf16[2,512,256]{2,1,0:T(8,128)(2,1)} %get-tuple-element.68.pair, bf16[2,512,256]{2,1,0:T(8,128)(2,1)} %copy-done.48, ...), custom_call_target="tpu_custom_call" | custom-call | flops 4831838208 | bytes 8000000 | tf_op jit(solution)/shard_map/attend/pallas_call | solution.py:366
  105.0 46.3 %collective-permute-done.9 = bf16[2,144,2304]{2,1,0:T(8,128)(2,1)S(1)} collective-permute-done((bf16[2,144,2304]{2,1,0:T(8,128)(2,1)S(1)}, bf16[2,144,2304]{2,1,0:T(8,128)(2,1)S(1)}, u32[]{:S(2)}, u32[]{:S(2)}) %collective-permute-start.9) | collective-permute-done | bytes 1327136 | tf_op jit(solution)/shard_map/ppermute | solution.py:104
  157.2 8.9 %collective-permute-done.10.far = bf16[4,288,2304]{2,1,0:T(8,128)(2,1)} collective-permute-done((bf16[4,288,2304]{2,1,0:T(8,128)(2,1)S(1)}, bf16[4,288,2304]{2,1,0:T(8,128)(2,1)}, u32[]{:S(2)}, u32[]{:S(2)}) %collective-permute-start.10) | collective-permute-done | bytes 5308448 | tf_op jit(solution)/shard_map/ppermute | solution.py:104
  166.1 11.0 %arrange.1.down = bf16[2304,2304]{1,0:T(8,128)(2,1)} custom-call(s32[2]{0:T(128)} %pad_add_fusion.place, bf16[4,288,2304]{2,1,0:T(8,128)(2,1)} %copy-done.6, bf16[4,288,2304]{2,1,0:T(8,128)(2,1)} %collective-permute-done.10.far), custom_call_target="tpu_custom_call" | custom-call | bytes 42467328 | tf_op jit(solution)/shard_map/arrange/pallas_call | solution.py:263
  177.0 17.2 %all-reduce.6.cloned.1.call-done.attn_out = bf16[512,2304]{1,0:T(8,128)(2,1)} async-done(((bf16[512,2304]{1,0:T(8,128)(2,1)}), bf16[512,2304]{1,0:T(8,128)(2,1)}) %all-reduce.6.cloned.1.call-update) | async-done | bytes 2359312 | tf_op jit(solution)/shard_map/psum | solution.py:99
  194.2 36.1 %all-gather.2.cloned.1.call-done.ffn.gate_up = bf16[2,2304,2304]{2,1,0:T(8,128)(2,1)} async-done(((bf16[2,288,2304]{2,1,0:T(8,128)(2,1)}), bf16[2,2304,2304]{2,1,0:T(8,128)(2,1)}) %all-gather.2.cloned.1.call-update) | async-done | bytes 21233680 | tf_op jit(solution)/shard_map/all_gather | solution.py:758
  230.4 24.2 %widen.1 = (bf16[512,2304]{1,0:T(8,128)(2,1)}, bf16[512,2304]{1,0:T(8,128)(2,1)}, bf16[512,2304]{1,0:T(8,128)(2,1)}, bf16[512,2304]{1,0:T(8,128)(2,1)}) custom-call(bf16[512,2304]{1,0:T(8,128)(2,1)} %all-reduce.6.cloned.1.call-done.attn_out, bf16[512,2304]{1,0:T(8,128)(2,1)} %bitcast.231, f32[8,2304]{1,0:T(8,128)} %get-tuple-element.70.gains, ...), custom_call_target="tpu_custom_call" | custom-call | flops 10871635968 | bytes 36000000 | tf_op jit(solution)/shard_map/widen/pallas_call | solution.py:417
  254.6 12.4 %narrow.1 = bf16[512,2304]{1,0:T(8,128)(2,1)} custom-call(bf16[512,2304]{1,0:T(8,128)(2,1)} %get-tuple-element.71.hidden, bf16[2304,2304]{1,0:T(8,128)(2,1)} %arrange.1.down), custom_call_target="tpu_custom_call" | custom-call | flops 5435817984 | bytes 16000000 | tf_op jit(solution)/shard_map/narrow/pallas_call | solution.py:443
  286.8 76.0 %all-reduce.8.cloned.1.call-done.ffn_out = bf16[512,2304]{1,0:T(8,128)(2,1)} async-done(((bf16[512,2304]{1,0:T(8,128)(2,1)}), bf16[512,2304]{1,0:T(8,128)(2,1)}) %all-reduce.8.cloned.1.call-update) | async-done | bytes 2359312 | tf_op jit(solution)/shard_map/psum | solution.py:99
  362.8 7.9 %top_back.1 = (bf16[512,2304]{1,0:T(8,128)(2,1)}, f32[8,2304]{1,0:T(8,128)}) custom-call(bf16[512,2304]{1,0:T(8,128)(2,1)} %all-reduce.8.cloned.1.call-done.ffn_out, bf16[512,2304]{1,0:T(8,128)(2,1)} %bitcast.243, f32[8,2304]{1,0:T(8,128)} %get-tuple-element.70.gains), custom_call_target="tpu_custom_call" | custom-call | flops 23592960 | bytes 8000000 | tf_op jit(solution)/shard_map/top_back/pallas_call | solution.py:471
  370.7 34.7 %ffn_back.1 = (bf16[512,2304]{1,0:T(8,128)(2,1)}, bf16[512,2304]{1,0:T(8,128)(2,1)}, bf16[512,2304]{1,0:T(8,128)(2,1)}) custom-call(bf16[512,2304]{1,0:T(8,128)(2,1)} %get-tuple-element.77.grad_ffn, bf16[2304,2304]{1,0:T(8,128)(2,1)} %arrange.1.down, bf16[2,2304,2304]{2,1,0:T(8,128)(2,1)} %all-gather.2.cloned.1.call-done.ffn.gate_up, ...), custom_call_target="tpu_custom_call" | custom-call | flops 16307453952 | bytes 52000000 | tf_op jit(solution)/shard_map/ffn_back/pallas_call | solution.py:507
  418.5 8.0 %convolution_convert_fusion.2 = bf16[1152,2304]{1,0:T(8,128)(2,1)S(1)} fusion(bf16[512,2304]{1,0:T(8,128)(2,1)} %collective-permute-done.12, bf16[512,2304]{1,0:T(8,128)(2,1)} %get-tuple-element.71.hidden, bf16[512,1152]{0,1:T(8,128)(2,1)S(1)} %collective-permute-done.11, bf16[512,288]{0,1:T(8,128)(2,1)S(1)} %get-tuple-element.233, ...), kind=kOutput, calls=%fused_computation.2 | convolution fusion | flops 5459705856 | bytes 12386304 | tf_op jit(solution)/shard_map/dot_general | solution.py:80
  431.7 7.7 %convolution_convert_fusion.1 = bf16[1152,2304]{1,0:T(8,128)(2,1)S(1)} fusion(bf16[512,2304]{1,0:T(8,128)(2,1)} %copy-done.47, bf16[512,2304]{1,0:T(8,128)(2,1)S(1)} %copy-done.46, bf16[512,1152]{0,1:T(8,128)(2,1)} %collective-permute-done.17, bf16[512,288]{0,1:T(8,128)(2,1)S(1)} %get-tuple-element.225, bf16[512,288]{0,1:T(8,128)(2,1)S(1)} %get-tuple-element.226, ...), kind=kOutput, calls=%fused_computation.1 | convolution fusion | flops 5459705856 | bytes 12386304 | tf_op jit(solution)/shard_map/dot_general | solution.py:80
  441.2 8.6 %convolution_convert_fusion = bf16[1152,2304]{1,0:T(8,128)(2,1)S(1)} fusion(bf16[512,2304]{1,0:T(8,128)(2,1)} %collective-permute-done.21, bf16[512,2304]{1,0:T(8,128)(2,1)} %get-tuple-element.83, bf16[512,1152]{0,1:T(8,128)(2,1)} %collective-permute-done.17, bf16[512,288]{0,1:T(8,128)(2,1)S(1)} %get-tuple-element.225, ...), kind=kOutput, calls=%fused_computation | convolution fusion | flops 5459705856 | bytes 12386304 | tf_op jit(solution)/shard_map/dot_general | solution.py:80
  452.7 7.7 %collective-permute-done.13 = bf16[2,144,2304]{2,1,0:T(8,128)(2,1)} collective-permute-done((bf16[2,144,2304]{2,1,0:T(8,128)(2,1)}, bf16[2,144,2304]{2,1,0:T(8,128)(2,1)}, u32[]{:S(2)}, u32[]{:S(2)}) %collective-permute-start.13) | collective-permute-done | bytes 1327136 | tf_op jit(solution)/shard_map/ppermute | solution.py:104
  467.7 36.2 %collective-permute-done.14 = bf16[144,2304]{1,0:T(8,128)(2,1)S(1)} collective-permute-done((bf16[144,2304]{1,0:T(8,128)(2,1)S(1)}, bf16[144,2304]{1,0:T(8,128)(2,1)S(1)}, u32[]{:S(2)}, u32[]{:S(2)}) %collective-permute-start.14) | collective-permute-done | bytes 663584 | tf_op jit(solution)/shard_map/ppermute | solution.py:104
  507.7 5.1 fusion.59
  514.3 21.7 %collective-permute-done.19 = bf16[2,144,2304]{2,1,0:T(8,128)(2,1)S(1)} collective-permute-done((bf16[2,144,2304]{2,1,0:T(8,128)(2,1)S(1)}, bf16[2,144,2304]{2,1,0:T(8,128)(2,1)S(1)}, u32[]{:S(2)}, u32[]{:S(2)}) %collective-permute-start.19) | collective-permute-done | bytes 1327136 | tf_op jit(solution)/shard_map/ppermute | solution.py:104
  540.5 15.5 %mid_back.1 = (f32[512,2304]{1,0:T(8,128)}, bf16[512,2304]{1,0:T(8,128)(2,1)}, bf16[512,512]{1,0:T(8,128)(2,1)}, f32[2,8,2304]{2,1,0:T(8,128)}) custom-call(s32[2]{0:T(128)} %pad_add_fusion.place, bf16[512,2304]{1,0:T(8,128)(2,1)} %all-reduce.10.cloned.1.call-done.grad_in, bf16[512,2304]{1,0:T(8,128)(2,1)} %bitcast.232, ...), custom_call_target="tpu_custom_call" | custom-call | flops 1207959552 | bytes 24000000 | tf_op jit(solution)/shard_map/mid_back/pallas_call | solution.py:563
  560.5 9.7 %attend_back.1 = (bf16[512,512]{1,0:T(8,128)(2,1)}, f32[2,512,256]{2,1,0:T(8,128)}, bf16[2,512,256]{2,1,0:T(8,128)(2,1)}) custom-call(s32[2]{0:T(128)} %pad_add_fusion.place, bf16[512,512]{1,0:T(8,128)(2,1)} %get-tuple-element.67.queries, bf16[2,512,256]{2,1,0:T(8,128)(2,1)} %get-tuple-element.68.pair, bf16[2,512,256]{2,1,0:T(8,128)(2,1)} %copy-done.48, ...), custom_call_target="tpu_custom_call" | custom-call | flops 5368709120 | bytes 5000000 | tf_op jit(solution)/shard_map/attend_back/pallas_call | solution.py:629
  575.8 9.5 %collective-permute-done.24 = bf16[144,2304]{1,0:T(8,128)(2,1)S(1)} collective-permute-done((bf16[144,2304]{1,0:T(8,128)(2,1)S(1)}, bf16[144,2304]{1,0:T(8,128)(2,1)S(1)}, u32[]{:S(2)}, u32[]{:S(2)}) %collective-permute-start.24) | collective-permute-done | bytes 663584 | tf_op jit(solution)/shard_map/ppermute | solution.py:104
  590.5 12.0 %project_back.1 = (bf16[512,1024]{1,0:T(8,128)(2,1)}, bf16[512,2304]{1,0:T(8,128)(2,1)}, f32[8,2304]{1,0:T(8,128)}) custom-call(s32[2]{0:T(128)} %pad_add_fusion.place, bf16[512,512]{1,0:T(8,128)(2,1)} %get-tuple-element.85.grad_q, f32[2,512,256]{2,1,0:T(8,128)} %get-tuple-element.86.grad_own, bf16[2,512,256]{2,1,0:T(8,128)(2,1)} %copy-done.29, ...), custom_call_target="tpu_custom_call" | custom-call | flops 2415919104 | bytes 14000000 | tf_op jit(solution)/shard_map/project_back/pallas_call | solution.py:679
  618.6 28.0 %multiply_subtract_fusion = (f32[288,2,2304]{2,1,0:T(2,128)}, f32[288,2,2304]{2,1,0:T(2,128)}, f32[288,2,2304]{2,1,0:T(2,128)}, f32[288,2,2304]{2,1,0:T(2,128)}) fusion(f32[288,2,2304]{2,1,0:T(2,128)} %param.21, f32[288,2,2304]{2,1,0:T(2,128)} %param.26, f32[288,2,2304]{2,1,0:T(2,128)} %param.31, f32[288,1,2304]{2,1,0:T(1,128)} %stack.150, ...), kind=kLoop, calls=%fused_computation.12 | loop fusion | flops 21233664 | bytes 42467328 | tf_op jit(solution)/shard_map/sub | solution.py:73
  654.5 4.5 convolution_convert_fusion.3
  665.3 10.7 %collective-permute-done.36 = bf16[144,512]{1,0:T(8,128)(2,1)S(1)} collective-permute-done((bf16[144,512]{1,0:T(8,128)(2,1)S(1)}, bf16[144,512]{1,0:T(8,128)(2,1)S(1)}, u32[]{:S(2)}, u32[]{:S(2)}) %collective-permute-start.36) | collective-permute-done | bytes 147488 | tf_op jit(solution)/shard_map/ppermute | solution.py:104
  689.0 9.5 %multiply_subtract_fusion.1 = (f32[288,1,1024]{2,1,0:T(1,128)}, f32[288,1,1024]{2,1,0:T(1,128)}, f32[288,1,1024]{2,1,0:T(1,128)}) fusion(f32[288,1,1024]{2,1,0:T(1,128)S(1)} %copy-done.11, f32[288,1,1024]{2,1,0:T(1,128)S(1)} %reshape_dynamic-update-slice_fusion, f32[288,1,1024]{2,1,0:T(1,128)S(1)} %copy-done.25, f32[288,1,1024]{2,1,0:T(1,128)S(1)} %copy-done.26), kind=kLoop, calls=%fused_computation.108 | loop fusion | flops 4423680 | bytes 8257536 | tf_op jit(solution)/shard_map/sub | solution.py:73
  698.5 6.4 all-reduce.12.cloned.1.call-done.grad_in
  704.9 9.0 %stream_back.1 = f32[512,2304]{1,0:T(8,128)} custom-call(bf16[512,2304]{1,0:T(8,128)(2,1)} %all-reduce.12.cloned.1.call-done.grad_in, bf16[512,2304]{1,0:T(8,128)(2,1)} %bitcast.234, f32[8,2304]{1,0:T(8,128)} %get-tuple-element.70.gains, f32[512,2304]{1,0:T(8,128)} %get-tuple-element.89.grad_mid, f32[288,1,1024]{2,1,0:T(1,128)} %get-tuple-element.172.rest_0_, ...), custom_call_target="tpu_custom_call" | custom-call | flops 23592960 | bytes 14000000 | tf_op jit(solution)/shard_map/stream_back/pallas_call | solution.py:711
  (285 shorter events, 163.0 us)
Async XLA Ops:
  8.0 186.2 %all-reduce.6.cloned.1.call-start = ((), (), s32[]{:S(2)}) async-start(), calls=%async_computation | async-start | bytes 4718592 | tf_op jit(solution)/shard_map/psum | solution.py:99
  29.3 21.8 %collective-permute-start.3 = (bf16[2,144,1664]{2,1,0:T(8,128)(2,1)S(1)}, bf16[2,144,1664]{2,1,0:T(8,128)(2,1)S(1)}, u32[]{:S(2)}, u32[]{:S(2)}) collective-permute-start(bf16[2,144,1664]{2,1,0:T(8,128)(2,1)S(1)} %pad_maximum_fusion.17), channel_id=1, source_target_pairs={{0,16},{8,24},{16,0},{24,8},{1,17},{9,25},{17,1},{25,9},{2,18},{10... | collective-permute-start | bytes 2875400 | tf_op jit(solution)/shard_map/ppermute | solution.py:104
  32.1 21.6 %collective-permute-start.2 = (bf16[2,144,1664]{2,1,0:T(8,128)(2,1)S(1)}, bf16[2,144,1664]{2,1,0:T(8,128)(2,1)S(1)}, u32[]{:S(2)}, u32[]{:S(2)}) collective-permute-start(bf16[2,144,1664]{2,1,0:T(8,128)(2,1)S(1)} %pad_maximum_fusion.16), channel_id=1, source_target_pairs={{0,8},{8,0},{16,24},{24,16},{1,9},{9,1},{17,25},{25,17},{2,10},{10... | collective-permute-start | bytes 2875400 | tf_op jit(solution)/shard_map/ppermute | solution.py:104
  56.1 19.4 %collective-permute-start.4 = (bf16[4,288,1664]{2,1,0:T(8,128)(2,1)}, bf16[4,288,1664]{2,1,0:T(8,128)(2,1)}, u32[]{:S(2)}, u32[]{:S(2)}) collective-permute-start(bf16[4,288,1664]{2,1,0:T(8,128)(2,1)} %pad_maximum_fusion.2.near), channel_id=1, source_target_pairs={{0,4},{4,0},{1,5},{5,1},{2,6},{6,2},{3,7},{7,3},{8,12},{12,8},{9,1... | collective-permute-start | bytes 11501576 | tf_op jit(solution)/shard_map/ppermute | solution.py:104
  57.0 17.6 %collective-permute-start.5 = (bf16[144,2304]{1,0:T(8,128)(2,1)}, bf16[144,2304]{1,0:T(8,128)(2,1)}, u32[]{:S(2)}, u32[]{:S(2)}) collective-permute-start(bf16[144,2304]{1,0:T(8,128)(2,1)} %get-tuple-element.72), channel_id=1, source_target_pairs={{0,8},{8,0},{16,24},{24,16},{1,9},{9,1},{17,25},{25,17},{2,10},{10... | collective-permute-start | bytes 1990664 | tf_op jit(solution)/shard_map/ppermute | solution.py:104
  98.7 131.6 %all-gather.2.cloned.1.call-start = ((), (), s32[]{:S(2)}) async-start(), calls=%async_computation.1 | async-start | bytes 23887872 | tf_op jit(solution)/shard_map/all_gather | solution.py:758
  99.3 263.4 %all-reduce.8.cloned.1.call-start = ((), (), s32[]{:S(2)}) async-start(), calls=%async_computation.2 | async-start | bytes 4718592 | tf_op jit(solution)/shard_map/psum | solution.py:99
  101.0 50.2 %collective-permute-start.9 = (bf16[2,144,2304]{2,1,0:T(8,128)(2,1)S(1)}, bf16[2,144,2304]{2,1,0:T(8,128)(2,1)S(1)}, u32[]{:S(2)}, u32[]{:S(2)}) collective-permute-start(bf16[2,144,2304]{2,1,0:T(8,128)(2,1)S(1)} %pad_maximum_fusion.8), channel_id=1, source_target_pairs={{0,16},{8,24},{16,0},{24,8},{1,17},{9,25},{17,1},{25,9},{2,18},{10... | collective-permute-start | bytes 3981320 | tf_op jit(solution)/shard_map/ppermute | solution.py:104
  102.8 52.2 %collective-permute-start.8 = (bf16[2,144,2304]{2,1,0:T(8,128)(2,1)S(1)}, bf16[2,144,2304]{2,1,0:T(8,128)(2,1)S(1)}, u32[]{:S(2)}, u32[]{:S(2)}) collective-permute-start(bf16[2,144,2304]{2,1,0:T(8,128)(2,1)S(1)} %pad_maximum_fusion.7), channel_id=1, source_target_pairs={{0,8},{8,0},{16,24},{24,16},{1,9},{9,1},{17,25},{25,17},{2,10},{10... | collective-permute-start | bytes 3981320 | tf_op jit(solution)/shard_map/ppermute | solution.py:104
  267.0 273.5 %all-reduce.10.cloned.1.call-start = ((), (), s32[]{:S(2)}) async-start(), calls=%async_computation.3 | async-start | bytes 4718592 | tf_op jit(solution)/shard_map/psum | solution.py:99
  275.6 378.9 %collective-permute-start.27 = (bf16[512,1152]{0,1:T(8,128)(2,1)}, bf16[512,1152]{0,1:T(8,128)(2,1)}, u32[]{:S(2)}, u32[]{:S(2)}) collective-permute-start(bf16[512,1152]{0,1:T(8,128)(2,1)} %pad_maximum_fusion.14), channel_id=1, source_target_pairs={{0,4},{4,0},{1,5},{5,1},{2,6},{6,2},{3,7},{7,3},{8,12},{12,8},{9,1... | collective-permute-start | bytes 3538952 | tf_op jit(solution)/shard_map/ppermute | solution.py:104
  277.4 370.9 %collective-permute-start.34 = (bf16[512,512]{1,0:T(8,128)(2,1)}, bf16[512,512]{1,0:T(8,128)(2,1)}, u32[]{:S(2)}, u32[]{:S(2)}) collective-permute-start(bf16[512,512]{1,0:T(8,128)(2,1)} %get-tuple-element.76.attended), channel_id=1, source_target_pairs={{0,4},{4,0},{1,5},{5,1},{2,6},{6,2},{3,7},{7,3},{8,12},{12,8},{9,1... | collective-permute-start | bytes 1572872 | tf_op jit(solution)/shard_map/ppermute | solution.py:104
  278.3 139.7 %collective-permute-start.12 = (bf16[512,2304]{1,0:T(8,128)(2,1)}, bf16[512,2304]{1,0:T(8,128)(2,1)}, u32[]{:S(2)}, u32[]{:S(2)}) collective-permute-start(bf16[512,2304]{1,0:T(8,128)(2,1)} %get-tuple-element.71.hidden), channel_id=1, source_target_pairs={{0,4},{4,0},{1,5},{5,1},{2,6},{6,2},{3,7},{7,3},{8,12},{12,8},{9,1... | collective-permute-start | bytes 7077896 | tf_op jit(solution)/shard_map/ppermute | solution.py:104
  286.5 142.5 %collective-permute-start.17 = (bf16[512,1152]{0,1:T(8,128)(2,1)}, bf16[512,1152]{0,1:T(8,128)(2,1)}, u32[]{:S(2)}, u32[]{:S(2)}) collective-permute-start(bf16[512,1152]{0,1:T(8,128)(2,1)} %pad_maximum_fusion.13), channel_id=1, source_target_pairs={{0,4},{4,0},{1,5},{5,1},{2,6},{6,2},{3,7},{7,3},{8,12},{12,8},{9,1... | collective-permute-start | bytes 3538952 | tf_op jit(solution)/shard_map/ppermute | solution.py:104
  409.8 295.1 %all-reduce.12.cloned.1.call-start = ((), (), s32[]{:S(2)}) async-start(), calls=%async_computation.4 | async-start | bytes 4718592 | tf_op jit(solution)/shard_map/psum | solution.py:99
  418.0 21.6 %collective-permute-start.21 = (bf16[512,2304]{1,0:T(8,128)(2,1)S(1)}, bf16[512,2304]{1,0:T(8,128)(2,1)}, u32[]{:S(2)}, u32[]{:S(2)}) collective-permute-start(bf16[512,2304]{1,0:T(8,128)(2,1)S(1)} %copy-done.45), channel_id=1, source_target_pairs={{0,4},{4,0},{1,5},{5,1},{2,6},{6,2},{3,7},{7,3},{8,12},{12,8},{9,1... | collective-permute-start | bytes 7077896 | tf_op jit(solution)/shard_map/ppermute | solution.py:104
  429.0 31.4 %collective-permute-start.13 = (bf16[2,144,2304]{2,1,0:T(8,128)(2,1)}, bf16[2,144,2304]{2,1,0:T(8,128)(2,1)}, u32[]{:S(2)}, u32[]{:S(2)}) collective-permute-start(bf16[2,144,2304]{2,1,0:T(8,128)(2,1)} %pad_maximum_fusion.9), channel_id=1, source_target_pairs={{0,8},{8,0},{16,24},{24,16},{1,9},{9,1},{17,25},{25,17},{2,10},{10... | collective-permute-start | bytes 3981320 | tf_op jit(solution)/shard_map/ppermute | solution.py:104
  430.2 32.3 %collective-permute-start.15 = (bf16[2,144,2304]{2,1,0:T(8,128)(2,1)}, bf16[2,144,2304]{2,1,0:T(8,128)(2,1)}, u32[]{:S(2)}, u32[]{:S(2)}) collective-permute-start(bf16[2,144,2304]{2,1,0:T(8,128)(2,1)} %stack.152), channel_id=1, source_target_pairs={{0,16},{8,24},{16,0},{24,8},{1,17},{9,25},{17,1},{25,9},{2,18},{10... | collective-permute-start | bytes 3981320 | tf_op jit(solution)/shard_map/ppermute | solution.py:104
  439.6 73.2 %collective-permute-start.20 = (bf16[2,144,2304]{2,1,0:T(8,128)(2,1)S(1)}, bf16[2,144,2304]{2,1,0:T(8,128)(2,1)}, u32[]{:S(2)}, u32[]{:S(2)}) collective-permute-start(bf16[2,144,2304]{2,1,0:T(8,128)(2,1)S(1)} %stack.153), channel_id=1, source_target_pairs={{0,16},{8,24},{16,0},{24,8},{1,17},{9,25},{17,1},{25,9},{2,18},{10... | collective-permute-start | bytes 3981320 | tf_op jit(solution)/shard_map/ppermute | solution.py:104
  464.3 39.7 %collective-permute-start.14 = (bf16[144,2304]{1,0:T(8,128)(2,1)S(1)}, bf16[144,2304]{1,0:T(8,128)(2,1)S(1)}, u32[]{:S(2)}, u32[]{:S(2)}) collective-permute-start(bf16[144,2304]{1,0:T(8,128)(2,1)S(1)} %get-tuple-element.192), channel_id=1, source_target_pairs={{0,16},{8,24},{16,0},{24,8},{1,17},{9,25},{17,1},{25,9},{2,18},{10... | collective-permute-start | bytes 1990664 | tf_op jit(solution)/shard_map/ppermute | solution.py:104
  465.8 38.9 %collective-permute-start.16 = (bf16[144,2304]{1,0:T(8,128)(2,1)S(1)}, bf16[144,2304]{1,0:T(8,128)(2,1)S(1)}, u32[]{:S(2)}, u32[]{:S(2)}) collective-permute-start(bf16[144,2304]{1,0:T(8,128)(2,1)S(1)} %get-tuple-element.193), channel_id=1, source_target_pairs={{0,8},{8,0},{16,24},{24,16},{1,9},{9,1},{17,25},{25,17},{2,10},{10... | collective-permute-start | bytes 1990664 | tf_op jit(solution)/shard_map/ppermute | solution.py:104
  503.9 32.1 %collective-permute-start.19 = (bf16[2,144,2304]{2,1,0:T(8,128)(2,1)S(1)}, bf16[2,144,2304]{2,1,0:T(8,128)(2,1)S(1)}, u32[]{:S(2)}, u32[]{:S(2)}) collective-permute-start(bf16[2,144,2304]{2,1,0:T(8,128)(2,1)S(1)} %pad_maximum_fusion.10), channel_id=1, source_target_pairs={{0,8},{8,0},{16,24},{24,16},{1,9},{9,1},{17,25},{25,17},{2,10},{10... | collective-permute-start | bytes 3981320 | tf_op jit(solution)/shard_map/ppermute | solution.py:104
  504.7 65.5 %collective-permute-start.26 = (bf16[2,144,2304]{2,1,0:T(8,128)(2,1)}, bf16[2,144,2304]{2,1,0:T(8,128)(2,1)}, u32[]{:S(2)}, u32[]{:S(2)}) collective-permute-start(bf16[2,144,2304]{2,1,0:T(8,128)(2,1)} %stack.154), channel_id=1, source_target_pairs={{0,16},{8,24},{16,0},{24,8},{1,17},{9,25},{17,1},{25,9},{2,18},{10... | collective-permute-start | bytes 3981320 | tf_op jit(solution)/shard_map/ppermute | solution.py:104
  512.8 58.0 %collective-permute-start.25 = (bf16[2,144,2304]{2,1,0:T(8,128)(2,1)}, bf16[2,144,2304]{2,1,0:T(8,128)(2,1)}, u32[]{:S(2)}, u32[]{:S(2)}) collective-permute-start(bf16[2,144,2304]{2,1,0:T(8,128)(2,1)} %pad_maximum_fusion.11), channel_id=1, source_target_pairs={{0,8},{8,0},{16,24},{24,16},{1,9},{9,1},{17,25},{25,17},{2,10},{10... | collective-permute-start | bytes 3981320 | tf_op jit(solution)/shard_map/ppermute | solution.py:104
  539.0 36.0 %collective-permute-start.23 = (bf16[144,2304]{1,0:T(8,128)(2,1)}, bf16[144,2304]{1,0:T(8,128)(2,1)}, u32[]{:S(2)}, u32[]{:S(2)}) collective-permute-start(bf16[144,2304]{1,0:T(8,128)(2,1)} %get-tuple-element.187.rest_1_), channel_id=1, source_target_pairs={{0,16},{8,24},{16,0},{24,8},{1,17},{9,25},{17,1},{25,9},{2,18},{10... | collective-permute-start | bytes 1990664 | tf_op jit(solution)/shard_map/ppermute | solution.py:104
  570.9 18.9 %collective-permute-start.22 = (bf16[2,512,256]{2,1,0:T(8,128)(2,1)}, bf16[2,512,256]{2,1,0:T(8,128)(2,1)S(1)}, u32[]{:S(2)}, u32[]{:S(2)}) collective-permute-start(bf16[2,512,256]{2,1,0:T(8,128)(2,1)} %get-tuple-element.87), channel_id=1, source_target_pairs={{4,0},{5,1},{6,2},{7,3},{12,8},{13,9},{14,10},{15,11},{20,16},{21,... | collective-permute-start | bytes 1572872 | tf_op jit(solution)/shard_map/ppermute | solution.py:27
  575.0 34.9 %collective-permute-start.39 = (bf16[144,2304]{1,0:T(8,128)(2,1)}, bf16[144,2304]{1,0:T(8,128)(2,1)}, u32[]{:S(2)}, u32[]{:S(2)}) collective-permute-start(bf16[144,2304]{1,0:T(8,128)(2,1)} %get-tuple-element.181.rest_1_), channel_id=1, source_target_pairs={{0,16},{8,24},{16,0},{24,8},{1,17},{9,25},{17,1},{25,9},{2,18},{10... | collective-permute-start | bytes 1990664 | tf_op jit(solution)/shard_map/ppermute | solution.py:104
  585.4 24.6 %collective-permute-start.40 = (bf16[144,2304]{1,0:T(8,128)(2,1)S(1)}, bf16[144,2304]{1,0:T(8,128)(2,1)}, u32[]{:S(2)}, u32[]{:S(2)}) collective-permute-start(bf16[144,2304]{1,0:T(8,128)(2,1)S(1)} %get-tuple-element.180.rest_2_), channel_id=1, source_target_pairs={{0,8},{8,0},{16,24},{24,16},{1,9},{9,1},{17,25},{25,17},{2,10},{10... | collective-permute-start | bytes 1990664 | tf_op jit(solution)/shard_map/ppermute | solution.py:104
  609.3 39.0 %collective-permute-start.33 = (bf16[512,1152]{0,1:T(8,128)(2,1)}, bf16[512,1152]{0,1:T(8,128)(2,1)}, u32[]{:S(2)}, u32[]{:S(2)}) collective-permute-start(bf16[512,1152]{0,1:T(8,128)(2,1)} %pad_maximum_fusion.15), channel_id=1, source_target_pairs={{0,4},{4,0},{1,5},{5,1},{2,6},{6,2},{3,7},{7,3},{8,12},{12,8},{9,1... | collective-permute-start | bytes 3538952 | tf_op jit(solution)/shard_map/ppermute | solution.py:104
  609.9 44.6 %collective-permute-start.28 = (bf16[512,1024]{1,0:T(8,128)(2,1)}, bf16[512,1024]{1,0:T(8,128)(2,1)}, u32[]{:S(2)}, u32[]{:S(2)}) collective-permute-start(bf16[512,1024]{1,0:T(8,128)(2,1)} %get-tuple-element.91), channel_id=1, source_target_pairs={{0,4},{4,0},{1,5},{5,1},{2,6},{6,2},{3,7},{7,3},{8,12},{12,8},{9,1... | collective-permute-start | bytes 3145736 | tf_op jit(solution)/shard_map/ppermute | solution.py:104
  618.6 28.1 %collective-permute-start.44 = (f32[4,2304]{1,0:T(4,128)S(1)}, f32[4,2304]{1,0:T(4,128)S(1)}, u32[]{:S(2)}, u32[]{:S(2)}) collective-permute-start(f32[4,2304]{1,0:T(4,128)S(1)} %add.457), channel_id=1, source_target_pairs={{0,1},{1,0},{2,3},{3,2},{4,5},{5,4},{6,7},{7,6},{8,9},{9,8},{10,11... | collective-permute-start | bytes 110600 | tf_op jit(solution)/shard_map/ppermute | solution.py:104
  646.7 17.8 %collective-permute-start.45 = (f32[4,2304]{1,0:T(4,128)S(1)}, f32[4,2304]{1,0:T(4,128)S(1)}, u32[]{:S(2)}, u32[]{:S(2)}) collective-permute-start(f32[4,2304]{1,0:T(4,128)S(1)} %add.458), channel_id=1, source_target_pairs={{0,2},{1,3},{2,0},{3,1},{4,6},{5,7},{6,4},{7,5},{8,10},{9,11},{10,... | collective-permute-start | bytes 110600 | tf_op jit(solution)/shard_map/ppermute | solution.py:104
  (68 other events, 746.6 us)
Sparse Core Ops, SparseCore 0:
  98.9 95.2 all-reduce.5
  267.1 95.6 all-reduce.7
  409.9 94.6 all-reduce.9
  609.4 95.4 all-reduce.11
Sparse Core Ops, SparseCore 1:
  101.7 128.6 all-gather.1

commit v2 on v1

--- a/solution.py
+++ b/solution.py
@@ -1,6 +1,8 @@
+import functools
 import jax
 import jax.numpy as jnp
 from jax import lax
+from jax.experimental.layout import Layout, with_layout_constraint
 from jax.experimental import pallas as pl
 from jax.experimental.pallas import tpu as pltpu
 from jax.sharding import PartitionSpec as P
@@ -104,25 +106,24 @@
     return lax.ppermute(value, axis, [(source, source ^ bit) for source in range(count)])
 
 
-def gather_begin(shard):
-    half = shard.shape[0] // 2
-    low, high = shard[:half], shard[half:]
-    return low, high, swap(low, "batch", 1), swap(high, "batch", 2)
-
-
-def gather_end(state):
-    low, high, low_one, high_two = state
-    low_far = swap(jnp.stack([low, low_one]), "batch", 2)
-    high_far = swap(jnp.stack([high, high_two]), "batch", 1)
-    near = jnp.stack(
-        [
-            jnp.concatenate([low, high]),
-            jnp.concatenate([low_one, high_far[0]]),
-            jnp.concatenate([low_far[0], high_two]),
-            jnp.concatenate([low_far[1], high_far[1]]),
-        ]
-    )
-    return near, swap(near, "seq", 1)
+def after(value, *earlier):
+    return lax.optimization_barrier((value, earlier))[0]
+
+
+def trade(value, turn):
+    pairs = []
+    for chip in range(4):
+        for core in range(2):
+            pairs.append((chip * 2 + core, (chip ^ (1 + (core ^ turn))) * 2 + core))
+    return lax.ppermute(value, ("batch", "seq"), pairs)
+
+
+def offsets(owner):
+    return (0, 1 + owner, 2 - owner, 3)
+
+
+def gather_end(shard, first, second):
+    return jnp.concatenate([shard[None], first[None], second], axis=0)
 
 
 def own_blocks(wide):
@@ -132,8 +133,8 @@
     halves = []
     for owner in (core, 1 - core):
         parts = [
-            lax.dynamic_index_in_dim(split, (chip ^ k) * 2 + owner, 1, keepdims=False)
-            for k in range(4)
+            lax.dynamic_index_in_dim(split, (chip ^ offset) * 2 + owner, 1, keepdims=False)
+            for offset in offsets(owner)
         ]
         halves.append(jnp.concatenate(parts, axis=1))
     return halves
@@ -150,28 +151,26 @@
 
 
 def scatter_begin(local):
-    half = local.shape[1] // 2
-    state = []
-    for part, first, second in ((local[:, :half], 1, 2), (local[:, half:], 2, 1)):
-        got = swap(jnp.stack([part[first], part[3]]), "batch", first)
-        far = part[second].astype(jnp.float32) + got[1].astype(jnp.float32)
-        state.append((part[0], got[0], far.astype(jnp.bfloat16)))
-    return state
+    got = trade(jnp.stack([local[1], local[3]]), 0)
+    far = local[2].astype(jnp.float32) + got[1].astype(jnp.float32)
+    return local[0], got[0], far.astype(jnp.bfloat16)
 
 
 def scatter_end(state):
-    total = []
-    for (own, got, far), second in zip(state, (2, 1)):
-        got_far = swap(far, "batch", second)
-        near = own.astype(jnp.float32) + got.astype(jnp.float32)
-        total.append(near + got_far.astype(jnp.float32))
-    return jnp.concatenate(total, axis=0)
+    own, got, far = state
+    return own, got, trade(far, 1)
 
 
 def everywhere_sum(value):
     for axis, bit in (("seq", 1), ("batch", 1), ("batch", 2), ("tensor", 1), ("tensor", 2)):
         value = value + swap(value, axis, bit)
     return value
+
+
+FFN_TILE = 768
+ROW_CHUNK = 16
+ROW_UNROLL = 4
+MID_ROWS = 128
 
 
 def spec_any():
@@ -225,6 +224,13 @@
     inner = upstream * (1.0 + gain)
     pulled = scale * (inner - normed * jnp.mean(normed * inner, axis=-1, keepdims=True))
     return pulled, upstream * normed
+
+
+def fold_rows(values):
+    total = values[:8]
+    for start in range(8, values.shape[0], 8):
+        total += values[start : start + 8]
+    return total
 
 
 def fetch_rows(place, near, far, target, sems, column, columns):
@@ -233,7 +239,9 @@
     copies = []
     for k in range(4):
         for which, source in enumerate((near, far)):
-            row = ((k ^ chip) * 2 + (which ^ core)) * rows
+            owner = which ^ core
+            offset = (0, 1 + owner, 2 - owner, 3)[k]
+            row = ((offset ^ chip) * 2 + owner) * rows
             copies.append(
                 pltpu.make_async_copy(
                     source.at[k, :, pl.ds(column, columns)],
@@ -241,8 +249,6 @@
                     sems.at[k * 2 + which],
                 )
             )
-    for copy in copies:
-        copy.start()
     return copies
 
 
@@ -255,7 +261,10 @@
 
 
 def arrange_kernel(place, near, far, result, sems):
-    for copy in fetch_rows(place, near, far, result, sems, 0, result.shape[1]):
+    copies = fetch_rows(place, near, far, result, sems, 0, result.shape[1])
+    for copy in copies:
+        copy.start()
+    for copy in copies:
         copy.wait()
 
 
@@ -276,14 +285,16 @@
     queries, pair, attn_in, gains, weight, sems = rest[-6:]
     copies = fetch_rows(place, near, far, weight, sems, 0, weight.shape[1])
     for copy in copies:
+        copy.start()
+    for copy in copies:
         copy.wait()
     width = (GROUP + 2) * HEAD_DIM
     tail = weight[:, width + GROUP * HEAD_DIM :].astype(jnp.float32)
     gains[...] = jnp.transpose(tail)[:8]
     gain = 1.0 + gains[0:1, :]
-    chunk = 16
-
-    @pl.loop(0, x.shape[0] // chunk, unroll=2)
+    chunk = ROW_CHUNK
+
+    @pl.loop(0, x.shape[0] // chunk, unroll=ROW_UNROLL)
     def _(step):
         rows = pl.ds(pl.multiple_of(step * chunk, chunk), chunk)
         stream = x[rows, :].astype(jnp.float32)
@@ -333,9 +344,12 @@
     return bent, powers
 
 
-def attend_kernel(place, queries, pair, behind, near, far, attended, result, weight, sems):
+def attend_kernel(place, queries, pair, behind, near, far, *rest):
+    attended, result, weight, sems = rest[-4:]
     width = (GROUP + 2) * HEAD_DIM
     copies = fetch_rows(place, near, far, weight, sems, width, GROUP * HEAD_DIM)
+    for copy in copies:
+        copy.start()
     core = place[1]
     chunk = 128
     tokens = queries.shape[0]
@@ -360,12 +374,12 @@
         result[:, column : column + tile] = part.astype(jnp.bfloat16)
 
 
-def attend(place, queries, pair, behind, near, far, width):
+def attend(place, queries, pair, behind, near, far, width, *earlier):
     tokens = queries.shape[0]
     bf16 = jnp.bfloat16
     return pl.pallas_call(
         attend_kernel,
-        in_specs=[spec_smem(), spec_vmem(), spec_vmem(), spec_vmem(), spec_any(), spec_any()],
+        in_specs=[spec_smem()] + [spec_vmem()] * 3 + [spec_any()] * (2 + len(earlier)),
         out_specs=[spec_vmem()] * 2,
         out_shape=[shaped((tokens, GROUP * HEAD_DIM), bf16), shaped((tokens, width), bf16)],
         scratch_shapes=[
@@ -375,168 +389,268 @@
         compiler_params=kernel_params(),
         cost_estimate=cost(4 * tokens * width * 1024, 8_000_000),
         name="attend",
-    )(place, queries, pair, behind, near, far)
-
-
-def widen_kernel(attn_out, x, gains, ffn, *rest):
-    ffn_in, hidden, by_gate, by_up = rest[-4:]
-    chunk = 16
-
-    @pl.when(pl.program_id(0) == 0)
-    def _():
-        @pl.loop(0, x.shape[0] // chunk, unroll=2)
-        def _(step):
-            rows = pl.ds(pl.multiple_of(step * chunk, chunk), chunk)
-            out = attn_out[rows, :].astype(jnp.float32)
-            mid = x[rows, :].astype(jnp.float32) + out * row_scale(out) * (1.0 + gains[1:2, :])
-            ffn_in[rows, :] = (mid * row_scale(mid) * (1.0 + gains[2:3, :])).astype(jnp.bfloat16)
-
-    value = ffn_in[...]
-    gate = dot_nn(value, ffn[0])
-    up = dot_nn(value, ffn[1])
-    square_of = gate * gate
-    bent = jnp.tanh(gate * (gelu_coef + gelu_coef * 0.044715 * square_of))
-    half = 0.5 + 0.5 * bent
-    curve = gate * half
-    slope = half + curve * (1.0 - bent) * (gelu_coef + 3.0 * gelu_coef * 0.044715 * square_of)
-    hidden[...] = (curve * up).astype(jnp.bfloat16)
-    by_gate[...] = (slope * up).astype(jnp.bfloat16)
-    by_up[...] = curve.astype(jnp.bfloat16)
+    )(place, queries, pair, behind, near, far, *earlier)
 
 
 def whole(shape):
     return pl.BlockSpec(shape, lambda *_: (0,) * len(shape))
 
 
-def widen(attn_out, x, gains, ffn, *earlier):
+def ffn_params():
+    return pltpu.CompilerParams(vmem_limit_bytes=58 * 1024 * 1024)
+
+
+def move(source, target, sem):
+    copy = pltpu.make_async_copy(source, target, sem)
+    copy.start()
+    return copy
+
+
+def ffn_kernel(attn_out, x, gains, gate_up, down, *rest):
+    outs, (sides, gate_up_here, down_here, in_sems, down_sems, out_sems) = rest[-11:-6], rest[-6:]
+    ffn_in, hidden, by_gate, by_up, result = (sides.at[k] for k in range(5))
     tokens, width = x.shape
-    units = ffn.shape[2]
-    tile = 256
+    units = gate_up.shape[2]
+    tile = FFN_TILE
+    steps, turns = units // tile, width // tile
+
+    def load(step):
+        columns = pl.ds(pl.multiple_of(step * tile, tile), tile)
+        return pltpu.make_async_copy(
+            gate_up.at[:, :, columns], gate_up_here.at[:, :, columns], in_sems.at[step]
+        )
+
+    def load_down(turn):
+        rows = pl.ds(pl.multiple_of(turn * tile, tile), tile)
+        return pltpu.make_async_copy(down.at[rows, :], down_here.at[rows, :], down_sems.at[turn])
+
+    for step in range(steps):
+        load(step).start()
+    for turn in range(turns):
+        load_down(turn).start()
+    chunk = ROW_CHUNK
+
+    @pl.loop(0, tokens // chunk, unroll=ROW_UNROLL)
+    def _(step):
+        rows = pl.ds(pl.multiple_of(step * chunk, chunk), chunk)
+        out = attn_out[rows, :].astype(jnp.float32)
+        mid = x[rows, :].astype(jnp.float32) + out * row_scale(out) * (1.0 + gains[1:2, :])
+        ffn_in[rows, :] = (mid * row_scale(mid) * (1.0 + gains[2:3, :])).astype(jnp.bfloat16)
+
+    stores = [move(ffn_in, outs[0], out_sems.at[0])]
+
+    @pl.loop(0, steps)
+    def _(step):
+        load(step).wait()
+        columns = pl.ds(pl.multiple_of(step * tile, tile), tile)
+        for rows in (slice(None),):
+            value = ffn_in[...]
+            gate = dot_nn(value, gate_up_here[0, :, columns])
+            up = dot_nn(value, gate_up_here[1, :, columns])
+            square_of = gate * gate
+            bent = jnp.tanh(gate * (gelu_coef + gelu_coef * 0.044715 * square_of))
+            half = 0.5 + 0.5 * bent
+            curve = gate * half
+            slope = half + curve * (1.0 - bent) * (
+                gelu_coef + 3.0 * gelu_coef * 0.044715 * square_of
+            )
+            hidden[rows, columns] = (curve * up).astype(jnp.bfloat16)
+            by_gate[rows, columns] = (slope * up).astype(jnp.bfloat16)
+            by_up[rows, columns] = curve.astype(jnp.bfloat16)
+
+    for k, side in ((1, hidden), (2, by_gate), (3, by_up)):
+        stores.append(move(side, outs[k], out_sems.at[k]))
+
+    def store(turn):
+        columns = pl.ds(pl.multiple_of(turn * tile, tile), tile)
+        return pltpu.make_async_copy(
+            result.at[:, columns], outs[4].at[:, columns], out_sems.at[4 + turn]
+        )
+
+    @pl.loop(0, turns)
+    def _(turn):
+        load_down(turn).wait()
+        rows = pl.ds(pl.multiple_of(turn * tile, tile), tile)
+        result[:, rows] = dot_nt(hidden[...], down_here[rows, :]).astype(jnp.bfloat16)
+        store(turn).start()
+
+    for copy in stores:
+        copy.wait()
+    for turn in range(turns):
+        store(turn).wait()
+
+
+def ffn_forward(attn_out, x, gains, gate_up, down, *earlier):
+    tokens, width = x.shape
+    units = gate_up.shape[2]
     bf16 = jnp.bfloat16
-    columns = pl.BlockSpec((tokens, tile), lambda i: (0, i))
     return pl.pallas_call(
-        widen_kernel,
-        grid=(units // tile,),
-        in_specs=[
-            whole((tokens, width)),
-            whole((tokens, width)),
-            whole((8, width)),
-            pl.BlockSpec((2, width, tile), lambda i: (0, 0, i)),
-        ]
-        + [spec_any()] * len(earlier),
-        out_specs=[whole((tokens, width)), columns, columns, columns],
-        out_shape=[shaped((tokens, width), bf16)] + [shaped((tokens, units), bf16)] * 3,
-        compiler_params=kernel_params(),
-        cost_estimate=cost(4 * tokens * width * units, 36_000_000),
-        name="widen",
-    )(attn_out, x, gains, ffn, *earlier)
-
-
-def narrow_kernel(hidden, down, result):
-    result[...] = dot_nt(hidden[...], down[...]).astype(jnp.bfloat16)
-
-
-def narrow(hidden, down):
-    tokens, units = hidden.shape
-    width = down.shape[0]
-    tile = 256
-    return pl.pallas_call(
-        narrow_kernel,
-        grid=(width // tile,),
-        in_specs=[whole((tokens, units)), pl.BlockSpec((tile, units), lambda i: (i, 0))],
-        out_specs=pl.BlockSpec((tokens, tile), lambda i: (0, i)),
-        out_shape=shaped((tokens, width), jnp.bfloat16),
-        compiler_params=kernel_params(),
-        cost_estimate=cost(2 * tokens * width * units, 16_000_000),
-        name="narrow",
-    )(hidden, down)
-
-
-def top_back_kernel(ffn_out, top, gains, grad_ffn, gain_out):
-    chunk = 16
+        ffn_kernel,
+        in_specs=[spec_vmem()] * 3 + [spec_any()] * (2 + len(earlier)),
+        out_specs=[spec_any()] * 5,
+        out_shape=[shaped((tokens, width), bf16)]
+        + [shaped((tokens, units), bf16)] * 3
+        + [shaped((tokens, width), bf16)],
+        scratch_shapes=[
+            pltpu.VMEM((5, tokens, width), bf16),
+            pltpu.VMEM((2, width, units), bf16),
+            pltpu.VMEM((width, units), bf16),
+            pltpu.SemaphoreType.DMA((units // FFN_TILE,)),
+            pltpu.SemaphoreType.DMA((width // FFN_TILE,)),
+            pltpu.SemaphoreType.DMA((4 + width // FFN_TILE,)),
+        ],
+        compiler_params=ffn_params(),
+        cost_estimate=cost(6 * tokens * width * units, 50_000_000),
+        name="ffn_forward",
+    )(attn_out, x, gains, gate_up, down, *earlier)
+
+
+def ffn_back_kernel(ffn_out, top, gains, gate_up, down, by_gate, by_up, *rest):
+    grad_out, gate_out, up_out, gain_out, result_out = rest[-13:-8]
+    sides, grads, gate_up_here, down_here, in_sems, down_sems, gate_sems, out_sems = rest[-8:]
+    grad_ffn, result = sides.at[0], sides.at[1]
+    tokens, width = top.shape
+    units = gate_up.shape[2]
+    grad_gate, grad_up = grads.at[:, pl.ds(0, units)], grads.at[:, pl.ds(units, units)]
+    tile = FFN_TILE
+    steps, turns = units // tile, width // tile
+
+    def load_down(step):
+        columns = pl.ds(pl.multiple_of(step * tile, tile), tile)
+        return pltpu.make_async_copy(
+            down.at[:, columns], down_here.at[:, columns], down_sems.at[step]
+        )
+
+    def load(turn, which):
+        rows = pl.ds(pl.multiple_of(turn * tile, tile), tile)
+        return pltpu.make_async_copy(
+            gate_up.at[which, rows, :],
+            gate_up_here.at[rows, pl.ds(which * units, units)],
+            gate_sems.at[turn, which],
+        )
+
+    load_down(0).start()
+    factors = [
+        move(by_gate, grad_gate, in_sems.at[0]),
+        move(by_up, grad_up, in_sems.at[1]),
+    ]
+    load_down(1).start()
     gain_out[...] = jnp.zeros_like(gain_out)
-
-    @pl.loop(0, ffn_out.shape[0] // chunk, unroll=2)
+    chunk = ROW_CHUNK
+
+    @pl.loop(0, tokens // chunk, unroll=ROW_UNROLL)
     def _(step):
         rows = pl.ds(pl.multiple_of(step * chunk, chunk), chunk)
         out = ffn_out[rows, :].astype(jnp.float32)
         upstream = top[rows, :].astype(jnp.float32)
         pulled, product = norm_pull(out, row_scale(out), gains[3:4, :], upstream)
         grad_ffn[rows, :] = pulled.astype(jnp.bfloat16)
-        gain_out[...] += product[:8] + product[8:]
-
-
-def top_back(ffn_out, top, gains):
+        gain_out[...] += fold_rows(product)
+
+    stores = [move(grad_ffn, grad_out, out_sems.at[0])]
+    for copy in factors:
+        copy.wait()
+
+    @pl.loop(0, steps)
+    def _(step):
+        load_down(step).wait()
+
+        @pl.when(step + 2 < steps)
+        def _():
+            load_down(step + 2).start()
+
+        @pl.when(step + 2 >= steps)
+        def _():
+            load(step + 2 - steps, 0).start()
+            load(step + 2 - steps, 1).start()
+
+        columns = pl.ds(pl.multiple_of(step * tile, tile), tile)
+        for start in range(0, tokens, tokens // 2):
+            rows = pl.ds(start, tokens // 2)
+            grad_hidden = dot_nn(grad_ffn[rows, :], down_here[:, columns])
+            one = grad_hidden * grad_gate[rows, columns].astype(jnp.float32)
+            two = grad_hidden * grad_up[rows, columns].astype(jnp.float32)
+            grad_gate[rows, columns] = one.astype(jnp.bfloat16)
+            grad_up[rows, columns] = two.astype(jnp.bfloat16)
+
+    stores.append(move(grad_gate, gate_out, out_sems.at[1]))
+    stores.append(move(grad_up, up_out, out_sems.at[2]))
+
+    def store(turn):
+        columns = pl.ds(pl.multiple_of(turn * tile, tile), tile)
+        return pltpu.make_async_copy(
+            result.at[:, columns], result_out.at[:, columns], out_sems.at[3 + turn]
+        )
+
+    @pl.loop(0, turns)
+    def _(turn):
+        load(turn, 0).wait()
+        load(turn, 1).wait()
+
+        @pl.when(turn + 2 < turns)
+        def _():
+            load(turn + 2, 0).start()
+            load(turn + 2, 1).start()
+
+        rows = pl.ds(pl.multiple_of(turn * tile, tile), tile)
+        part = dot_nt(grads[...], gate_up_here[rows, :])
+        result[:, rows] = part.astype(jnp.bfloat16)
+        store(turn).start()
+
+    for copy in stores:
+        copy.wait()
+    for turn in range(turns):
+        store(turn).wait()
+
+
+def ffn_back(ffn_out, top, gains, gate_up, down, by_gate, by_up, *earlier):
     tokens, width = top.shape
-    return pl.pallas_call(
-        top_back_kernel,
-        in_specs=[spec_vmem()] * 3,
-        out_specs=[spec_vmem()] * 2,
-        out_shape=[shaped((tokens, width), jnp.bfloat16), shaped((8, width), jnp.float32)],
-        compiler_params=kernel_params(),
-        cost_estimate=cost(20 * tokens * width, 8_000_000),
-        name="top_back",
-    )(ffn_out, top, gains)
-
-
-def ffn_back_kernel(grad_ffn, down, gate_up, by_gate, by_up, *rest):
-    grad_gate, grad_up, result, total = rest[-4:]
-
-    @pl.when(pl.program_id(0) == 0)
-    def _():
-        total[...] = jnp.zeros_like(total)
-
-    grad_hidden = dot_nn(grad_ffn[...], down[...])
-    one = (grad_hidden * by_gate[...].astype(jnp.float32)).astype(jnp.bfloat16)
-    two = (grad_hidden * by_up[...].astype(jnp.float32)).astype(jnp.bfloat16)
-    grad_gate[...] = one
-    grad_up[...] = two
-    total[...] += dot_nt(one, gate_up[0]) + dot_nt(two, gate_up[1])
-
-    @pl.when(pl.program_id(0) == pl.num_programs(0) - 1)
-    def _():
-        result[...] = total[...].astype(jnp.bfloat16)
-
-
-def ffn_back(grad_ffn, down, gate_up, by_gate, by_up, *earlier):
-    tokens, width = grad_ffn.shape
     units = by_up.shape[1]
-    tile = 256
     bf16 = jnp.bfloat16
-    columns = pl.BlockSpec((tokens, tile), lambda i: (0, i))
     return pl.pallas_call(
         ffn_back_kernel,
-        grid=(units // tile,),
-        in_specs=[
-            whole((tokens, width)),
-            pl.BlockSpec((width, tile), lambda i: (0, i)),
-            pl.BlockSpec((2, width, tile), lambda i: (0, 0, i)),
-            columns,
-            columns,
-        ]
-        + [spec_any()] * len(earlier),
-        out_specs=[columns, columns, whole((tokens, width))],
+        in_specs=[spec_vmem()] * 3 + [spec_any()] * (4 + len(earlier)),
+        out_specs=[spec_any()] * 3 + [spec_vmem(), spec_any()],
         out_shape=[
+            shaped((tokens, width), bf16),
             shaped((tokens, units), bf16),
             shaped((tokens, units), bf16),
+            shaped((8, width), jnp.float32),
             shaped((tokens, width), bf16),
         ],
-        scratch_shapes=[pltpu.VMEM((tokens, width), jnp.float32)],
-        compiler_params=kernel_params(),
-        cost_estimate=cost(6 * tokens * width * units, 52_000_000),
+        scratch_shapes=[
+            pltpu.VMEM((2, tokens, width), bf16),
+            pltpu.VMEM((tokens, 2 * units), bf16),
+            pltpu.VMEM((width, 2 * units), bf16),
+            pltpu.VMEM((width, units), bf16),
+            pltpu.SemaphoreType.DMA((2,)),
+            pltpu.SemaphoreType.DMA((units // FFN_TILE,)),
+            pltpu.SemaphoreType.DMA((width // FFN_TILE, 2)),
+            pltpu.SemaphoreType.DMA((3 + width // FFN_TILE,)),
+        ],
+        compiler_params=ffn_params(),
+        cost_estimate=cost(6 * tokens * width * units, 55_000_000),
         name="ffn_back",
-    )(grad_ffn, down, gate_up, by_gate, by_up, *earlier)
+    )(ffn_out, top, gains, gate_up, down, by_gate, by_up, *earlier)
 
 
 def mid_back_kernel(place, grad_in, x, attn_out, top, gains, near, far, *rest):
     grad_mid, grad_attn, grad_att, gain_out, weight, sems = rest[-6:]
     width = (GROUP + 2) * HEAD_DIM
-    copies = fetch_rows(place, near, far, weight, sems, width, GROUP * HEAD_DIM)
-    gain_out[...] = jnp.zeros_like(gain_out)
-    chunk = 16
-    tokens = x.shape[0]
-
-    @pl.loop(0, tokens // chunk, unroll=2)
+    first = pl.program_id(0) == 0
+
+    def fetch():
+        return fetch_rows(place, near, far, weight, sems, width, GROUP * HEAD_DIM)
+
+    @pl.when(first)
+    def _():
+        gain_out[...] = jnp.zeros_like(gain_out)
+        for copy in fetch():
+            copy.start()
+
+    chunk = ROW_CHUNK
+
+    @pl.loop(0, x.shape[0] // chunk, unroll=ROW_UNROLL)
     def _(step):
         rows = pl.ds(pl.multiple_of(step * chunk, chunk), chunk)
         out = attn_out[rows, :].astype(jnp.float32)
@@ -544,15 +658,18 @@
         mid = x[rows, :].astype(jnp.float32) + out * out_scale * (1.0 + gains[1:2, :])
         upstream = grad_in[rows, :].astype(jnp.float32)
         pulled, product = norm_pull(mid, row_scale(mid), gains[2:3, :], upstream)
-        gain_out[1] += product[:8] + product[8:]
+        gain_out[1] += fold_rows(product)
         at_mid = top[rows, :].astype(jnp.float32) + pulled
         grad_mid[rows, :] = at_mid
         pulled, product = norm_pull(out, out_scale, gains[1:2, :], at_mid)
-        gain_out[0] += product[:8] + product[8:]
+        gain_out[0] += fold_rows(product)
         grad_attn[rows, :] = pulled.astype(jnp.bfloat16)
 
-    for copy in copies:
-        copy.wait()
+    @pl.when(first)
+    def _():
+        for copy in fetch():
+            copy.wait()
+
     grad_att[...] = dot_nn(grad_attn[...], weight[...]).astype(jnp.bfloat16)
 
 
@@ -560,13 +677,20 @@
     tokens, width = x.shape
     heads = GROUP * HEAD_DIM
     bf16 = jnp.bfloat16
+    rows = pl.BlockSpec((MID_ROWS, width), lambda i: (i, 0))
     return pl.pallas_call(
         mid_back_kernel,
+        grid=(tokens // MID_ROWS,),
         in_specs=[spec_smem()]
-        + [spec_vmem()] * 5
-        + [spec_any()] * 2
-        + [spec_any()] * len(earlier),
-        out_specs=[spec_vmem()] * 4,
+        + [rows] * 4
+        + [whole((8, width))]
+        + [spec_any()] * (2 + len(earlier)),
+        out_specs=[
+            rows,
+            rows,
+            pl.BlockSpec((MID_ROWS, heads), lambda i: (i, 0)),
+            whole((2, 8, width)),
+        ],
         out_shape=[
             shaped((tokens, width), jnp.float32),
             shaped((tokens, width), bf16),
@@ -581,8 +705,9 @@
 
 
 def attend_back_kernel(
-    place, queries, pair, behind, attended, grad_att, cosine, sine, grad_q, grad_own, grad_old, sums
+    place, queries, pair, behind, attended, grad_att, cosine, sine, *rest
 ):
+    grad_q, grad_own, grad_old, sums = rest[-4:]
     core = place[1]
     chunk = 128
     tokens = queries.shape[0]
@@ -623,12 +748,12 @@
     grad_own[1] = sums[3]
 
 
-def attend_back(place, queries, pair, behind, attended, grad_att, cosine, sine):
+def attend_back(place, queries, pair, behind, attended, grad_att, cosine, sine, *earlier):
     tokens, heads = queries.shape
     bf16 = jnp.bfloat16
     return pl.pallas_call(
         attend_back_kernel,
-        in_specs=[spec_smem()] + [spec_vmem()] * 7,
+        in_specs=[spec_smem()] + [spec_vmem()] * 7 + [spec_any()] * len(earlier),
         out_specs=[spec_vmem()] * 3,
         out_shape=[
             shaped((tokens, heads), bf16),
@@ -639,7 +764,7 @@
         compiler_params=kernel_params(),
         cost_estimate=cost(20 * tokens * 1024 * heads, 5_000_000),
         name="attend_back",
-    )(place, queries, pair, behind, attended, grad_att, cosine, sine)
+    )(place, queries, pair, behind, attended, grad_att, cosine, sine, *earlier)
 
 
 def project_back_kernel(
@@ -648,6 +773,8 @@
     proj, result, gain_out, weight, sems = rest[-5:]
     width = (GROUP + 2) * HEAD_DIM
     copies = fetch_rows(place, near, far, weight, sems, 0, width)
+    for copy in copies:
+        copy.start()
     heads = GROUP * HEAD_DIM
     proj[:, :heads] = grad_q[...]
     grad_key = grad_own[0] + grad_ahead[0].astype(jnp.float32)
@@ -662,14 +789,14 @@
     for column in range(0, result.shape[1], tile):
         part = dot_nt(proj[...], weight[column : column + tile, :])
         result[:, column : column + tile] = part.astype(jnp.bfloat16)
-    chunk = 16
-
-    @pl.loop(0, x.shape[0] // chunk, unroll=2)
+    chunk = ROW_CHUNK
+
+    @pl.loop(0, x.shape[0] // chunk, unroll=ROW_UNROLL)
     def _(step):
         rows = pl.ds(pl.multiple_of(step * chunk, chunk), chunk)
         stream = x[rows, :].astype(jnp.float32)
         product = result[rows, :].astype(jnp.float32) * (stream * row_scale(stream))
-        gain_out[...] += product[:8] + product[8:]
+        gain_out[...] += fold_rows(product)
 
 
 def project_back(place, grad_q, grad_own, grad_ahead, cosine, sine, x, near, far, *earlier):
@@ -697,16 +824,20 @@
 
 def stream_back_kernel(grad_in, x, gains, grad_mid, *rest):
     result = rest[-1]
-    stream = x[...].astype(jnp.float32)
-    pulled, _ = norm_pull(
-        stream, row_scale(stream), gains[0:1, :], grad_in[...].astype(jnp.float32)
-    )
-    result[...] = grad_mid[...] + pulled
+    chunk = ROW_CHUNK
+
+    @pl.loop(0, x.shape[0] // chunk, unroll=ROW_UNROLL)
+    def _(step):
+        rows = pl.ds(pl.multiple_of(step * chunk, chunk), chunk)
+        stream = x[rows, :].astype(jnp.float32)
+        upstream = grad_in[rows, :].astype(jnp.float32)
+        pulled, _ = norm_pull(stream, row_scale(stream), gains[0:1, :], upstream)
+        result[rows, :] = grad_mid[rows, :] + pulled
 
 
 def stream_back(grad_in, x, gains, grad_mid, *earlier):
     tokens, width = x.shape
-    tile = 64
+    tile = MID_ROWS
     rows = pl.BlockSpec((tile, width), lambda i: (i, 0))
     return pl.pallas_call(
         stream_back_kernel,
@@ -718,6 +849,77 @@
         cost_estimate=cost(20 * tokens * width, 14_000_000),
         name="stream_back",
     )(grad_in, x, gains, grad_mid, *earlier)
+
+
+def flat(values):
+    rows, pair, width = values.shape
+    lanes = width // 128
+    if pair == 1:
+        return values.reshape(rows * lanes, 128)
+    tiles = with_layout_constraint(
+        values.reshape(rows, pair, lanes, 128), Layout(major_to_minor=(0, 2, 1, 3))
+    )
+    return tiles.transpose(0, 2, 1, 3).reshape(rows * pair * lanes, 128)
+
+
+def unflat(values, shape):
+    rows, pair, width = shape
+    lanes = width // 128
+    if pair == 1:
+        return values.reshape(shape)
+    tiles = values.reshape(rows, lanes, pair, 128).transpose(0, 2, 1, 3)
+    return with_layout_constraint(tiles, Layout(major_to_minor=(0, 2, 1, 3))).reshape(shape)
+
+
+def join_kernel(*refs):
+    result = refs[-1]
+    for which in range(2):
+        own, got, far = (refs[which * 3 + k][...].astype(jnp.float32) for k in range(3))
+        result[:, which, :] = own + got + far
+
+
+def join(gate, up):
+    rows, width = gate[0].shape
+    tile = 32
+    block = pl.BlockSpec((tile, width), lambda i: (i, 0))
+    return pl.pallas_call(
+        join_kernel,
+        grid=(rows // tile,),
+        in_specs=[block] * 6,
+        out_specs=pl.BlockSpec((tile, 2, width), lambda i: (i, 0, 0)),
+        out_shape=shaped((rows, 2, width), jnp.float32),
+        compiler_params=kernel_params(),
+        cost_estimate=cost(0, 200_000_000),
+        name="join",
+    )(*gate, *up)
+
+
+def adam_kernel(parts, decay, *refs):
+    weight, first, second = (ref[...] for ref in refs[parts : parts + 3])
+    outs = refs[parts + 3 :]
+    grad = refs[0][...].astype(jnp.float32)
+    for ref in refs[1:parts]:
+        grad += ref[...].astype(jnp.float32)
+    if parts > 1:
+        outs[-1][...] = grad
+    outs[0][...], outs[1][...], outs[2][...] = adam_step(weight, grad, first, second, decay)
+
+
+def adam(grads, weight, first, second, decay):
+    rows, width = weight.shape
+    tile = rows // 9
+    block = pl.BlockSpec((tile, width), lambda i: (i, 0))
+    count = 3 if len(grads) == 1 else 4
+    return pl.pallas_call(
+        functools.partial(adam_kernel, len(grads), decay),
+        grid=(9,),
+        in_specs=[block] * (len(grads) + 3),
+        out_specs=[block] * count,
+        out_shape=[shaped((rows, width), jnp.float32)] * count,
+        compiler_params=kernel_params(),
+        cost_estimate=cost(0, 200_000_000),
+        name="adam",
+    )(*grads, weight, first, second)
 
 
 def on_square(
@@ -748,13 +950,18 @@
     attn_cast = jnp.concatenate([qkv_weight[:, 0], out_weight.T, gains_cast], axis=1)
     gate_up_cast = gate_up_weight.astype(jnp.bfloat16).transpose(1, 0, 2)
     down_cast = down_weight.T.astype(jnp.bfloat16)
-    state, down_cast, gate_up_cast = lax.optimization_barrier(
-        (gather_begin(attn_cast.astype(jnp.bfloat16)), down_cast, gate_up_cast)
-    )
-    near, far = gather_end(state)
-    down_state = gather_begin(down_cast)
-    near, far, down_state = lax.optimization_barrier((near, far, down_state))
-    down = arrange(place, *gather_end(down_state))
+    attn_cast = attn_cast.astype(jnp.bfloat16)
+    first, down_cast, gate_up_cast = lax.optimization_barrier(
+        (trade(attn_cast, 0), down_cast, gate_up_cast)
+    )
+    second = trade(jnp.stack([attn_cast, first]), 1)
+    down_one = trade(down_cast, 0)
+    near = gather_end(attn_cast, first, second)
+    far = swap(near, "seq", 1)
+    down_one, far = lax.optimization_barrier((down_one, far))
+    down_two = trade(jnp.stack([down_cast, down_one]), 1)
+    down_near = gather_end(down_cast, down_one, down_two)
+    down = arrange(place, down_near, swap(down_near, "seq", 1))
     gate_up = lax.all_gather(gate_up_cast, plane, axis=1, tiled=True)
     positions = core * tok_rows + jnp.arange(tok_rows, dtype=jnp.int32)
     cosine, sine = rope_tables(positions, HEAD_DIM)
@@ -763,44 +970,52 @@
         place, stream, near, far, cosine, sine, gate_up_cast
     )
     behind = from_behind(pair, "seq", 1)
-    attended, attn_part = attend(place, queries, pair, behind, near, far, stream.shape[1])
+    attended, attn_part = attend(
+        place, queries, pair, behind, near, far, stream.shape[1], down_two
+    )
     attn_out = tensor_sum(attn_part)
-    ffn_in, hidden, by_gate, by_up = widen(attn_out, stream, gains, gate_up)
-    ffn_out = tensor_sum(narrow(hidden, down))
-
-    grad_ffn, gain_ffn = top_back(ffn_out, top, gains)
-    grad_gate, grad_up, grad_ffn_part = ffn_back(grad_ffn, down, gate_up, by_gate, by_up)
-    grad_ffn_in = tensor_sum(grad_ffn_part)
+    ffn_in, hidden, by_gate, by_up, ffn_part = ffn_forward(attn_out, stream, gains, gate_up, down)
+    ffn_out = tensor_sum(ffn_part)
+
+    att_both = jnp.concatenate([attended, swap(attended, "seq", 1)], axis=0)
+    attn_in_both = both_cores(attn_in)
     ffn_in_both = both_cores(ffn_in)
     hidden_both = jnp.concatenate([hidden, swap(hidden, "seq", 1)], axis=0)
+    grad_ffn, grad_gate, grad_up, gain_ffn, grad_ffn_part = ffn_back(
+        ffn_out, top, gains, gate_up, down, by_gate, by_up, att_both, attn_in_both, ffn_in_both,
+        hidden_both
+    )
+    grad_ffn_in = tensor_sum(grad_ffn_part)
     grad_gate_both = jnp.concatenate([grad_gate, swap(grad_gate, "seq", 1)], axis=0)
     grad_up_both = jnp.concatenate([grad_up, swap(grad_up, "seq", 1)], axis=0)
-    down_grad = scatter_end(scatter_begin(weight_local(both_cores(grad_ffn), hidden_both)))
-    gate_state = scatter_begin(weight_local(ffn_in_both, grad_gate_both))
+    down_local = weight_local(both_cores(grad_ffn), hidden_both)
+    gate_local = weight_local(ffn_in_both, grad_gate_both)
     up_local = weight_local(ffn_in_both, grad_up_both)
+    down_state = scatter_begin(down_local)
+    gate_state = scatter_begin(gate_local)
+    up_state = scatter_begin(up_local)
+    down_grad = scatter_end(down_state)
 
     grad_mid, grad_attn, grad_att, gain_mid = mid_back(
-        place, grad_ffn_in, stream, attn_out, top, gains, near, far, down_grad, gate_state[0][2],
-        gate_state[1][2], up_local
+        place, grad_ffn_in, stream, attn_out, top, gains, near, far, down_state[2], gate_state[1]
     )
     gate_grad = scatter_end(gate_state)
-    up_state = scatter_begin(up_local)
     grad_q, grad_own, grad_old = attend_back(
         place, queries, pair, behind, attended, grad_att, cosine, sine
     )
     grad_ahead = from_behind(grad_old, "seq", -1)
     grad_proj, grad_attn_part, gain_attn = project_back(
-        place, grad_q, grad_own, grad_ahead, cosine, sine, stream, near, far, gate_grad,
-        up_state[0][2], up_state[1][2]
+        place, grad_q, grad_own, grad_ahead, cosine, sine, stream, near, far, down_grad[2], up_state[1]
     )
     grad_attn_in = tensor_sum(grad_attn_part)
     up_grad = scatter_end(up_state)
-    gate_up_grad = jnp.stack([gate_grad, up_grad], axis=1)
-
-    att_both = jnp.concatenate([attended, swap(attended, "seq", 1)], axis=0)
-    out_grad = scatter_end(scatter_begin(weight_local(both_cores(grad_attn), att_both)))
+    gate_up_grad = join(gate_grad, up_grad)
+
+    out_local = weight_local(both_cores(grad_attn), att_both)
+    out_grad = scatter_end(scatter_begin(out_local))
     proj_both = jnp.concatenate([grad_proj, swap(grad_proj, "seq", 1)], axis=0)
-    qkv_grad = scatter_end(scatter_begin(weight_local(both_cores(attn_in), proj_both)))[:, None]
+    qkv_local = weight_local(attn_in_both, proj_both)
+    qkv_grad = sum(part.astype(jnp.float32) for part in scatter_end(scatter_begin(qkv_local)))[:, None]
     gains_rest = jnp.concatenate([gain_mid, gain_ffn[None]], axis=0).sum(axis=1)
     gains_rest = jnp.where(lax.axis_index("tensor") == 0, gains_rest, 0.0)
     gains_total = everywhere_sum(jnp.concatenate([gain_attn.sum(axis=0)[None], gains_rest], axis=0))
@@ -811,17 +1026,28 @@
     attn_float = attn_out.astype(jnp.float32)
     mid_stream = stream.astype(jnp.float32) + rms_norm(attn_float, gains[1])
     layer_out = (mid_stream + rms_norm(ffn_out.astype(jnp.float32), gains[3])).astype(jnp.bfloat16)
-    qkv_new, qkv_first_new, qkv_second_new = adam_step(
-        qkv_weight, qkv_grad, qkv_first, qkv_second, decay_rate
-    )
-    out_new, out_first_new, out_second_new = adam_step(
-        out_weight.T, out_grad, out_first.T, out_second.T, decay_rate
-    )
-    gate_up_new, gate_up_first_new, gate_up_second_new = adam_step(
-        gate_up_weight, gate_up_grad, gate_up_first, gate_up_second, decay_rate
-    )
-    down_new, down_first_new, down_second_new = adam_step(
-        down_weight.T, down_grad, down_first.T, down_second.T, decay_rate
+    qkv_shape, gate_up_shape = qkv_weight.shape, gate_up_weight.shape
+    qkv_new, qkv_first_new, qkv_second_new = (
+        unflat(value, qkv_shape)
+        for value in adam(
+            [flat(qkv_grad)], flat(qkv_weight), flat(qkv_first), flat(qkv_second), decay_rate
+        )
+    )
+    out_new, out_first_new, out_second_new, out_grad = adam(
+        out_grad, out_weight.T, out_first.T, out_second.T, decay_rate
+    )
+    gate_up_new, gate_up_first_new, gate_up_second_new = (
+        unflat(value, gate_up_shape)
+        for value in adam(
+            [flat(gate_up_grad)],
+            flat(gate_up_weight),
+            flat(gate_up_first),
+            flat(gate_up_second),
+            decay_rate,
+        )
+    )
+    down_new, down_first_new, down_second_new, down_grad = adam(
+        down_grad, down_weight.T, down_first.T, down_second.T, decay_rate
     )
     gains_new, gains_first_new, gains_second_new = adam_step(
         norm_gains, gains_grad, gains_first, gains_second, 0.0

time: 730 us -> 664 us (0.910)
  other arithmetic: 93.6 us -> 38.4 us
  waiting for transfers between devices: 330 us -> 275 us
  local copies, waits for them, and re-layouts: 48.5 us -> 82.5 us
  Pallas kernels: 156 us -> 171 us
  starting transfers between devices: 44.5 us -> 32.6 us
    ppermute x44 -> x16, waiting for transfers between devices: 192 us -> 10.3 us  [swap(): lax.ppermute(value, axis, [(source, source ^ bit) for source in range(cou...]
    ppermute x0 -> x14, waiting for transfers between devices: none -> 107 us  [trade(): return lax.ppermute(value, ('batch', 'seq'), pairs)]
    psum x4, waiting for transfers between devices: 99.5 us -> 139 us  [tensor_sum(): return lax.psum(part, 'tensor')]
    sub x3 -> x1, other arithmetic: 38.3 us -> 0.7 us  [adam_step(): weight - learn_rate * (first_hat / (jnp.sqrt(second_hat) + adam_eps) + de...]
    ppermute x44 -> x16, starting transfers between devices: 41 us -> 6.62 us  [swap(): lax.ppermute(value, axis, [(source, source ^ bit) for source in range(cou...]
    ppermute x0 -> x14, starting transfers between devices: none -> 22.4 us  [trade(): return lax.ppermute(value, ('batch', 'seq'), pairs)]
    all_gather x1, waiting for transfers between devices: 36.1 us -> 15.7 us  [on_square(): gate_up = lax.all_gather(gate_up_cast, plane, axis=1, tiled=True)]
    pallas_call x6 -> x9, Pallas kernels: 102 us -> 122 us  [the longest x4 42.9 us: adam(): pl.pallas_call(functools.partial(adam_kernel, len(grads), decay), grid=(9...]
  transfers between devices with their start and end apart: 51 -> 37, of which waited for: 24 -> 15; matrix products, arithmetic and copies ran while one was open for 22% -> 22% of each run, Pallas kernels for 13% -> 16%
where the time goes in v2:
time: 664 us; the launch traced here: 655 us
  waiting for transfers between devices  275 us (41%)
  Pallas kernels  171 us (26%)
  local copies, waits for them, and re-layouts  82.5 us (12%)
  matrix products  39.1 us (6%)
  other arithmetic  38.4 us (6%)
  starting transfers between devices  32.6 us (5%)
  between operations  16.3 us (2%)
    psum x4, waiting for transfers between devices, tensor_sum(): return lax.psum(part, 'tensor')  139 us
    ppermute x14, waiting for transfers between devices, trade(): return lax.ppermute(value, ('batch', 'seq'), pairs)  107 us
    pallas_call x4, Pallas kernels, adam(): pl.pallas_call(functools.partial(adam_kernel, len(grads), decay), grid=(9...  42.9 us
    dot_general x5, matrix products, rows_product(): lax.dot_general(left, right, (((0,), (0,)), ((), ())), preferred_element_...  39.1 us
    pallas_call x1, Pallas kernels, ffn_back(): pl.pallas_call(ffn_back_kernel, in_specs=[spec_vmem()] * 3 + [spec_any()]...  26.2 us
    pallas_call x1, Pallas kernels, ffn_forward(): pl.pallas_call(ffn_kernel, in_specs=[spec_vmem()] * 3 + [spec_any()] * (2...  24.3 us
    unnamed x88, local copies, waits for them, and re-layouts  22.4 us
    ppermute x14, starting transfers between devices, trade(): return lax.ppermute(value, ('batch', 'seq'), pairs)  22.4 us
  transfers between devices with their start and end apart: 37, of which 15 were waited for; matrix products, arithmetic and copies ran while one was open for 22% of the time, Pallas kernels for 16%

profile of v2, /device:TPU:0, one launch (start us, length us, event | category | flops | bytes accessed | tf_op | source)
XLA Modules:
  0.0 654.8 jit_solution(7867479870351183856)
XLA Ops:
  14.3 4.4 copy.95
  19.0 6.4 collective-permute-done
  27.7 22.1 %collective-permute-done.1 = bf16[2,288,1664]{2,1,0:T(8,128)(2,1)S(1)} collective-permute-done((bf16[2,288,1664]{2,1,0:T(8,128)(2,1)S(1)}, bf16[2,288,1664]{2,1,0:T(8,128)(2,1)S(1)}, u32[]{:S(2)}, u32[]{:S(2)}) %collective-permute-start.1) | collective-permute-done | bytes 1916960 | tf_op jit(solution)/shard_map/ppermute | solution.py:118
  54.0 15.8 %collective-permute-done.2 = bf16[288,2304]{1,0:T(8,128)(2,1)S(1)} collective-permute-done((bf16[288,2304]{1,0:T(8,128)(2,1)S(1)}, bf16[288,2304]{1,0:T(8,128)(2,1)S(1)}, u32[]{:S(2)}, u32[]{:S(2)}) %collective-permute-start.2) | collective-permute-done | bytes 1327136 | tf_op jit(solution)/shard_map/ppermute | solution.py:118
  77.8 10.8 %project.1 = (bf16[512,512]{1,0:T(8,128)(2,1)}, bf16[2,512,256]{2,1,0:T(8,128)(2,1)}, bf16[512,2304]{1,0:T(8,128)(2,1)}, f32[8,2304]{1,0:T(8,128)}) custom-call(s32[2]{0:T(128)} %pad_add_fusion.place, bf16[512,2304]{1,0:T(8,128)(2,1)} %bitcast.197, bf16[4,288,1664]{2,1,0:T(8,128)(2,1)} %copy-done, bf16[4,288,1664]{2,1,0:T(8,128)(2,1)} %copy-done.2, ...), custom_call_target="tpu_custom_call" | custom-call | flops 2415919104 | bytes 12000000 | tf_op jit(solution)/shard_map/project/pallas_call | solution.py:317
  91.7 14.1 %collective-permute-done.5.rest_0_ = bf16[2,288,2304]{2,1,0:T(8,128)(2,1)} collective-permute-done((bf16[2,288,2304]{2,1,0:T(8,128)(2,1)}, bf16[2,288,2304]{2,1,0:T(8,128)(2,1)}, u32[]{:S(2)}, u32[]{:S(2)}) %collective-permute-start.5) | collective-permute-done | bytes 2654240 | tf_op jit(solution)/shard_map/ppermute | solution.py:118
  105.7 7.7 %attend.1 = (bf16[512,512]{1,0:T(8,128)(2,1)}, bf16[512,2304]{1,0:T(8,128)(2,1)}) custom-call(s32[2]{0:T(128)} %pad_add_fusion.place, bf16[512,512]{1,0:T(8,128)(2,1)} %get-tuple-element.71.queries, bf16[2,512,256]{2,1,0:T(8,128)(2,1)} %get-tuple-element.72.pair, bf16[2,512,256]{2,1,0:T(8,128)(2,1)} %copy-done.40, bf16[4,288,1664]{2,1,0:T(8,128)(2,1)} %copy-done, ...), custom_call_target="tpu_custom_call" | custom-call | flops 4831838208 | bytes 8000000 | tf_op jit(solution)/shard_map/attend/pallas_call | solution.py:380
  117.1 8.9 %collective-permute-done.6.far = bf16[4,288,2304]{2,1,0:T(8,128)(2,1)} collective-permute-done((bf16[4,288,2304]{2,1,0:T(8,128)(2,1)S(1)}, bf16[4,288,2304]{2,1,0:T(8,128)(2,1)}, u32[]{:S(2)}, u32[]{:S(2)}) %collective-permute-start.6) | collective-permute-done | bytes 5308448 | tf_op jit(solution)/shard_map/ppermute | solution.py:106
  126.0 10.2 %arrange.1.down = bf16[2304,2304]{1,0:T(8,128)(2,1)} custom-call(s32[2]{0:T(128)} %pad_add_fusion.place, bf16[4,288,2304]{2,1,0:T(8,128)(2,1)} %copy-done.5, bf16[4,288,2304]{2,1,0:T(8,128)(2,1)} %collective-permute-done.6.far), custom_call_target="tpu_custom_call" | custom-call | bytes 42467328 | tf_op jit(solution)/shard_map/arrange/pallas_call | solution.py:272
  136.2 74.8 %all-reduce.6.cloned.1.call-done.attn_out = bf16[512,2304]{1,0:T(8,128)(2,1)} async-done(((bf16[512,2304]{1,0:T(8,128)(2,1)}), bf16[512,2304]{1,0:T(8,128)(2,1)}) %all-reduce.6.cloned.1.call-update) | async-done | bytes 2359312 | tf_op jit(solution)/shard_map/psum | solution.py:101
  211.0 15.7 %all-gather.2.cloned.1.call-done.gate_up = bf16[2,2304,2304]{2,1,0:T(8,128)(2,1)} async-done(((bf16[2,288,2304]{2,1,0:T(8,128)(2,1)}), bf16[2,2304,2304]{2,1,0:T(8,128)(2,1)}) %all-gather.2.cloned.1.call-update) | async-done | bytes 21233680 | tf_op jit(solution)/shard_map/all_gather | solution.py:965
  226.7 24.3 %ffn_forward.1 = (bf16[512,2304]{1,0:T(8,128)(2,1)}, bf16[512,2304]{1,0:T(8,128)(2,1)}, bf16[512,2304]{1,0:T(8,128)(2,1)}, bf16[512,2304]{1,0:T(8,128)(2,1)}, bf16[512,2304]{1,0:T(8,128)(2,1)}) custom-call(bf16[512,2304]{1,0:T(8,128)(2,1)} %all-reduce.6.cloned.1.call-done.attn_out, bf16[512,2304]{1,0:T(8,128)(2,1)} %bitcast.198, ...), custom_call_target="tpu_custom_call" | custom-call | flops 16307453952 | bytes 50000000 | tf_op jit(solution)/shard_map/ffn_forward/pallas_call | solution.py:487
  254.2 4.3 copy.73
  258.8 3.5 constant_dynamic-slice_fusion.6
  302.1 52.2 %all-reduce.8.cloned.1.call-done.ffn_out = bf16[512,2304]{1,0:T(8,128)(2,1)} async-done(((bf16[512,2304]{1,0:T(8,128)(2,1)}), bf16[512,2304]{1,0:T(8,128)(2,1)}) %all-reduce.8.cloned.1.call-update) | async-done | bytes 2359312 | tf_op jit(solution)/shard_map/psum | solution.py:101
  354.3 26.2 %ffn_back.1 = (bf16[512,2304]{1,0:T(8,128)(2,1)}, bf16[512,2304]{1,0:T(8,128)(2,1)}, bf16[512,2304]{1,0:T(8,128)(2,1)}, f32[8,2304]{1,0:T(8,128)}, bf16[512,2304]{1,0:T(8,128)(2,1)}) custom-call(bf16[512,2304]{1,0:T(8,128)(2,1)} %all-reduce.8.cloned.1.call-done.ffn_out, bf16[512,2304]{1,0:T(8,128)(2,1)} %bitcast.231, f32[8,2304]{1,0:T(8,128)} %get-tuple-element.75.gains, ...), custom_call_target="tpu_custom_call" | custom-call | flops 16307453952 | bytes 55000000 | tf_op jit(solution)/shard_map/ffn_back/pallas_call | solution.py:610
  390.2 14.5 %convolution_convert_fusion.2 = bf16[1152,2304]{1,0:T(8,128)(2,1)S(1)} fusion(bf16[1024,2304]{1,0:T(8,128)(2,1)} %constant_dynamic-update-slice_fusion.2.rest_3_, bf16[512,1152]{0,1:T(8,128)(2,1)} %collective-permute-done.11, bf16[512,288]{0,1:T(8,128)(2,1)S(1)} %copy-done.31, bf16[512,288]{0,1:T(8,128)(2,1)S(1)} %copy-done.32, ...), kind=kOutput, calls=%fused_computation.2 | convolution fusion | flops 5450268672 | bytes 12386304 | tf_op jit(solution)/shard_map/dot_general | solution.py:82
  407.9 8.6 %convolution_convert_fusion.1 = bf16[1152,2304]{1,0:T(8,128)(2,1)S(1)} fusion(bf16[512,2304]{1,0:T(8,128)(2,1)} %collective-permute-done.13, bf16[512,2304]{1,0:T(8,128)(2,1)} %get-tuple-element.85, bf16[512,1152]{1,0:T(8,128)(2,1)} %collective-permute-done.9, bf16[512,1152]{1,0:T(8,128)(2,1)S(1)} %copy-done.12), kind=kOutput, calls=%fused_computation.1 | convolution fusion | flops 5452627968 | bytes 12386304 | tf_op jit(solution)/shard_map/dot_general | solution.py:82
  419.4 8.8 %convolution_convert_fusion = bf16[1152,2304]{1,0:T(8,128)(2,1)S(1)} fusion(bf16[512,2304]{1,0:T(8,128)(2,1)} %collective-permute-done.17, bf16[512,2304]{1,0:T(8,128)(2,1)} %get-tuple-element.90, bf16[512,1152]{1,0:T(8,128)(2,1)} %collective-permute-done.9, bf16[512,1152]{1,0:T(8,128)(2,1)S(1)} %copy-done.12), kind=kOutput, calls=%fused_computation | convolution fusion | flops 5452627968 | bytes 12386304 | tf_op jit(solution)/shard_map/dot_general | solution.py:82
  441.5 39.7 %collective-permute-done.14 = bf16[2,288,2304]{2,1,0:T(8,128)(2,1)} collective-permute-done((bf16[2,288,2304]{2,1,0:T(8,128)(2,1)S(1)}, bf16[2,288,2304]{2,1,0:T(8,128)(2,1)}, u32[]{:S(2)}, u32[]{:S(2)}) %collective-permute-start.14) | collective-permute-done | bytes 2654240 | tf_op jit(solution)/shard_map/ppermute | solution.py:118
  483.7 11.6 %mid_back.1 = (f32[512,2304]{1,0:T(8,128)}, bf16[512,2304]{1,0:T(8,128)(2,1)}, bf16[512,512]{1,0:T(8,128)(2,1)}, f32[2,8,2304]{2,1,0:T(8,128)}) custom-call(s32[2]{0:T(128)} %pad_add_fusion.place, bf16[512,2304]{1,0:T(8,128)(2,1)} %all-reduce.10.cloned.1.call-done.grad_in, bf16[512,2304]{1,0:T(8,128)(2,1)} %bitcast.199, ...), custom_call_target="tpu_custom_call" | custom-call | flops 1207959552 | bytes 24000000 | tf_op jit(solution)/shard_map/mid_back/pallas_call | solution.py:681
  495.3 9.6 %attend_back.1 = (bf16[512,512]{1,0:T(8,128)(2,1)}, f32[2,512,256]{2,1,0:T(8,128)}, bf16[2,512,256]{2,1,0:T(8,128)(2,1)}) custom-call(s32[2]{0:T(128)} %pad_add_fusion.place, bf16[512,512]{1,0:T(8,128)(2,1)} %get-tuple-element.71.queries, bf16[2,512,256]{2,1,0:T(8,128)(2,1)} %get-tuple-element.72.pair, bf16[2,512,256]{2,1,0:T(8,128)(2,1)} %copy-done.40, ...), custom_call_target="tpu_custom_call" | custom-call | flops 5368709120 | bytes 5000000 | tf_op jit(solution)/shard_map/attend_back/pallas_call | solution.py:754
  521.4 10.6 %project_back.1 = (bf16[512,1024]{1,0:T(8,128)(2,1)}, bf16[512,2304]{1,0:T(8,128)(2,1)}, f32[8,2304]{1,0:T(8,128)}) custom-call(s32[2]{0:T(128)} %pad_add_fusion.place, bf16[512,512]{1,0:T(8,128)(2,1)} %get-tuple-element.87.grad_q, f32[2,512,256]{2,1,0:T(8,128)} %get-tuple-element.88.grad_own, bf16[2,512,256]{2,1,0:T(8,128)(2,1)} %collective-permute-done.15.grad_ahead, ...), custom_call_target="tpu_custom_call" | custom-call | flops 2415919104 | bytes 14000000 | tf_op jit(solution)/shard_map/project_back/pallas_call | solution.py:806
  544.9 4.5 convolution_convert_fusion.3
  558.0 12.4 %adam.7 = (f32[288,2304]{1,0:T(8,128)}, f32[288,2304]{1,0:T(8,128)}, f32[288,2304]{1,0:T(8,128)}, f32[288,2304]{1,0:T(8,128)}) custom-call(bf16[288,2304]{1,0:T(8,128)(2,1)} %get-tuple-element.162.refs_0_, bf16[288,2304]{1,0:T(8,128)(2,1)} %slice_bitcast_fusion.refs_1_, bf16[288,2304]{1,0:T(8,128)(2,1)} %collective-permute-done.16.rest_0_.refs_2_, ...), custom_call_target="tpu_custom_call" | custom-call | bytes 200000000 | tf_op jit(solution)/shard_map/adam/pallas_call | solution.py:913
  574.3 4.8 collective-permute-done.23
  582.5 9.5 %join.1 = f32[288,2,2304]{2,1,0:T(2,128)} custom-call(bf16[288,2304]{1,0:T(8,128)(2,1)} %get-tuple-element.168.refs_0_, bf16[288,2304]{1,0:T(8,128)(2,1)} %slice_bitcast_fusion.6.rest_1_.refs_1_, bf16[288,2304]{1,0:T(8,128)(2,1)} %copy-done.16, bf16[288,2304]{1,0:T(8,128)(2,1)} %get-tuple-element.165.refs_3_, ...), custom_call_target="tpu_custom_call" | custom-call | bytes 200000000 | tf_op jit(solution)/shard_map/join/pallas_call | solution.py:885
  591.9 16.8 %adam.6 = (f32[10368,128]{1,0:T(8,128)}, f32[10368,128]{1,0:T(8,128)}, f32[10368,128]{1,0:T(8,128)}) custom-call(f32[10368,128]{1,0:T(8,128)} %bitcast.204, f32[10368,128]{1,0:T(8,128)} %bitcast.205, f32[10368,128]{1,0:T(8,128)} %bitcast.218, f32[10368,128]{1,0:T(8,128)} %bitcast.219), custom_call_target="tpu_custom_call" | custom-call | bytes 200000000 | tf_op jit(solution)/shard_map/adam/pallas_call | solution.py:913
  610.2 6.4 adam.5
  620.5 7.3 %adam.4 = (f32[2304,128]{1,0:T(8,128)}, f32[2304,128]{1,0:T(8,128)}, f32[2304,128]{1,0:T(8,128)}) custom-call(f32[2304,128]{1,0:T(8,128)} %reshape_broadcast_in_dim.3.refs_0_, f32[2304,128]{1,0:T(8,128)} %bitcast.224, f32[2304,128]{1,0:T(8,128)} %bitcast.251, f32[2304,128]{1,0:T(8,128)} %bitcast.252), custom_call_target="tpu_custom_call" | custom-call | bytes 200000000 | tf_op jit(solution)/shard_map/adam/pallas_call | solution.py:913
  627.7 12.2 %all-reduce.12.cloned.1.call-done.grad_in = bf16[512,2304]{1,0:T(8,128)(2,1)} async-done(((bf16[512,2304]{1,0:T(8,128)(2,1)}), bf16[512,2304]{1,0:T(8,128)(2,1)}) %all-reduce.12.cloned.1.call-update) | async-done | bytes 2359312 | tf_op jit(solution)/shard_map/psum | solution.py:101
  640.0 7.5 %stream_back.1 = f32[512,2304]{1,0:T(8,128)} custom-call(bf16[512,2304]{1,0:T(8,128)(2,1)} %all-reduce.12.cloned.1.call-done.grad_in, bf16[512,2304]{1,0:T(8,128)(2,1)} %bitcast.201, f32[8,2304]{1,0:T(8,128)} %get-tuple-element.75.gains, f32[512,2304]{1,0:T(8,128)} %get-tuple-element.92.grad_mid, f32[288,1,1024]{2,1,0:T(1,128)} %bitcast.249, ...), custom_call_target="tpu_custom_call" | custom-call | flops 23592960 | bytes 14000000 | tf_op jit(solution)/shard_map/stream_back/pallas_call | solution.py:842
  (238 shorter events, 152.2 us)
Async XLA Ops:
  8.0 202.9 %all-reduce.6.cloned.1.call-start = ((), (), s32[]{:S(2)}) async-start(), calls=%async_computation | async-start | bytes 4718592 | tf_op jit(solution)/shard_map/psum | solution.py:101
  10.6 14.8 %collective-permute-start = (bf16[288,1664]{1,0:T(8,128)(2,1)S(1)}, bf16[288,1664]{1,0:T(8,128)(2,1)S(1)}, u32[]{:S(2)}, u32[]{:S(2)}) collective-permute-start(bf16[288,1664]{1,0:T(8,128)(2,1)S(1)} %pad_maximum_fusion.12), channel_id=1, source_target_pairs={{0,8},{4,20},{8,0},{12,28},{16,24},{20,4},{24,16},{28,12},{1,9},{5... | collective-permute-start | bytes 2875400 | tf_op jit(solution)/shard_map/ppermute | solution.py:118
  25.5 24.2 %collective-permute-start.1 = (bf16[2,288,1664]{2,1,0:T(8,128)(2,1)S(1)}, bf16[2,288,1664]{2,1,0:T(8,128)(2,1)S(1)}, u32[]{:S(2)}, u32[]{:S(2)}) collective-permute-start(bf16[2,288,1664]{2,1,0:T(8,128)(2,1)S(1)} %pad_maximum_fusion.8), channel_id=1, source_target_pairs={{0,16},{4,12},{8,24},{12,4},{16,0},{20,28},{24,8},{28,20},{1,17},{... | collective-permute-start | bytes 5750792 | tf_op jit(solution)/shard_map/ppermute | solution.py:118
  52.0 17.8 %collective-permute-start.3 = (bf16[4,288,1664]{2,1,0:T(8,128)(2,1)S(1)}, bf16[4,288,1664]{2,1,0:T(8,128)(2,1)S(1)}, u32[]{:S(2)}, u32[]{:S(2)}) collective-permute-start(bf16[4,288,1664]{2,1,0:T(8,128)(2,1)S(1)} %pad_maximum_fusion.1.near), channel_id=1, source_target_pairs={{0,4},{4,0},{1,5},{5,1},{2,6},{6,2},{3,7},{7,3},{8,12},{12,8},{9,1... | collective-permute-start | bytes 11501576 | tf_op jit(solution)/shard_map/ppermute | solution.py:106
  52.0 17.8 %collective-permute-start.2 = (bf16[288,2304]{1,0:T(8,128)(2,1)S(1)}, bf16[288,2304]{1,0:T(8,128)(2,1)S(1)}, u32[]{:S(2)}, u32[]{:S(2)}) collective-permute-start(bf16[288,2304]{1,0:T(8,128)(2,1)S(1)} %bitcast_convert_fusion), channel_id=1, source_target_pairs={{0,8},{4,20},{8,0},{12,28},{16,24},{20,4},{24,16},{28,12},{1,9},{5... | collective-permute-start | bytes 3981320 | tf_op jit(solution)/shard_map/ppermute | solution.py:118
  73.4 32.3 %collective-permute-start.5 = (bf16[2,288,2304]{2,1,0:T(8,128)(2,1)}, bf16[2,288,2304]{2,1,0:T(8,128)(2,1)}, u32[]{:S(2)}, u32[]{:S(2)}) collective-permute-start(bf16[2,288,2304]{2,1,0:T(8,128)(2,1)} %pad_maximum_fusion.2), channel_id=1, source_target_pairs={{0,16},{4,12},{8,24},{12,4},{16,0},{20,28},{24,8},{28,20},{1,17},{... | collective-permute-start | bytes 7962632 | tf_op jit(solution)/shard_map/ppermute | solution.py:118
  113.4 113.3 %all-gather.2.cloned.1.call-start = ((), (), s32[]{:S(2)}) async-start(), calls=%async_computation.1 | async-start | bytes 23887872 | tf_op jit(solution)/shard_map/all_gather | solution.py:965
  114.0 240.3 %all-reduce.8.cloned.1.call-start = ((), (), s32[]{:S(2)}) async-start(), calls=%async_computation.2 | async-start | bytes 4718592 | tf_op jit(solution)/shard_map/psum | solution.py:101
  117.0 8.9 %collective-permute-start.6 = (bf16[4,288,2304]{2,1,0:T(8,128)(2,1)S(1)}, bf16[4,288,2304]{2,1,0:T(8,128)(2,1)}, u32[]{:S(2)}, u32[]{:S(2)}) collective-permute-start(bf16[4,288,2304]{2,1,0:T(8,128)(2,1)S(1)} %pad_maximum_fusion.near), channel_id=1, source_target_pairs={{0,4},{4,0},{1,5},{5,1},{2,6},{6,2},{3,7},{7,3},{8,12},{12,8},{9,1... | collective-permute-start | bytes 15925256 | tf_op jit(solution)/shard_map/ppermute | solution.py:106
  251.0 47.9 %collective-permute-start.10 = (bf16[512,2304]{1,0:T(8,128)(2,1)}, bf16[512,2304]{1,0:T(8,128)(2,1)}, u32[]{:S(2)}, u32[]{:S(2)}) collective-permute-start(bf16[512,2304]{1,0:T(8,128)(2,1)} %get-tuple-element.82), channel_id=1, source_target_pairs={{0,4},{4,0},{1,5},{5,1},{2,6},{6,2},{3,7},{7,3},{8,12},{12,8},{9,1... | collective-permute-start | bytes 7077896 | tf_op jit(solution)/shard_map/ppermute | solution.py:106
  258.5 225.2 %all-reduce.10.cloned.1.call-start = ((), (), s32[]{:S(2)}) async-start(), calls=%async_computation.3 | async-start | bytes 4718592 | tf_op jit(solution)/shard_map/psum | solution.py:101
  269.9 23.2 %collective-permute-start.9 = (bf16[512,1152]{1,0:T(8,128)(2,1)}, bf16[512,1152]{1,0:T(8,128)(2,1)}, u32[]{:S(2)}, u32[]{:S(2)}) collective-permute-start(bf16[512,1152]{1,0:T(8,128)(2,1)} %concatenate.95), channel_id=1, source_target_pairs={{0,4},{4,0},{1,5},{5,1},{2,6},{6,2},{3,7},{7,3},{8,12},{12,8},{9,1... | collective-permute-start | bytes 3538952 | tf_op jit(solution)/shard_map/ppermute | solution.py:106
  270.2 7.2 %collective-permute-start.7 = (bf16[512,512]{1,0:T(8,128)(2,1)}, bf16[512,512]{1,0:T(8,128)(2,1)}, u32[]{:S(2)}, u32[]{:S(2)}) collective-permute-start(bf16[512,512]{1,0:T(8,128)(2,1)} %get-tuple-element.77.attended), channel_id=1, source_target_pairs={{0,4},{4,0},{1,5},{5,1},{2,6},{6,2},{3,7},{7,3},{8,12},{12,8},{9,1... | collective-permute-start | bytes 1572872 | tf_op jit(solution)/shard_map/ppermute | solution.py:106
  276.1 20.0 %collective-permute-start.8 = (bf16[512,1152]{1,0:T(8,128)(2,1)}, bf16[512,1152]{1,0:T(8,128)(2,1)}, u32[]{:S(2)}, u32[]{:S(2)}) collective-permute-start(bf16[512,1152]{1,0:T(8,128)(2,1)} %concatenate.92), channel_id=1, source_target_pairs={{0,4},{4,0},{1,5},{5,1},{2,6},{6,2},{3,7},{7,3},{8,12},{12,8},{9,1... | collective-permute-start | bytes 3538952 | tf_op jit(solution)/shard_map/ppermute | solution.py:106
  387.8 20.1 %collective-permute-start.13 = (bf16[512,2304]{1,0:T(8,128)(2,1)}, bf16[512,2304]{1,0:T(8,128)(2,1)}, u32[]{:S(2)}, u32[]{:S(2)}) collective-permute-start(bf16[512,2304]{1,0:T(8,128)(2,1)} %get-tuple-element.85), channel_id=1, source_target_pairs={{0,4},{4,0},{1,5},{5,1},{2,6},{6,2},{3,7},{7,3},{8,12},{12,8},{9,1... | collective-permute-start | bytes 7077896 | tf_op jit(solution)/shard_map/ppermute | solution.py:106
  388.4 251.6 %all-reduce.12.cloned.1.call-start = ((), (), s32[]{:S(2)}) async-start(), calls=%async_computation.4 | async-start | bytes 4718592 | tf_op jit(solution)/shard_map/psum | solution.py:101
  388.9 30.5 %collective-permute-start.17 = (bf16[512,2304]{1,0:T(8,128)(2,1)}, bf16[512,2304]{1,0:T(8,128)(2,1)}, u32[]{:S(2)}, u32[]{:S(2)}) collective-permute-start(bf16[512,2304]{1,0:T(8,128)(2,1)} %get-tuple-element.90), channel_id=1, source_target_pairs={{0,4},{4,0},{1,5},{5,1},{2,6},{6,2},{3,7},{7,3},{8,12},{12,8},{9,1... | collective-permute-start | bytes 7077896 | tf_op jit(solution)/shard_map/ppermute | solution.py:106
  406.4 32.1 %collective-permute-start.12 = (bf16[2,288,2304]{2,1,0:T(8,128)(2,1)S(1)}, bf16[2,288,2304]{2,1,0:T(8,128)(2,1)S(1)}, u32[]{:S(2)}, u32[]{:S(2)}) collective-permute-start(bf16[2,288,2304]{2,1,0:T(8,128)(2,1)S(1)} %pad_maximum_fusion.3), channel_id=1, source_target_pairs={{0,8},{4,20},{8,0},{12,28},{16,24},{20,4},{24,16},{28,12},{1,9},{5... | collective-permute-start | bytes 7962632 | tf_op jit(solution)/shard_map/ppermute | solution.py:118
  418.3 62.8 %collective-permute-start.14 = (bf16[2,288,2304]{2,1,0:T(8,128)(2,1)S(1)}, bf16[2,288,2304]{2,1,0:T(8,128)(2,1)}, u32[]{:S(2)}, u32[]{:S(2)}) collective-permute-start(bf16[2,288,2304]{2,1,0:T(8,128)(2,1)S(1)} %pad_maximum_fusion.4), channel_id=1, source_target_pairs={{0,8},{4,20},{8,0},{12,28},{16,24},{20,4},{24,16},{28,12},{1,9},{5... | collective-permute-start | bytes 7962632 | tf_op jit(solution)/shard_map/ppermute | solution.py:118
  432.7 76.9 %collective-permute-start.18 = (bf16[2,288,2304]{2,1,0:T(8,128)(2,1)}, bf16[2,288,2304]{2,1,0:T(8,128)(2,1)}, u32[]{:S(2)}, u32[]{:S(2)}) collective-permute-start(bf16[2,288,2304]{2,1,0:T(8,128)(2,1)} %pad_maximum_fusion.5), channel_id=1, source_target_pairs={{0,8},{4,20},{8,0},{12,28},{16,24},{20,4},{24,16},{28,12},{1,9},{5... | collective-permute-start | bytes 7962632 | tf_op jit(solution)/shard_map/ppermute | solution.py:118
  440.0 81.4 %collective-permute-start.16 = (bf16[288,2304]{1,0:T(8,128)(2,1)}, bf16[288,2304]{1,0:T(8,128)(2,1)}, u32[]{:S(2)}, u32[]{:S(2)}) collective-permute-start(bf16[288,2304]{1,0:T(8,128)(2,1)} %fusion.16.rest_0_), channel_id=1, source_target_pairs={{0,16},{4,12},{8,24},{12,4},{16,0},{20,28},{24,8},{28,20},{1,17},{... | collective-permute-start | bytes 3981320 | tf_op jit(solution)/shard_map/ppermute | solution.py:118
  504.9 16.4 %collective-permute-start.15 = (bf16[2,512,256]{2,1,0:T(8,128)(2,1)}, bf16[2,512,256]{2,1,0:T(8,128)(2,1)}, u32[]{:S(2)}, u32[]{:S(2)}) collective-permute-start(bf16[2,512,256]{2,1,0:T(8,128)(2,1)} %get-tuple-element.89), channel_id=1, source_target_pairs={{4,0},{5,1},{6,2},{7,3},{12,8},{13,9},{14,10},{15,11},{20,16},{21,... | collective-permute-start | bytes 1572872 | tf_op jit(solution)/shard_map/ppermute | solution.py:29
  512.7 68.7 %collective-permute-start.26 = (bf16[288,2304]{1,0:T(8,128)(2,1)}, bf16[288,2304]{1,0:T(8,128)(2,1)}, u32[]{:S(2)}, u32[]{:S(2)}) collective-permute-start(bf16[288,2304]{1,0:T(8,128)(2,1)} %fusion.14), channel_id=1, source_target_pairs={{0,16},{4,12},{8,24},{12,4},{16,0},{20,28},{24,8},{28,20},{1,17},{... | collective-permute-start | bytes 3981320 | tf_op jit(solution)/shard_map/ppermute | solution.py:118
  534.9 10.0 %collective-permute-start.19 = (bf16[512,1024]{1,0:T(8,128)(2,1)}, bf16[512,1024]{1,0:T(8,128)(2,1)}, u32[]{:S(2)}, u32[]{:S(2)}) collective-permute-start(bf16[512,1024]{1,0:T(8,128)(2,1)} %get-tuple-element.93), channel_id=1, source_target_pairs={{0,4},{4,0},{1,5},{5,1},{2,6},{6,2},{3,7},{7,3},{8,12},{12,8},{9,1... | collective-permute-start | bytes 3145736 | tf_op jit(solution)/shard_map/ppermute | solution.py:106
  538.1 13.2 %collective-permute-start.22 = (bf16[512,1152]{0,1:T(8,128)(2,1)}, bf16[512,1152]{0,1:T(8,128)(2,1)}, u32[]{:S(2)}, u32[]{:S(2)}) collective-permute-start(bf16[512,1152]{0,1:T(8,128)(2,1)} %pad_maximum_fusion.11), channel_id=1, source_target_pairs={{0,4},{4,0},{1,5},{5,1},{2,6},{6,2},{3,7},{7,3},{8,12},{12,8},{9,1... | collective-permute-start | bytes 3538952 | tf_op jit(solution)/shard_map/ppermute | solution.py:106
  543.2 38.2 %collective-permute-start.25 = (bf16[288,2304]{1,0:T(8,128)(2,1)}, bf16[288,2304]{1,0:T(8,128)(2,1)S(1)}, u32[]{:S(2)}, u32[]{:S(2)}) collective-permute-start(bf16[288,2304]{1,0:T(8,128)(2,1)} %fusion.15), channel_id=1, source_target_pairs={{0,16},{4,12},{8,24},{12,4},{16,0},{20,28},{24,8},{28,20},{1,17},{... | collective-permute-start | bytes 3981320 | tf_op jit(solution)/shard_map/ppermute | solution.py:118
  544.7 25.7 %collective-permute-start.30 = (f32[4,2304]{1,0:T(4,128)S(1)}, f32[4,2304]{1,0:T(4,128)}, u32[]{:S(2)}, u32[]{:S(2)}) collective-permute-start(f32[4,2304]{1,0:T(4,128)S(1)} %add.247), channel_id=1, source_target_pairs={{0,1},{1,0},{2,3},{3,2},{4,5},{5,4},{6,7},{7,6},{8,9},{9,8},{10,11... | collective-permute-start | bytes 110600 | tf_op jit(solution)/shard_map/ppermute | solution.py:106
  549.7 23.4 %collective-permute-start.20 = (bf16[2,288,1024]{2,1,0:T(8,128)(2,1)S(1)}, bf16[2,288,1024]{2,1,0:T(8,128)(2,1)S(1)}, u32[]{:S(2)}, u32[]{:S(2)}) collective-permute-start(bf16[2,288,1024]{2,1,0:T(8,128)(2,1)S(1)} %pad_maximum_fusion.10), channel_id=1, source_target_pairs={{0,8},{4,20},{8,0},{12,28},{16,24},{20,4},{24,16},{28,12},{1,9},{5... | collective-permute-start | bytes 3538952 | tf_op jit(solution)/shard_map/ppermute | solution.py:118
  555.6 23.5 %collective-permute-start.23 = (bf16[2,288,512]{2,1,0:T(8,128)(2,1)}, bf16[2,288,512]{2,1,0:T(8,128)(2,1)S(1)}, u32[]{:S(2)}, u32[]{:S(2)}) collective-permute-start(bf16[2,288,512]{2,1,0:T(8,128)(2,1)} %pad_maximum_fusion.13), channel_id=1, source_target_pairs={{0,8},{4,20},{8,0},{12,28},{16,24},{20,4},{24,16},{28,12},{1,9},{5... | collective-permute-start | bytes 1769480 | tf_op jit(solution)/shard_map/ppermute | solution.py:118
  571.2 9.4 %collective-permute-start.31 = (f32[4,2304]{1,0:T(4,128)S(1)}, f32[4,2304]{1,0:T(4,128)S(1)}, u32[]{:S(2)}, u32[]{:S(2)}) collective-permute-start(f32[4,2304]{1,0:T(4,128)S(1)} %add.248), channel_id=1, source_target_pairs={{0,2},{1,3},{2,0},{3,1},{4,6},{5,7},{6,4},{7,5},{8,10},{9,11},{10,... | collective-permute-start | bytes 110600 | tf_op jit(solution)/shard_map/ppermute | solution.py:106
  573.4 43.2 %collective-permute-start.21 = (bf16[288,1024]{1,0:T(8,128)(2,1)S(1)}, bf16[288,1024]{1,0:T(8,128)(2,1)S(1)}, u32[]{:S(2)}, u32[]{:S(2)}) collective-permute-start(bf16[288,1024]{1,0:T(8,128)(2,1)S(1)} %fusion.39), channel_id=1, source_target_pairs={{0,16},{4,12},{8,24},{12,4},{16,0},{20,28},{24,8},{28,20},{1,17},{... | collective-permute-start | bytes 1769480 | tf_op jit(solution)/shard_map/ppermute | solution.py:118
  579.1 30.4 %collective-permute-start.24 = (bf16[288,512]{1,0:T(8,128)(2,1)S(1)}, bf16[288,512]{1,0:T(8,128)(2,1)S(1)}, u32[]{:S(2)}, u32[]{:S(2)}) collective-permute-start(bf16[288,512]{1,0:T(8,128)(2,1)S(1)} %fusion.41), channel_id=1, source_target_pairs={{0,16},{4,12},{8,24},{12,4},{16,0},{20,28},{24,8},{28,20},{1,17},{... | collective-permute-start | bytes 884744 | tf_op jit(solution)/shard_map/ppermute | solution.py:118
  (46 other events, 228.2 us)
Sparse Core Ops, SparseCore 0:
  113.6 97.3 all-reduce.5
  258.6 95.6 all-reduce.7
  388.5 94.6 all-reduce.9
  544.8 95.1 all-reduce.11
Sparse Core Ops, SparseCore 1:
  116.4 110.3 all-gather.1

commit v3 on v2

--- a/solution.py
+++ b/solution.py
@@ -120,10 +120,6 @@
 
 def offsets(owner):
     return (0, 1 + owner, 2 - owner, 3)
-
-
-def gather_end(shard, first, second):
-    return jnp.concatenate([shard[None], first[None], second], axis=0)
 
 
 def own_blocks(wide):
@@ -235,18 +231,18 @@
 
 def fetch_rows(place, near, far, target, sems, column, columns):
     chip, core = place[0], place[1]
-    rows = near.shape[1]
+    rows = near[0].shape[1]
     copies = []
-    for k in range(4):
-        for which, source in enumerate((near, far)):
-            owner = which ^ core
-            offset = (0, 1 + owner, 2 - owner, 3)[k]
+    for which, (one, two) in enumerate((near, far)):
+        owner = which ^ core
+        blocks = ((one.at[0], 0), (one.at[1], 1 + owner), (two.at[0], 2 - owner), (two.at[1], 3))
+        for block, offset in blocks:
             row = ((offset ^ chip) * 2 + owner) * rows
             copies.append(
                 pltpu.make_async_copy(
-                    source.at[k, :, pl.ds(column, columns)],
+                    block.at[:, pl.ds(column, columns)],
                     target.at[pl.ds(pl.multiple_of(row, 16), rows), :],
-                    sems.at[k * 2 + which],
+                    sems.at[len(copies)],
                 )
             )
     return copies
@@ -260,8 +256,8 @@
     )
 
 
-def arrange_kernel(place, near, far, result, sems):
-    copies = fetch_rows(place, near, far, result, sems, 0, result.shape[1])
+def arrange_kernel(place, one, two, one_far, two_far, result, sems):
+    copies = fetch_rows(place, (one, two), (one_far, two_far), result, sems, 0, result.shape[1])
     for copy in copies:
         copy.start()
     for copy in copies:
@@ -271,19 +267,19 @@
 def arrange(place, near, far):
     return pl.pallas_call(
         arrange_kernel,
-        in_specs=[spec_smem(), spec_any(), spec_any()],
+        in_specs=[spec_smem()] + [spec_any()] * 4,
         out_specs=spec_vmem(),
-        out_shape=shaped((8 * near.shape[1], near.shape[2]), jnp.bfloat16),
+        out_shape=shaped((8 * near[0].shape[1], near[0].shape[2]), jnp.bfloat16),
         scratch_shapes=[pltpu.SemaphoreType.DMA((8,))],
         compiler_params=kernel_params(),
-        cost_estimate=cost(0, 4 * near.size * 4),
+        cost_estimate=cost(0, 16 * near[0].size),
         name="arrange",
-    )(place, near, far)
-
-
-def project_kernel(place, x, near, far, cosine, sine, *rest):
+    )(place, *near, *far)
+
+
+def project_kernel(place, x, one, two, one_far, two_far, cosine, sine, *rest):
     queries, pair, attn_in, gains, weight, sems = rest[-6:]
-    copies = fetch_rows(place, near, far, weight, sems, 0, weight.shape[1])
+    copies = fetch_rows(place, (one, two), (one_far, two_far), weight, sems, 0, weight.shape[1])
     for copy in copies:
         copy.start()
     for copy in copies:
@@ -316,7 +312,9 @@
     bf16 = jnp.bfloat16
     return pl.pallas_call(
         project_kernel,
-        in_specs=[spec_smem(), spec_vmem(), spec_any(), spec_any(), spec_vmem(), spec_vmem()]
+        in_specs=[spec_smem(), spec_vmem()]
+        + [spec_any()] * 4
+        + [spec_vmem()] * 2
         + [spec_any()] * len(earlier),
         out_specs=[spec_vmem()] * 4,
         out_shape=[
@@ -325,11 +323,11 @@
             shaped((tokens, width), bf16),
             shaped((8, width), jnp.float32),
         ],
-        scratch_shapes=[pltpu.VMEM((width, near.shape[2]), bf16), pltpu.SemaphoreType.DMA((8,))],
+        scratch_shapes=[pltpu.VMEM((width, near[0].shape[2]), bf16), pltpu.SemaphoreType.DMA((8,))],
         compiler_params=kernel_params(),
         cost_estimate=cost(2 * tokens * width * 1024, 12_000_000),
         name="project",
-    )(place, x, near, far, cosine, sine, *earlier)
+    )(place, x, *near, *far, cosine, sine, *earlier)
 
 
 def chunk_scores(query, key, behind, row, core):
@@ -344,10 +342,10 @@
     return bent, powers
 
 
-def attend_kernel(place, queries, pair, behind, near, far, *rest):
+def attend_kernel(place, queries, pair, behind, one, two, one_far, two_far, *rest):
     attended, result, weight, sems = rest[-4:]
     width = (GROUP + 2) * HEAD_DIM
-    copies = fetch_rows(place, near, far, weight, sems, width, GROUP * HEAD_DIM)
+    copies = fetch_rows(place, (one, two), (one_far, two_far), weight, sems, width, GROUP * HEAD_DIM)
     for copy in copies:
         copy.start()
     core = place[1]
@@ -379,7 +377,7 @@
     bf16 = jnp.bfloat16
     return pl.pallas_call(
         attend_kernel,
-        in_specs=[spec_smem()] + [spec_vmem()] * 3 + [spec_any()] * (2 + len(earlier)),
+        in_specs=[spec_smem()] + [spec_vmem()] * 3 + [spec_any()] * (4 + len(earlier)),
         out_specs=[spec_vmem()] * 2,
         out_shape=[shaped((tokens, GROUP * HEAD_DIM), bf16), shaped((tokens, width), bf16)],
         scratch_shapes=[
@@ -389,7 +387,7 @@
         compiler_params=kernel_params(),
         cost_estimate=cost(4 * tokens * width * 1024, 8_000_000),
         name="attend",
-    )(place, queries, pair, behind, near, far, *earlier)
+    )(place, queries, pair, behind, *near, *far, *earlier)
 
 
 def whole(shape):
@@ -406,28 +404,31 @@
     return copy
 
 
-def ffn_kernel(attn_out, x, gains, gate_up, down, *rest):
+def ffn_kernel(place, attn_out, x, gains, up_full, *rest):
+    gate_near, gate_far, down_near, down_far = (rest[k : k + 2] for k in (0, 2, 4, 6))
     outs, (sides, gate_up_here, down_here, in_sems, down_sems, out_sems) = rest[-11:-6], rest[-6:]
     ffn_in, hidden, by_gate, by_up, result = (sides.at[k] for k in range(5))
     tokens, width = x.shape
-    units = gate_up.shape[2]
+    units = up_full.shape[1]
     tile = FFN_TILE
     steps, turns = units // tile, width // tile
 
     def load(step):
         columns = pl.ds(pl.multiple_of(step * tile, tile), tile)
-        return pltpu.make_async_copy(
-            gate_up.at[:, :, columns], gate_up_here.at[:, :, columns], in_sems.at[step]
+        up_copy = pltpu.make_async_copy(
+            up_full.at[:, columns], gate_up_here.at[1, :, columns], in_sems.at[step, 8]
         )
-
-    def load_down(turn):
-        rows = pl.ds(pl.multiple_of(turn * tile, tile), tile)
-        return pltpu.make_async_copy(down.at[rows, :], down_here.at[rows, :], down_sems.at[turn])
-
+        target = gate_up_here.at[0, :, columns]
+        return [up_copy] + fetch_rows(
+            place, gate_near, gate_far, target, in_sems.at[step], columns.start, tile
+        )
+
+    down_copies = fetch_rows(place, down_near, down_far, down_here, down_sems, 0, units)
     for step in range(steps):
-        load(step).start()
-    for turn in range(turns):
-        load_down(turn).start()
+        for copy in load(step):
+            copy.start()
+    for copy in down_copies:
+        copy.start()
     chunk = ROW_CHUNK
 
     @pl.loop(0, tokens // chunk, unroll=ROW_UNROLL)
@@ -441,7 +442,8 @@
 
     @pl.loop(0, steps)
     def _(step):
-        load(step).wait()
+        for copy in load(step):
+            copy.wait()
         columns = pl.ds(pl.multiple_of(step * tile, tile), tile)
         for rows in (slice(None),):
             value = ffn_in[...]
@@ -467,9 +469,11 @@
             result.at[:, columns], outs[4].at[:, columns], out_sems.at[4 + turn]
         )
 
+    for copy in down_copies:
+        copy.wait()
+
     @pl.loop(0, turns)
     def _(turn):
-        load_down(turn).wait()
         rows = pl.ds(pl.multiple_of(turn * tile, tile), tile)
         result[:, rows] = dot_nt(hidden[...], down_here[rows, :]).astype(jnp.bfloat16)
         store(turn).start()
@@ -480,13 +484,13 @@
         store(turn).wait()
 
 
-def ffn_forward(attn_out, x, gains, gate_up, down, *earlier):
+def ffn_forward(place, attn_out, x, gains, up, gate, down):
     tokens, width = x.shape
-    units = gate_up.shape[2]
+    units = up.shape[1]
     bf16 = jnp.bfloat16
     return pl.pallas_call(
         ffn_kernel,
-        in_specs=[spec_vmem()] * 3 + [spec_any()] * (2 + len(earlier)),
+        in_specs=[spec_smem()] + [spec_vmem()] * 3 + [spec_any()] * 9,
         out_specs=[spec_any()] * 5,
         out_shape=[shaped((tokens, width), bf16)]
         + [shaped((tokens, units), bf16)] * 3
@@ -495,22 +499,22 @@
             pltpu.VMEM((5, tokens, width), bf16),
             pltpu.VMEM((2, width, units), bf16),
             pltpu.VMEM((width, units), bf16),
-            pltpu.SemaphoreType.DMA((units // FFN_TILE,)),
-            pltpu.SemaphoreType.DMA((width // FFN_TILE,)),
+            pltpu.SemaphoreType.DMA((units // FFN_TILE, 9)),
+            pltpu.SemaphoreType.DMA((8,)),
             pltpu.SemaphoreType.DMA((4 + width // FFN_TILE,)),
         ],
         compiler_params=ffn_params(),
         cost_estimate=cost(6 * tokens * width * units, 50_000_000),
         name="ffn_forward",
-    )(attn_out, x, gains, gate_up, down, *earlier)
-
-
-def ffn_back_kernel(ffn_out, top, gains, gate_up, down, by_gate, by_up, *rest):
+    )(place, attn_out, x, gains, up, *gate[0], *gate[1], *down[0], *down[1])
+
+
+def ffn_back_kernel(ffn_out, top, gains, gate, up_full, down, by_gate, by_up, *rest):
     grad_out, gate_out, up_out, gain_out, result_out = rest[-13:-8]
     sides, grads, gate_up_here, down_here, in_sems, down_sems, gate_sems, out_sems = rest[-8:]
     grad_ffn, result = sides.at[0], sides.at[1]
     tokens, width = top.shape
-    units = gate_up.shape[2]
+    units = gate.shape[1]
     grad_gate, grad_up = grads.at[:, pl.ds(0, units)], grads.at[:, pl.ds(units, units)]
     tile = FFN_TILE
     steps, turns = units // tile, width // tile
@@ -524,7 +528,7 @@
     def load(turn, which):
         rows = pl.ds(pl.multiple_of(turn * tile, tile), tile)
         return pltpu.make_async_copy(
-            gate_up.at[which, rows, :],
+            (gate, up_full)[which].at[rows, :],
             gate_up_here.at[rows, pl.ds(which * units, units)],
             gate_sems.at[turn, which],
         )
@@ -603,13 +607,13 @@
         store(turn).wait()
 
 
-def ffn_back(ffn_out, top, gains, gate_up, down, by_gate, by_up, *earlier):
+def ffn_back(ffn_out, top, gains, gate, up, down, by_gate, by_up, *earlier):
     tokens, width = top.shape
     units = by_up.shape[1]
     bf16 = jnp.bfloat16
     return pl.pallas_call(
         ffn_back_kernel,
-        in_specs=[spec_vmem()] * 3 + [spec_any()] * (4 + len(earlier)),
+        in_specs=[spec_vmem()] * 3 + [spec_any()] * (5 + len(earlier)),
         out_specs=[spec_any()] * 3 + [spec_vmem(), spec_any()],
         out_shape=[
             shaped((tokens, width), bf16),
@@ -631,16 +635,16 @@
         compiler_params=ffn_params(),
         cost_estimate=cost(6 * tokens * width * units, 55_000_000),
         name="ffn_back",
-    )(ffn_out, top, gains, gate_up, down, by_gate, by_up, *earlier)
-
-
-def mid_back_kernel(place, grad_in, x, attn_out, top, gains, near, far, *rest):
+    )(ffn_out, top, gains, gate, up, down, by_gate, by_up, *earlier)
+
+
+def mid_back_kernel(place, grad_in, x, attn_out, top, gains, one, two, one_far, two_far, *rest):
     grad_mid, grad_attn, grad_att, gain_out, weight, sems = rest[-6:]
     width = (GROUP + 2) * HEAD_DIM
     first = pl.program_id(0) == 0
 
     def fetch():
-        return fetch_rows(place, near, far, weight, sems, width, GROUP * HEAD_DIM)
+        return fetch_rows(place, (one, two), (one_far, two_far), weight, sems, width, GROUP * HEAD_DIM)
 
     @pl.when(first)
     def _():
@@ -684,7 +688,7 @@
         in_specs=[spec_smem()]
         + [rows] * 4
         + [whole((8, width))]
-        + [spec_any()] * (2 + len(earlier)),
+        + [spec_any()] * (4 + len(earlier)),
         out_specs=[
             rows,
             rows,
@@ -701,7 +705,7 @@
         compiler_params=kernel_params(),
         cost_estimate=cost(2 * tokens * width * heads, 24_000_000),
         name="mid_back",
-    )(place, grad_in, x, attn_out, top, gains, near, far, *earlier)
+    )(place, grad_in, x, attn_out, top, gains, *near, *far, *earlier)
 
 
 def attend_back_kernel(
@@ -768,11 +772,11 @@
 
 
 def project_back_kernel(
-    place, grad_q, grad_own, grad_ahead, cosine, sine, x, near, far, *rest
+    place, grad_q, grad_own, grad_ahead, cosine, sine, x, one, two, one_far, two_far, *rest
 ):
     proj, result, gain_out, weight, sems = rest[-5:]
     width = (GROUP + 2) * HEAD_DIM
-    copies = fetch_rows(place, near, far, weight, sems, 0, width)
+    copies = fetch_rows(place, (one, two), (one_far, two_far), weight, sems, 0, width)
     for copy in copies:
         copy.start()
     heads = GROUP * HEAD_DIM
@@ -807,7 +811,7 @@
         project_back_kernel,
         in_specs=[spec_smem()]
         + [spec_vmem()] * 6
-        + [spec_any()] * 2
+        + [spec_any()] * 4
         + [spec_any()] * len(earlier),
         out_specs=[spec_vmem()] * 3,
         out_shape=[
@@ -819,7 +823,7 @@
         compiler_params=kernel_params(),
         cost_estimate=cost(2 * tokens * width * proj_width, 14_000_000),
         name="project_back",
-    )(place, grad_q, grad_own, grad_ahead, cosine, sine, x, near, far, *earlier)
+    )(place, grad_q, grad_own, grad_ahead, cosine, sine, x, *near, *far, *earlier)
 
 
 def stream_back_kernel(grad_in, x, gains, grad_mid, *rest):
@@ -948,41 +952,49 @@
     stream, top = layer_in[0], cotangent[0]
     gains_cast = jnp.pad(norm_gains.T, ((0, 0), (0, 128 - norm_gains.shape[0])))
     attn_cast = jnp.concatenate([qkv_weight[:, 0], out_weight.T, gains_cast], axis=1)
-    gate_up_cast = gate_up_weight.astype(jnp.bfloat16).transpose(1, 0, 2)
+    gate_cast = gate_up_weight[:, 0].astype(jnp.bfloat16)
+    up_cast = gate_up_weight[:, 1].astype(jnp.bfloat16)
     down_cast = down_weight.T.astype(jnp.bfloat16)
     attn_cast = attn_cast.astype(jnp.bfloat16)
-    first, down_cast, gate_up_cast = lax.optimization_barrier(
-        (trade(attn_cast, 0), down_cast, gate_up_cast)
-    )
-    second = trade(jnp.stack([attn_cast, first]), 1)
+    first, gate_cast, up_cast, down_cast = lax.optimization_barrier(
+        (trade(attn_cast, 0), gate_cast, up_cast, down_cast)
+    )
+    attn_pair = jnp.stack([attn_cast, first])
+    near = (attn_pair, trade(attn_pair, 1))
+    far = tuple(swap(part, "seq", 1) for part in near)
     down_one = trade(down_cast, 0)
-    near = gather_end(attn_cast, first, second)
-    far = swap(near, "seq", 1)
-    down_one, far = lax.optimization_barrier((down_one, far))
-    down_two = trade(jnp.stack([down_cast, down_one]), 1)
-    down_near = gather_end(down_cast, down_one, down_two)
-    down = arrange(place, down_near, swap(down_near, "seq", 1))
-    gate_up = lax.all_gather(gate_up_cast, plane, axis=1, tiled=True)
+    gate_one = trade(gate_cast, 0)
+    down_pair, gate_pair = jnp.stack([down_cast, down_one]), jnp.stack([gate_cast, gate_one])
+    down_pair_far, gate_pair_far = swap(down_pair, "seq", 1), swap(gate_pair, "seq", 1)
+    down_two = trade(down_pair, 1)
+    gate_two = trade(after(gate_pair, down_pair_far, gate_pair_far), 1)
+    down_parts = (down_pair, down_two), (down_pair_far, swap(down_two, "seq", 1))
+    gate_parts = (gate_pair, gate_two), (gate_pair_far, swap(gate_two, "seq", 1))
+    up = lax.all_gather(up_cast, plane, axis=0, tiled=True)
     positions = core * tok_rows + jnp.arange(tok_rows, dtype=jnp.int32)
     cosine, sine = rope_tables(positions, HEAD_DIM)
 
     queries, pair, attn_in, gains = project(
-        place, stream, near, far, cosine, sine, gate_up_cast
+        place, stream, near, far, cosine, sine, up_cast
     )
     behind = from_behind(pair, "seq", 1)
     attended, attn_part = attend(
-        place, queries, pair, behind, near, far, stream.shape[1], down_two
+        place, queries, pair, behind, near, far, stream.shape[1], down_one, gate_one
     )
     attn_out = tensor_sum(attn_part)
-    ffn_in, hidden, by_gate, by_up, ffn_part = ffn_forward(attn_out, stream, gains, gate_up, down)
+    ffn_in, hidden, by_gate, by_up, ffn_part = ffn_forward(
+        place, attn_out, stream, gains, up, gate_parts, down_parts
+    )
     ffn_out = tensor_sum(ffn_part)
 
+    gate = arrange(place, *gate_parts)
+    down = arrange(place, *down_parts)
     att_both = jnp.concatenate([attended, swap(attended, "seq", 1)], axis=0)
     attn_in_both = both_cores(attn_in)
     ffn_in_both = both_cores(ffn_in)
     hidden_both = jnp.concatenate([hidden, swap(hidden, "seq", 1)], axis=0)
     grad_ffn, grad_gate, grad_up, gain_ffn, grad_ffn_part = ffn_back(
-        ffn_out, top, gains, gate_up, down, by_gate, by_up, att_both, attn_in_both, ffn_in_both,
+        ffn_out, top, gains, gate, up, down, by_gate, by_up, att_both, attn_in_both, ffn_in_both,
         hidden_both
     )
     grad_ffn_in = tensor_sum(grad_ffn_part)

time: 664 us -> 647 us (0.974)
  waiting for transfers between devices: 275 us -> 247 us
  Pallas kernels: 171 us -> 179 us
    psum x4, waiting for transfers between devices: 139 us -> 47.9 us  [tensor_sum(): return lax.psum(part, 'tensor')]
    ppermute x14 -> x16, waiting for transfers between devices: 107 us -> 187 us  [trade(): return lax.ppermute(value, ('batch', 'seq'), pairs)]
    all_gather x1, waiting for transfers between devices: 15.7 us -> 0.01 us  [on_square(): up = lax.all_gather(up_cast, plane, axis=0, tiled=True)]
    pallas_call x3 -> x4, Pallas kernels: 45.3 us -> 53.3 us  [the longest x1 24.9 us: ffn_forward(): pl.pallas_call(ffn_kernel, in_specs=[spec_smem()] + [spec_vmem()] * 3 + [...]
    ppermute x14 -> x16, starting transfers between devices: 22.4 us -> 23.9 us  [trade(): return lax.ppermute(value, ('batch', 'seq'), pairs)]
    unnamed x88 -> x104, local copies, waits for them, and re-layouts: 22.4 us -> 21.1 us
  transfers between devices with their start and end apart: 37 -> 43, of which waited for: 15 -> 15; matrix products, arithmetic and copies ran while one was open for 22% -> 22% of each run, Pallas kernels for 16% -> 18%
where the time goes in v3:
time: 647 us; the launch traced here: 638 us
  waiting for transfers between devices  247 us (38%)
  Pallas kernels  179 us (28%)
  local copies, waits for them, and re-layouts  82.1 us (13%)
  other arithmetic  40.3 us (6%)
  matrix products  39 us (6%)
  starting transfers between devices  35 us (5%)
  between operations  16.4 us (3%)
    ppermute x16, waiting for transfers between devices, trade(): return lax.ppermute(value, ('batch', 'seq'), pairs)  187 us
    psum x4, waiting for transfers between devices, tensor_sum(): return lax.psum(part, 'tensor')  47.9 us
    pallas_call x4, Pallas kernels, adam(): pl.pallas_call(functools.partial(adam_kernel, len(grads), decay), grid=(9...  42.9 us
    dot_general x5, matrix products, rows_product(): lax.dot_general(left, right, (((0,), (0,)), ((), ())), preferred_element_...  39 us
    pallas_call x1, Pallas kernels, ffn_back(): pl.pallas_call(ffn_back_kernel, in_specs=[spec_vmem()] * 3 + [spec_any()]...  26.2 us
    pallas_call x1, Pallas kernels, ffn_forward(): pl.pallas_call(ffn_kernel, in_specs=[spec_smem()] + [spec_vmem()] * 3 + [...  24.9 us
    ppermute x16, starting transfers between devices, trade(): return lax.ppermute(value, ('batch', 'seq'), pairs)  23.9 us
    unnamed x104, local copies, waits for them, and re-layouts  21.1 us
  transfers between devices with their start and end apart: 43, of which 15 were waited for; matrix products, arithmetic and copies ran while one was open for 22% of the time, Pallas kernels for 18%

profile of v3, /device:TPU:0, one launch (start us, length us, event | category | flops | bytes accessed | tf_op | source)
XLA Modules:
  0.0 638.2 jit_solution(14133544745028725526)
XLA Ops:
  19.8 7.9 %collective-permute-done = bf16[288,1664]{1,0:T(8,128)(2,1)} collective-permute-done((bf16[288,1664]{1,0:T(8,128)(2,1)S(1)}, bf16[288,1664]{1,0:T(8,128)(2,1)}, u32[]{:S(2)}, u32[]{:S(2)}) %collective-permute-start) | collective-permute-done | bytes 958496 | tf_op jit(solution)/shard_map/ppermute | solution.py:118
  31.3 22.2 %collective-permute-done.1.two = bf16[2,288,1664]{2,1,0:T(8,128)(2,1)} collective-permute-done((bf16[2,288,1664]{2,1,0:T(8,128)(2,1)S(1)}, bf16[2,288,1664]{2,1,0:T(8,128)(2,1)}, u32[]{:S(2)}, u32[]{:S(2)}) %collective-permute-start.1) | collective-permute-done | bytes 1916960 | tf_op jit(solution)/shard_map/ppermute | solution.py:118
  58.0 10.8 %project.1 = (bf16[512,512]{1,0:T(8,128)(2,1)}, bf16[2,512,256]{2,1,0:T(8,128)(2,1)}, bf16[512,2304]{1,0:T(8,128)(2,1)}, f32[8,2304]{1,0:T(8,128)}) custom-call(s32[2]{0:T(128)} %pad_add_fusion.place, bf16[512,2304]{1,0:T(8,128)(2,1)} %bitcast.200, bf16[2,288,1664]{2,1,0:T(8,128)(2,1)} %copy-done.1, bf16[2,288,1664]{2,1,0:T(8,128)(2,1)} %collective-permute-done.1.two, ...), custom_call_target="tpu_custom_call" | custom-call | flops 2415919104 | bytes 12000000 | tf_op jit(solution)/shard_map/project/pallas_call | solution.py:313
  71.6 14.2 %collective-permute-done.6.rest_1_ = bf16[288,2304]{1,0:T(8,128)(2,1)} collective-permute-done((bf16[288,2304]{1,0:T(8,128)(2,1)S(1)}, bf16[288,2304]{1,0:T(8,128)(2,1)}, u32[]{:S(2)}, u32[]{:S(2)}) %collective-permute-start.6) | collective-permute-done | bytes 1327136 | tf_op jit(solution)/shard_map/ppermute | solution.py:118
  86.6 7.7 %attend.1 = (bf16[512,512]{1,0:T(8,128)(2,1)}, bf16[512,2304]{1,0:T(8,128)(2,1)}) custom-call(s32[2]{0:T(128)} %pad_add_fusion.place, bf16[512,512]{1,0:T(8,128)(2,1)} %get-tuple-element.69.queries, bf16[2,512,256]{2,1,0:T(8,128)(2,1)} %get-tuple-element.70.pair, bf16[2,512,256]{2,1,0:T(8,128)(2,1)} %copy-done.48, bf16[2,288,1664]{2,1,0:T(8,128)(2,1)} %copy-done.1, ...), custom_call_target="tpu_custom_call" | custom-call | flops 4831838208 | bytes 8000000 | tf_op jit(solution)/shard_map/attend/pallas_call | solution.py:378
  102.2 3.8 collective-permute-done.8.rest_2_.one_far
  108.1 54.4 %collective-permute-done.11.rest_5_.two = bf16[2,288,2304]{2,1,0:T(8,128)(2,1)S(1)} collective-permute-done((bf16[2,288,2304]{2,1,0:T(8,128)(2,1)S(1)}, bf16[2,288,2304]{2,1,0:T(8,128)(2,1)S(1)}, u32[]{:S(2)}, u32[]{:S(2)}) %collective-permute-start.11) | collective-permute-done | bytes 2654240 | tf_op jit(solution)/shard_map/ppermute | solution.py:118
  162.5 40.6 %collective-permute-done.9.rest_1_.two = bf16[2,288,2304]{2,1,0:T(8,128)(2,1)} collective-permute-done((bf16[2,288,2304]{2,1,0:T(8,128)(2,1)S(1)}, bf16[2,288,2304]{2,1,0:T(8,128)(2,1)}, u32[]{:S(2)}, u32[]{:S(2)}) %collective-permute-start.9) | collective-permute-done | bytes 2654240 | tf_op jit(solution)/shard_map/ppermute | solution.py:118
  203.2 5.3 collective-permute-done.10.rest_3_.two_far
  208.4 24.9 %ffn_forward.1 = (bf16[512,2304]{1,0:T(8,128)(2,1)}, bf16[512,2304]{1,0:T(8,128)(2,1)}, bf16[512,2304]{1,0:T(8,128)(2,1)}, bf16[512,2304]{1,0:T(8,128)(2,1)}, bf16[512,2304]{1,0:T(8,128)(2,1)}) custom-call(s32[2]{0:T(128)} %pad_add_fusion.place, bf16[512,2304]{1,0:T(8,128)(2,1)} %all-reduce.6.cloned.1.call-done.attn_out, bf16[512,2304]{1,0:T(8,128)(2,1)} %bitcast.201, ...), custom_call_target="tpu_custom_call" | custom-call | flops 16307453952 | bytes 50000000 | tf_op jit(solution)/shard_map/ffn_forward/pallas_call | solution.py:491
  236.4 4.3 copy.73
  240.9 3.5 constant_dynamic-slice_fusion.6
  262.3 8.8 %arrange.3.down = bf16[2304,2304]{1,0:T(8,128)(2,1)} custom-call(s32[2]{0:T(128)} %pad_add_fusion.place, bf16[2,288,2304]{2,1,0:T(8,128)(2,1)} %copy-done.5, bf16[2,288,2304]{2,1,0:T(8,128)(2,1)} %copy-done.18, bf16[2,288,2304]{2,1,0:T(8,128)(2,1)} %copy-done.16, bf16[2,288,2304]{2,1,0:T(8,128)(2,1)} %collective-permute-done.12.rest_7_.two_far), custom_call_target="tpu_custom_call" | custom-call | bytes 21233664 | tf_op jit(solution)/shard_map/arrange/pallas_call | solution.py:268
  271.1 8.9 %arrange.2.gate = bf16[2304,2304]{1,0:T(8,128)(2,1)} custom-call(s32[2]{0:T(128)} %pad_add_fusion.place, bf16[2,288,2304]{2,1,0:T(8,128)(2,1)} %copy-done.6, bf16[2,288,2304]{2,1,0:T(8,128)(2,1)} %collective-permute-done.9.rest_1_.two, bf16[2,288,2304]{2,1,0:T(8,128)(2,1)} %copy-done.17, bf16[2,288,2304]{2,1,0:T(8,128)(2,1)} %collective-permute-done.10.rest_3_.two_far), custom_call_target="tpu_custom_call" | custom-call | bytes 21233664 | tf_op jit(solution)/shard_map/arrange/pallas_call | solution.py:268
  302.7 35.5 %all-reduce.8.cloned.1.call-done.ffn_out = bf16[512,2304]{1,0:T(8,128)(2,1)} async-done(((bf16[512,2304]{1,0:T(8,128)(2,1)}), bf16[512,2304]{1,0:T(8,128)(2,1)}) %all-reduce.8.cloned.1.call-update) | async-done | bytes 2359312 | tf_op jit(solution)/shard_map/psum | solution.py:101
  338.2 26.2 %ffn_back.1 = (bf16[512,2304]{1,0:T(8,128)(2,1)}, bf16[512,2304]{1,0:T(8,128)(2,1)}, bf16[512,2304]{1,0:T(8,128)(2,1)}, f32[8,2304]{1,0:T(8,128)}, bf16[512,2304]{1,0:T(8,128)(2,1)}) custom-call(bf16[512,2304]{1,0:T(8,128)(2,1)} %all-reduce.8.cloned.1.call-done.ffn_out, bf16[512,2304]{1,0:T(8,128)(2,1)} %bitcast.227, f32[8,2304]{1,0:T(8,128)} %get-tuple-element.74.gains, ...), custom_call_target="tpu_custom_call" | custom-call | flops 16307453952 | bytes 55000000 | tf_op jit(solution)/shard_map/ffn_back/pallas_call | solution.py:614
  374.1 14.5 %convolution_convert_fusion.2 = bf16[1152,2304]{1,0:T(8,128)(2,1)S(1)} fusion(bf16[1024,2304]{1,0:T(8,128)(2,1)} %constant_dynamic-update-slice_fusion.2.rest_3_, bf16[512,1152]{0,1:T(8,128)(2,1)} %collective-permute-done.17, bf16[512,288]{0,1:T(8,128)(2,1)S(1)} %copy-done.40, bf16[512,288]{0,1:T(8,128)(2,1)S(1)} %copy-done.41, ...), kind=kOutput, calls=%fused_computation.2 | convolution fusion | flops 5450268672 | bytes 12386304 | tf_op jit(solution)/shard_map/dot_general | solution.py:82
  391.7 8.6 %convolution_convert_fusion.1 = bf16[1152,2304]{1,0:T(8,128)(2,1)S(1)} fusion(bf16[512,2304]{1,0:T(8,128)(2,1)} %collective-permute-done.19, bf16[512,2304]{1,0:T(8,128)(2,1)} %get-tuple-element.85, bf16[512,1152]{1,0:T(8,128)(2,1)} %collective-permute-done.15, bf16[512,1152]{1,0:T(8,128)(2,1)S(1)} %copy-done.15), kind=kOutput, calls=%fused_computation.1 | convolution fusion | flops 5452627968 | bytes 12386304 | tf_op jit(solution)/shard_map/dot_general | solution.py:82
  404.9 8.4 %convolution_convert_fusion = bf16[1152,2304]{1,0:T(8,128)(2,1)S(1)} fusion(bf16[512,2304]{1,0:T(8,128)(2,1)} %collective-permute-done.23, bf16[512,2304]{1,0:T(8,128)(2,1)S(1)} %copy-done.47, bf16[512,1152]{1,0:T(8,128)(2,1)} %collective-permute-done.15, bf16[512,1152]{1,0:T(8,128)(2,1)S(1)} %copy-done.15), kind=kOutput, calls=%fused_computation | convolution fusion | flops 5452627968 | bytes 12386304 | tf_op jit(solution)/shard_map/dot_general | solution.py:82
  425.9 39.1 %collective-permute-done.20 = bf16[2,288,2304]{2,1,0:T(8,128)(2,1)S(1)} collective-permute-done((bf16[2,288,2304]{2,1,0:T(8,128)(2,1)S(1)}, bf16[2,288,2304]{2,1,0:T(8,128)(2,1)S(1)}, u32[]{:S(2)}, u32[]{:S(2)}) %collective-permute-start.20) | collective-permute-done | bytes 2654240 | tf_op jit(solution)/shard_map/ppermute | solution.py:118
  467.6 11.5 %mid_back.1 = (f32[512,2304]{1,0:T(8,128)}, bf16[512,2304]{1,0:T(8,128)(2,1)}, bf16[512,512]{1,0:T(8,128)(2,1)}, f32[2,8,2304]{2,1,0:T(8,128)}) custom-call(s32[2]{0:T(128)} %pad_add_fusion.place, bf16[512,2304]{1,0:T(8,128)(2,1)} %all-reduce.10.cloned.1.call-done.grad_in, bf16[512,2304]{1,0:T(8,128)(2,1)} %bitcast.202, ...), custom_call_target="tpu_custom_call" | custom-call | flops 1207959552 | bytes 24000000 | tf_op jit(solution)/shard_map/mid_back/pallas_call | solution.py:685
  479.1 9.6 %attend_back.1 = (bf16[512,512]{1,0:T(8,128)(2,1)}, f32[2,512,256]{2,1,0:T(8,128)}, bf16[2,512,256]{2,1,0:T(8,128)(2,1)}) custom-call(s32[2]{0:T(128)} %pad_add_fusion.place, bf16[512,512]{1,0:T(8,128)(2,1)} %get-tuple-element.69.queries, bf16[2,512,256]{2,1,0:T(8,128)(2,1)} %get-tuple-element.70.pair, bf16[2,512,256]{2,1,0:T(8,128)(2,1)} %copy-done.48, ...), custom_call_target="tpu_custom_call" | custom-call | flops 5368709120 | bytes 5000000 | tf_op jit(solution)/shard_map/attend_back/pallas_call | solution.py:758
  505.2 10.6 %project_back.1 = (bf16[512,1024]{1,0:T(8,128)(2,1)}, bf16[512,2304]{1,0:T(8,128)(2,1)}, f32[8,2304]{1,0:T(8,128)}) custom-call(s32[2]{0:T(128)} %pad_add_fusion.place, bf16[512,512]{1,0:T(8,128)(2,1)} %get-tuple-element.87.grad_q, f32[2,512,256]{2,1,0:T(8,128)} %get-tuple-element.88.grad_own, bf16[2,512,256]{2,1,0:T(8,128)(2,1)} %collective-permute-done.21.grad_ahead, ...), custom_call_target="tpu_custom_call" | custom-call | flops 2415919104 | bytes 14000000 | tf_op jit(solution)/shard_map/project_back/pallas_call | solution.py:810
  528.3 4.5 convolution_convert_fusion.3
  541.4 12.4 %adam.7 = (f32[288,2304]{1,0:T(8,128)}, f32[288,2304]{1,0:T(8,128)}, f32[288,2304]{1,0:T(8,128)}, f32[288,2304]{1,0:T(8,128)}) custom-call(bf16[288,2304]{1,0:T(8,128)(2,1)} %get-tuple-element.162.refs_0_, bf16[288,2304]{1,0:T(8,128)(2,1)} %slice_bitcast_fusion.refs_1_, bf16[288,2304]{1,0:T(8,128)(2,1)} %collective-permute-done.22.rest_0_.refs_2_, ...), custom_call_target="tpu_custom_call" | custom-call | bytes 200000000 | tf_op jit(solution)/shard_map/adam/pallas_call | solution.py:917
  557.6 4.9 collective-permute-done.29
  565.9 9.5 %join.1 = f32[288,2,2304]{2,1,0:T(2,128)} custom-call(bf16[288,2304]{1,0:T(8,128)(2,1)} %get-tuple-element.168.refs_0_, bf16[288,2304]{1,0:T(8,128)(2,1)} %slice_bitcast_fusion.6.rest_1_.refs_1_, bf16[288,2304]{1,0:T(8,128)(2,1)} %copy-done.23, bf16[288,2304]{1,0:T(8,128)(2,1)} %get-tuple-element.165.refs_3_, ...), custom_call_target="tpu_custom_call" | custom-call | bytes 200000000 | tf_op jit(solution)/shard_map/join/pallas_call | solution.py:889
  575.3 16.8 %adam.6 = (f32[10368,128]{1,0:T(8,128)}, f32[10368,128]{1,0:T(8,128)}, f32[10368,128]{1,0:T(8,128)}) custom-call(f32[10368,128]{1,0:T(8,128)} %bitcast.205, f32[10368,128]{1,0:T(8,128)} %bitcast.206, f32[10368,128]{1,0:T(8,128)} %bitcast.214, f32[10368,128]{1,0:T(8,128)} %bitcast.215), custom_call_target="tpu_custom_call" | custom-call | bytes 200000000 | tf_op jit(solution)/shard_map/adam/pallas_call | solution.py:917
  593.6 6.4 adam.5
  603.8 7.3 %adam.4 = (f32[2304,128]{1,0:T(8,128)}, f32[2304,128]{1,0:T(8,128)}, f32[2304,128]{1,0:T(8,128)}) custom-call(f32[2304,128]{1,0:T(8,128)} %reshape_broadcast_in_dim.3.refs_0_, f32[2304,128]{1,0:T(8,128)} %bitcast.222, f32[2304,128]{1,0:T(8,128)} %bitcast.247, f32[2304,128]{1,0:T(8,128)} %bitcast.248), custom_call_target="tpu_custom_call" | custom-call | bytes 200000000 | tf_op jit(solution)/shard_map/adam/pallas_call | solution.py:917
  611.1 12.3 %all-reduce.12.cloned.1.call-done.grad_in = bf16[512,2304]{1,0:T(8,128)(2,1)} async-done(((bf16[512,2304]{1,0:T(8,128)(2,1)}), bf16[512,2304]{1,0:T(8,128)(2,1)}) %all-reduce.12.cloned.1.call-update) | async-done | bytes 2359312 | tf_op jit(solution)/shard_map/psum | solution.py:101
  623.4 7.5 %stream_back.1 = f32[512,2304]{1,0:T(8,128)} custom-call(bf16[512,2304]{1,0:T(8,128)(2,1)} %all-reduce.12.cloned.1.call-done.grad_in, bf16[512,2304]{1,0:T(8,128)(2,1)} %bitcast.204, f32[8,2304]{1,0:T(8,128)} %get-tuple-element.74.gains, f32[512,2304]{1,0:T(8,128)} %get-tuple-element.92.grad_mid, f32[288,1,1024]{2,1,0:T(1,128)} %bitcast.245, ...), custom_call_target="tpu_custom_call" | custom-call | flops 23592960 | bytes 14000000 | tf_op jit(solution)/shard_map/stream_back/pallas_call | solution.py:846
  (267 shorter events, 159.0 us)
Async XLA Ops:
  8.0 195.1 %all-reduce.6.cloned.1.call-start = ((), (), s32[]{:S(2)}) async-start(), calls=%async_computation | async-start | bytes 4718592 | tf_op jit(solution)/shard_map/psum | solution.py:101
  12.7 14.9 %collective-permute-start = (bf16[288,1664]{1,0:T(8,128)(2,1)S(1)}, bf16[288,1664]{1,0:T(8,128)(2,1)}, u32[]{:S(2)}, u32[]{:S(2)}) collective-permute-start(bf16[288,1664]{1,0:T(8,128)(2,1)S(1)} %pad_maximum_fusion.11), channel_id=1, source_target_pairs={{0,8},{4,20},{8,0},{12,28},{16,24},{20,4},{24,16},{28,12},{1,9},{5... | collective-permute-start | bytes 2875400 | tf_op jit(solution)/shard_map/ppermute | solution.py:118
  29.2 24.3 %collective-permute-start.1 = (bf16[2,288,1664]{2,1,0:T(8,128)(2,1)S(1)}, bf16[2,288,1664]{2,1,0:T(8,128)(2,1)}, u32[]{:S(2)}, u32[]{:S(2)}) collective-permute-start(bf16[2,288,1664]{2,1,0:T(8,128)(2,1)S(1)} %pad_maximum_fusion.7.one), channel_id=1, source_target_pairs={{0,16},{4,12},{8,24},{12,4},{16,0},{20,28},{24,8},{28,20},{1,17},{... | collective-permute-start | bytes 5750792 | tf_op jit(solution)/shard_map/ppermute | solution.py:118
  31.3 26.6 %collective-permute-start.2 = (bf16[2,288,1664]{2,1,0:T(8,128)(2,1)S(1)}, bf16[2,288,1664]{2,1,0:T(8,128)(2,1)}, u32[]{:S(2)}, u32[]{:S(2)}) collective-permute-start(bf16[2,288,1664]{2,1,0:T(8,128)(2,1)S(1)} %pad_maximum_fusion.7.one), channel_id=1, source_target_pairs={{0,4},{4,0},{1,5},{5,1},{2,6},{6,2},{3,7},{7,3},{8,12},{12,8},{9,1... | collective-permute-start | bytes 5750792 | tf_op jit(solution)/shard_map/ppermute | solution.py:106
  53.5 18.1 %collective-permute-start.5 = (bf16[288,2304]{1,0:T(8,128)(2,1)}, bf16[288,2304]{1,0:T(8,128)(2,1)}, u32[]{:S(2)}, u32[]{:S(2)}) collective-permute-start(bf16[288,2304]{1,0:T(8,128)(2,1)} %bitcast_convert_fusion), channel_id=1, source_target_pairs={{0,8},{4,20},{8,0},{12,28},{16,24},{20,4},{24,16},{28,12},{1,9},{5... | collective-permute-start | bytes 3981320 | tf_op jit(solution)/shard_map/ppermute | solution.py:118
  55.5 30.3 %collective-permute-start.6 = (bf16[288,2304]{1,0:T(8,128)(2,1)S(1)}, bf16[288,2304]{1,0:T(8,128)(2,1)}, u32[]{:S(2)}, u32[]{:S(2)}) collective-permute-start(bf16[288,2304]{1,0:T(8,128)(2,1)S(1)} %get-tuple-element.72), channel_id=1, source_target_pairs={{0,8},{4,20},{8,0},{12,28},{16,24},{20,4},{24,16},{28,12},{1,9},{5... | collective-permute-start | bytes 3981320 | tf_op jit(solution)/shard_map/ppermute | solution.py:118
  68.8 17.1 %collective-permute-start.4 = (bf16[2,512,256]{2,1,0:T(8,128)(2,1)}, bf16[2,512,256]{2,1,0:T(8,128)(2,1)S(1)}, u32[]{:S(2)}, u32[]{:S(2)}) collective-permute-start(bf16[2,512,256]{2,1,0:T(8,128)(2,1)} %get-tuple-element.70.pair), channel_id=1, source_target_pairs={{0,4},{1,5},{2,6},{3,7},{8,12},{9,13},{10,14},{11,15},{16,20},{17,... | collective-permute-start | bytes 1572872 | tf_op jit(solution)/shard_map/ppermute | solution.py:29
  94.4 114.1 %all-gather.2.cloned.1.call-start = ((), (), s32[]{:S(2)}) async-start(), calls=%async_computation.1 | async-start | bytes 11943936 | tf_op jit(solution)/shard_map/all_gather | solution.py:973
  94.9 243.3 %all-reduce.8.cloned.1.call-start = ((), (), s32[]{:S(2)}) async-start(), calls=%async_computation.2 | async-start | bytes 4718592 | tf_op jit(solution)/shard_map/psum | solution.py:101
  99.9 62.6 %collective-permute-start.11 = (bf16[2,288,2304]{2,1,0:T(8,128)(2,1)S(1)}, bf16[2,288,2304]{2,1,0:T(8,128)(2,1)S(1)}, u32[]{:S(2)}, u32[]{:S(2)}) collective-permute-start(bf16[2,288,2304]{2,1,0:T(8,128)(2,1)S(1)} %pad_maximum_fusion.1.rest_4_.one), channel_id=1, source_target_pairs={{0,16},{4,12},{8,24},{12,4},{16,0},{20,28},{24,8},{28,20},{1,17},{... | collective-permute-start | bytes 7962632 | tf_op jit(solution)/shard_map/ppermute | solution.py:118
  106.0 97.1 %collective-permute-start.9 = (bf16[2,288,2304]{2,1,0:T(8,128)(2,1)S(1)}, bf16[2,288,2304]{2,1,0:T(8,128)(2,1)}, u32[]{:S(2)}, u32[]{:S(2)}) collective-permute-start(bf16[2,288,2304]{2,1,0:T(8,128)(2,1)S(1)} %pad_maximum_fusion.rest_0_.one), channel_id=1, source_target_pairs={{0,16},{4,12},{8,24},{12,4},{16,0},{20,28},{24,8},{28,20},{1,17},{... | collective-permute-start | bytes 7962632 | tf_op jit(solution)/shard_map/ppermute | solution.py:118
  162.5 40.6 %collective-permute-start.12 = (bf16[2,288,2304]{2,1,0:T(8,128)(2,1)S(1)}, bf16[2,288,2304]{2,1,0:T(8,128)(2,1)}, u32[]{:S(2)}, u32[]{:S(2)}) collective-permute-start(bf16[2,288,2304]{2,1,0:T(8,128)(2,1)S(1)} %collective-permute-done.11.rest_5_.two), channel_id=1, source_target_pairs={{0,4},{4,0},{1,5},{5,1},{2,6},{6,2},{3,7},{7,3},{8,12},{12,8},{9,1... | collective-permute-start | bytes 7962632 | tf_op jit(solution)/shard_map/ppermute | solution.py:106
  233.3 66.2 %collective-permute-start.16 = (bf16[512,2304]{1,0:T(8,128)(2,1)}, bf16[512,2304]{1,0:T(8,128)(2,1)}, u32[]{:S(2)}, u32[]{:S(2)}) collective-permute-start(bf16[512,2304]{1,0:T(8,128)(2,1)} %get-tuple-element.82), channel_id=1, source_target_pairs={{0,4},{4,0},{1,5},{5,1},{2,6},{6,2},{3,7},{7,3},{8,12},{12,8},{9,1... | collective-permute-start | bytes 7077896 | tf_op jit(solution)/shard_map/ppermute | solution.py:106
  240.7 227.0 %all-reduce.10.cloned.1.call-start = ((), (), s32[]{:S(2)}) async-start(), calls=%async_computation.3 | async-start | bytes 4718592 | tf_op jit(solution)/shard_map/psum | solution.py:101
  252.1 41.6 %collective-permute-start.15 = (bf16[512,1152]{1,0:T(8,128)(2,1)}, bf16[512,1152]{1,0:T(8,128)(2,1)}, u32[]{:S(2)}, u32[]{:S(2)}) collective-permute-start(bf16[512,1152]{1,0:T(8,128)(2,1)} %concatenate.87), channel_id=1, source_target_pairs={{0,4},{4,0},{1,5},{5,1},{2,6},{6,2},{3,7},{7,3},{8,12},{12,8},{9,1... | collective-permute-start | bytes 3538952 | tf_op jit(solution)/shard_map/ppermute | solution.py:106
  258.2 38.3 %collective-permute-start.14 = (bf16[512,1152]{1,0:T(8,128)(2,1)}, bf16[512,1152]{1,0:T(8,128)(2,1)}, u32[]{:S(2)}, u32[]{:S(2)}) collective-permute-start(bf16[512,1152]{1,0:T(8,128)(2,1)} %concatenate.84), channel_id=1, source_target_pairs={{0,4},{4,0},{1,5},{5,1},{2,6},{6,2},{3,7},{7,3},{8,12},{12,8},{9,1... | collective-permute-start | bytes 3538952 | tf_op jit(solution)/shard_map/ppermute | solution.py:106
  371.7 20.1 %collective-permute-start.19 = (bf16[512,2304]{1,0:T(8,128)(2,1)}, bf16[512,2304]{1,0:T(8,128)(2,1)}, u32[]{:S(2)}, u32[]{:S(2)}) collective-permute-start(bf16[512,2304]{1,0:T(8,128)(2,1)} %get-tuple-element.85), channel_id=1, source_target_pairs={{0,4},{4,0},{1,5},{5,1},{2,6},{6,2},{3,7},{7,3},{8,12},{12,8},{9,1... | collective-permute-start | bytes 7077896 | tf_op jit(solution)/shard_map/ppermute | solution.py:106
  372.3 251.1 %all-reduce.12.cloned.1.call-start = ((), (), s32[]{:S(2)}) async-start(), calls=%async_computation.4 | async-start | bytes 4718592 | tf_op jit(solution)/shard_map/psum | solution.py:101
  372.8 31.6 %collective-permute-start.23 = (bf16[512,2304]{1,0:T(8,128)(2,1)}, bf16[512,2304]{1,0:T(8,128)(2,1)}, u32[]{:S(2)}, u32[]{:S(2)}) collective-permute-start(bf16[512,2304]{1,0:T(8,128)(2,1)} %get-tuple-element.90), channel_id=1, source_target_pairs={{0,4},{4,0},{1,5},{5,1},{2,6},{6,2},{3,7},{7,3},{8,12},{12,8},{9,1... | collective-permute-start | bytes 7077896 | tf_op jit(solution)/shard_map/ppermute | solution.py:106
  390.2 32.6 %collective-permute-start.18 = (bf16[2,288,2304]{2,1,0:T(8,128)(2,1)S(1)}, bf16[2,288,2304]{2,1,0:T(8,128)(2,1)S(1)}, u32[]{:S(2)}, u32[]{:S(2)}) collective-permute-start(bf16[2,288,2304]{2,1,0:T(8,128)(2,1)S(1)} %pad_maximum_fusion.2), channel_id=1, source_target_pairs={{0,8},{4,20},{8,0},{12,28},{16,24},{20,4},{24,16},{28,12},{1,9},{5... | collective-permute-start | bytes 7962632 | tf_op jit(solution)/shard_map/ppermute | solution.py:118
  403.4 61.5 %collective-permute-start.20 = (bf16[2,288,2304]{2,1,0:T(8,128)(2,1)S(1)}, bf16[2,288,2304]{2,1,0:T(8,128)(2,1)S(1)}, u32[]{:S(2)}, u32[]{:S(2)}) collective-permute-start(bf16[2,288,2304]{2,1,0:T(8,128)(2,1)S(1)} %pad_maximum_fusion.3), channel_id=1, source_target_pairs={{0,8},{4,20},{8,0},{12,28},{16,24},{20,4},{24,16},{28,12},{1,9},{5... | collective-permute-start | bytes 7962632 | tf_op jit(solution)/shard_map/ppermute | solution.py:118
  418.1 75.4 %collective-permute-start.24 = (bf16[2,288,2304]{2,1,0:T(8,128)(2,1)}, bf16[2,288,2304]{2,1,0:T(8,128)(2,1)}, u32[]{:S(2)}, u32[]{:S(2)}) collective-permute-start(bf16[2,288,2304]{2,1,0:T(8,128)(2,1)} %pad_maximum_fusion.4), channel_id=1, source_target_pairs={{0,8},{4,20},{8,0},{12,28},{16,24},{20,4},{24,16},{28,12},{1,9},{5... | collective-permute-start | bytes 7962632 | tf_op jit(solution)/shard_map/ppermute | solution.py:118
  424.4 80.8 %collective-permute-start.22 = (bf16[288,2304]{1,0:T(8,128)(2,1)}, bf16[288,2304]{1,0:T(8,128)(2,1)}, u32[]{:S(2)}, u32[]{:S(2)}) collective-permute-start(bf16[288,2304]{1,0:T(8,128)(2,1)} %fusion.15.rest_0_), channel_id=1, source_target_pairs={{0,16},{4,12},{8,24},{12,4},{16,0},{20,28},{24,8},{28,20},{1,17},{... | collective-permute-start | bytes 3981320 | tf_op jit(solution)/shard_map/ppermute | solution.py:118
  488.8 16.5 %collective-permute-start.21 = (bf16[2,512,256]{2,1,0:T(8,128)(2,1)}, bf16[2,512,256]{2,1,0:T(8,128)(2,1)}, u32[]{:S(2)}, u32[]{:S(2)}) collective-permute-start(bf16[2,512,256]{2,1,0:T(8,128)(2,1)} %get-tuple-element.89), channel_id=1, source_target_pairs={{4,0},{5,1},{6,2},{7,3},{12,8},{13,9},{14,10},{15,11},{20,16},{21,... | collective-permute-start | bytes 1572872 | tf_op jit(solution)/shard_map/ppermute | solution.py:29
  496.6 68.2 %collective-permute-start.32 = (bf16[288,2304]{1,0:T(8,128)(2,1)}, bf16[288,2304]{1,0:T(8,128)(2,1)}, u32[]{:S(2)}, u32[]{:S(2)}) collective-permute-start(bf16[288,2304]{1,0:T(8,128)(2,1)} %fusion.13), channel_id=1, source_target_pairs={{0,16},{4,12},{8,24},{12,4},{16,0},{20,28},{24,8},{28,20},{1,17},{... | collective-permute-start | bytes 3981320 | tf_op jit(solution)/shard_map/ppermute | solution.py:118
  521.9 12.8 %collective-permute-start.28 = (bf16[512,1152]{0,1:T(8,128)(2,1)}, bf16[512,1152]{0,1:T(8,128)(2,1)}, u32[]{:S(2)}, u32[]{:S(2)}) collective-permute-start(bf16[512,1152]{0,1:T(8,128)(2,1)} %pad_maximum_fusion.10), channel_id=1, source_target_pairs={{0,4},{4,0},{1,5},{5,1},{2,6},{6,2},{3,7},{7,3},{8,12},{12,8},{9,1... | collective-permute-start | bytes 3538952 | tf_op jit(solution)/shard_map/ppermute | solution.py:106
  526.6 38.2 %collective-permute-start.31 = (bf16[288,2304]{1,0:T(8,128)(2,1)}, bf16[288,2304]{1,0:T(8,128)(2,1)S(1)}, u32[]{:S(2)}, u32[]{:S(2)}) collective-permute-start(bf16[288,2304]{1,0:T(8,128)(2,1)} %fusion.14), channel_id=1, source_target_pairs={{0,16},{4,12},{8,24},{12,4},{16,0},{20,28},{24,8},{28,20},{1,17},{... | collective-permute-start | bytes 3981320 | tf_op jit(solution)/shard_map/ppermute | solution.py:118
  528.2 25.7 %collective-permute-start.36 = (f32[4,2304]{1,0:T(4,128)S(1)}, f32[4,2304]{1,0:T(4,128)}, u32[]{:S(2)}, u32[]{:S(2)}) collective-permute-start(f32[4,2304]{1,0:T(4,128)S(1)} %add.247), channel_id=1, source_target_pairs={{0,1},{1,0},{2,3},{3,2},{4,5},{5,4},{6,7},{7,6},{8,9},{9,8},{10,11... | collective-permute-start | bytes 110600 | tf_op jit(solution)/shard_map/ppermute | solution.py:106
  533.1 23.4 %collective-permute-start.26 = (bf16[2,288,1024]{2,1,0:T(8,128)(2,1)S(1)}, bf16[2,288,1024]{2,1,0:T(8,128)(2,1)S(1)}, u32[]{:S(2)}, u32[]{:S(2)}) collective-permute-start(bf16[2,288,1024]{2,1,0:T(8,128)(2,1)S(1)} %pad_maximum_fusion.9), channel_id=1, source_target_pairs={{0,8},{4,20},{8,0},{12,28},{16,24},{20,4},{24,16},{28,12},{1,9},{5... | collective-permute-start | bytes 3538952 | tf_op jit(solution)/shard_map/ppermute | solution.py:118
  539.3 23.1 %collective-permute-start.29 = (bf16[2,288,512]{2,1,0:T(8,128)(2,1)}, bf16[2,288,512]{2,1,0:T(8,128)(2,1)S(1)}, u32[]{:S(2)}, u32[]{:S(2)}) collective-permute-start(bf16[2,288,512]{2,1,0:T(8,128)(2,1)} %pad_maximum_fusion.12), channel_id=1, source_target_pairs={{0,8},{4,20},{8,0},{12,28},{16,24},{20,4},{24,16},{28,12},{1,9},{5... | collective-permute-start | bytes 1769480 | tf_op jit(solution)/shard_map/ppermute | solution.py:118
  556.8 43.3 %collective-permute-start.27 = (bf16[288,1024]{1,0:T(8,128)(2,1)S(1)}, bf16[288,1024]{1,0:T(8,128)(2,1)S(1)}, u32[]{:S(2)}, u32[]{:S(2)}) collective-permute-start(bf16[288,1024]{1,0:T(8,128)(2,1)S(1)} %fusion.38), channel_id=1, source_target_pairs={{0,16},{4,12},{8,24},{12,4},{16,0},{20,28},{24,8},{28,20},{1,17},{... | collective-permute-start | bytes 1769480 | tf_op jit(solution)/shard_map/ppermute | solution.py:118
  562.6 30.4 %collective-permute-start.30 = (bf16[288,512]{1,0:T(8,128)(2,1)S(1)}, bf16[288,512]{1,0:T(8,128)(2,1)S(1)}, u32[]{:S(2)}, u32[]{:S(2)}) collective-permute-start(bf16[288,512]{1,0:T(8,128)(2,1)S(1)} %fusion.40), channel_id=1, source_target_pairs={{0,16},{4,12},{8,24},{12,4},{16,0},{20,28},{24,8},{28,20},{1,17},{... | collective-permute-start | bytes 884744 | tf_op jit(solution)/shard_map/ppermute | solution.py:118
  (60 other events, 602.8 us)
Sparse Core Ops, SparseCore 0:
  94.5 97.3 all-reduce.5
  240.8 97.4 all-reduce.7
  372.4 94.6 all-reduce.9
  528.3 95.0 all-reduce.11
Sparse Core Ops, SparseCore 1:
  97.3 86.9 all-gather.1

commit v4 on v3

--- a/solution.py
+++ b/solution.py
@@ -146,15 +146,16 @@
     return local.reshape(4, -1, local.shape[1])
 
 
-def scatter_begin(local):
-    got = trade(jnp.stack([local[1], local[3]]), 0)
+def scatter_begin(local, got=None):
+    if got is None:
+        got = trade(jnp.stack([local[1], local[3]]), 0)
     far = local[2].astype(jnp.float32) + got[1].astype(jnp.float32)
-    return local[0], got[0], far.astype(jnp.bfloat16)
+    return local, got, far.astype(jnp.bfloat16)
 
 
 def scatter_end(state):
-    own, got, far = state
-    return own, got, trade(far, 1)
+    local, got, far = state
+    return local[0], got[0], trade(far, 1)
 
 
 def everywhere_sum(value):
@@ -911,12 +912,13 @@
 
 def adam(grads, weight, first, second, decay):
     rows, width = weight.shape
-    tile = rows // 9
+    steps = 3 if rows * width < 1_000_000 else 6
+    tile = rows // steps
     block = pl.BlockSpec((tile, width), lambda i: (i, 0))
     count = 3 if len(grads) == 1 else 4
     return pl.pallas_call(
         functools.partial(adam_kernel, len(grads), decay),
-        grid=(9,),
+        grid=(steps,),
         in_specs=[block] * (len(grads) + 3),
         out_specs=[block] * count,
         out_shape=[shaped((rows, width), jnp.float32)] * count,
@@ -1005,7 +1007,7 @@
     up_local = weight_local(ffn_in_both, grad_up_both)
     down_state = scatter_begin(down_local)
     gate_state = scatter_begin(gate_local)
-    up_state = scatter_begin(up_local)
+    up_got = trade(jnp.stack([up_local[1], up_local[3]]), 0)
     down_grad = scatter_end(down_state)
 
     grad_mid, grad_attn, grad_att, gain_mid = mid_back(
@@ -1017,10 +1019,13 @@
     )
     grad_ahead = from_behind(grad_old, "seq", -1)
     grad_proj, grad_attn_part, gain_attn = project_back(
-        place, grad_q, grad_own, grad_ahead, cosine, sine, stream, near, far, down_grad[2], up_state[1]
+        place, grad_q, grad_own, grad_ahead, cosine, sine, stream, near, far, down_grad[2], up_got
     )
     grad_attn_in = tensor_sum(grad_attn_part)
-    up_grad = scatter_end(up_state)
+    grad_attn, gain_mid, up_got, down_grad = after(
+        (grad_attn, gain_mid, up_got, down_grad), grad_attn_part
+    )
+    up_grad = scatter_end(scatter_begin(up_local, up_got))
     gate_up_grad = join(gate_grad, up_grad)
 
     out_local = weight_local(both_cores(grad_attn), att_both)

time: 647 us -> 631 us (0.975)
  waiting for transfers between devices: 247 us -> 234 us
  Pallas kernels: 179 us -> 170 us
    ppermute x16, waiting for transfers between devices: 187 us -> 151 us  [trade(): return lax.ppermute(value, ('batch', 'seq'), pairs)]
    psum x4, waiting for transfers between devices: 47.9 us -> 70.2 us  [tensor_sum(): return lax.psum(part, 'tensor')]
    pallas_call x4, Pallas kernels: 42.9 us -> 34.5 us  [adam(): pl.pallas_call(functools.partial(adam_kernel, len(grads), decay), grid=(s...]
    unnamed x104 -> x100, local copies, waits for them, and re-layouts: 21.1 us -> 20.8 us
  transfers between devices with their start and end apart: 43 -> 43, of which waited for: 15 -> 17; matrix products, arithmetic and copies ran while one was open for 22% -> 25% of each run, Pallas kernels for 18% -> 17%
where the time goes in v4:
time: 631 us; the launch traced here: 623 us
  waiting for transfers between devices  234 us (37%)
  Pallas kernels  170 us (27%)
  local copies, waits for them, and re-layouts  81.3 us (13%)
  matrix products  43.9 us (7%)
  other arithmetic  43.3 us (7%)
  starting transfers between devices  33 us (5%)
  between operations  16.7 us (3%)
    ppermute x16, waiting for transfers between devices, trade(): return lax.ppermute(value, ('batch', 'seq'), pairs)  151 us
    psum x4, waiting for transfers between devices, tensor_sum(): return lax.psum(part, 'tensor')  70.2 us
    dot_general x5, matrix products, rows_product(): lax.dot_general(left, right, (((0,), (0,)), ((), ())), preferred_element_...  43.9 us
    pallas_call x4, Pallas kernels, adam(): pl.pallas_call(functools.partial(adam_kernel, len(grads), decay), grid=(s...  34.5 us
    pallas_call x1, Pallas kernels, ffn_back(): pl.pallas_call(ffn_back_kernel, in_specs=[spec_vmem()] * 3 + [spec_any()]...  26.1 us
    pallas_call x1, Pallas kernels, ffn_forward(): pl.pallas_call(ffn_kernel, in_specs=[spec_smem()] + [spec_vmem()] * 3 + [...  24.7 us
    ppermute x16, starting transfers between devices, trade(): return lax.ppermute(value, ('batch', 'seq'), pairs)  21.5 us
    unnamed x100, local copies, waits for them, and re-layouts  20.8 us
  transfers between devices with their start and end apart: 43, of which 17 were waited for; matrix products, arithmetic and copies ran while one was open for 25% of the time, Pallas kernels for 17%

profile of v4, /device:TPU:0, one launch (start us, length us, event | category | flops | bytes accessed | tf_op | source)
XLA Modules:
  0.0 623.1 jit_solution(5892174952617777340)
XLA Ops:
  19.8 7.9 %collective-permute-done = bf16[288,1664]{1,0:T(8,128)(2,1)} collective-permute-done((bf16[288,1664]{1,0:T(8,128)(2,1)S(1)}, bf16[288,1664]{1,0:T(8,128)(2,1)}, u32[]{:S(2)}, u32[]{:S(2)}) %collective-permute-start) | collective-permute-done | bytes 958496 | tf_op jit(solution)/shard_map/ppermute | solution.py:118
  31.3 22.2 %collective-permute-done.1.two = bf16[2,288,1664]{2,1,0:T(8,128)(2,1)} collective-permute-done((bf16[2,288,1664]{2,1,0:T(8,128)(2,1)S(1)}, bf16[2,288,1664]{2,1,0:T(8,128)(2,1)}, u32[]{:S(2)}, u32[]{:S(2)}) %collective-permute-start.1) | collective-permute-done | bytes 1916960 | tf_op jit(solution)/shard_map/ppermute | solution.py:118
  58.0 10.8 %project.1 = (bf16[512,512]{1,0:T(8,128)(2,1)}, bf16[2,512,256]{2,1,0:T(8,128)(2,1)}, bf16[512,2304]{1,0:T(8,128)(2,1)}, f32[8,2304]{1,0:T(8,128)}) custom-call(s32[2]{0:T(128)} %pad_add_fusion.place, bf16[512,2304]{1,0:T(8,128)(2,1)} %bitcast.198, bf16[2,288,1664]{2,1,0:T(8,128)(2,1)} %copy-done.1, bf16[2,288,1664]{2,1,0:T(8,128)(2,1)} %collective-permute-done.1.two, ...), custom_call_target="tpu_custom_call" | custom-call | flops 2415919104 | bytes 12000000 | tf_op jit(solution)/shard_map/project/pallas_call | solution.py:314
  71.6 14.2 %collective-permute-done.6.rest_1_ = bf16[288,2304]{1,0:T(8,128)(2,1)} collective-permute-done((bf16[288,2304]{1,0:T(8,128)(2,1)S(1)}, bf16[288,2304]{1,0:T(8,128)(2,1)}, u32[]{:S(2)}, u32[]{:S(2)}) %collective-permute-start.6) | collective-permute-done | bytes 1327136 | tf_op jit(solution)/shard_map/ppermute | solution.py:118
  86.6 7.7 %attend.1 = (bf16[512,512]{1,0:T(8,128)(2,1)}, bf16[512,2304]{1,0:T(8,128)(2,1)}) custom-call(s32[2]{0:T(128)} %pad_add_fusion.place, bf16[512,512]{1,0:T(8,128)(2,1)} %get-tuple-element.75.queries, bf16[2,512,256]{2,1,0:T(8,128)(2,1)} %get-tuple-element.76.pair, bf16[2,512,256]{2,1,0:T(8,128)(2,1)} %copy-done.46, bf16[2,288,1664]{2,1,0:T(8,128)(2,1)} %copy-done.1, ...), custom_call_target="tpu_custom_call" | custom-call | flops 4831838208 | bytes 8000000 | tf_op jit(solution)/shard_map/attend/pallas_call | solution.py:379
  108.2 54.7 %collective-permute-done.11.rest_5_.two = bf16[2,288,2304]{2,1,0:T(8,128)(2,1)S(1)} collective-permute-done((bf16[2,288,2304]{2,1,0:T(8,128)(2,1)S(1)}, bf16[2,288,2304]{2,1,0:T(8,128)(2,1)S(1)}, u32[]{:S(2)}, u32[]{:S(2)}) %collective-permute-start.11) | collective-permute-done | bytes 2654240 | tf_op jit(solution)/shard_map/ppermute | solution.py:118
  162.8 40.4 %collective-permute-done.9.rest_1_.two = bf16[2,288,2304]{2,1,0:T(8,128)(2,1)} collective-permute-done((bf16[2,288,2304]{2,1,0:T(8,128)(2,1)S(1)}, bf16[2,288,2304]{2,1,0:T(8,128)(2,1)}, u32[]{:S(2)}, u32[]{:S(2)}) %collective-permute-start.9) | collective-permute-done | bytes 2654240 | tf_op jit(solution)/shard_map/ppermute | solution.py:118
  203.3 5.2 collective-permute-done.10.rest_3_.two_far
  208.5 24.7 %ffn_forward.1 = (bf16[512,2304]{1,0:T(8,128)(2,1)}, bf16[512,2304]{1,0:T(8,128)(2,1)}, bf16[512,2304]{1,0:T(8,128)(2,1)}, bf16[512,2304]{1,0:T(8,128)(2,1)}, bf16[512,2304]{1,0:T(8,128)(2,1)}) custom-call(s32[2]{0:T(128)} %pad_add_fusion.place, bf16[512,2304]{1,0:T(8,128)(2,1)} %all-reduce.6.cloned.1.call-done.attn_out, bf16[512,2304]{1,0:T(8,128)(2,1)} %bitcast.199, ...), custom_call_target="tpu_custom_call" | custom-call | flops 16307453952 | bytes 50000000 | tf_op jit(solution)/shard_map/ffn_forward/pallas_call | solution.py:492
  236.7 4.3 copy.73
  257.0 8.8 %arrange.3.down = bf16[2304,2304]{1,0:T(8,128)(2,1)} custom-call(s32[2]{0:T(128)} %pad_add_fusion.place, bf16[2,288,2304]{2,1,0:T(8,128)(2,1)} %copy-done.6, bf16[2,288,2304]{2,1,0:T(8,128)(2,1)} %copy-done.20, bf16[2,288,2304]{2,1,0:T(8,128)(2,1)} %copy-done.19, bf16[2,288,2304]{2,1,0:T(8,128)(2,1)} %collective-permute-done.12.rest_7_.two_far), custom_call_target="tpu_custom_call" | custom-call | bytes 21233664 | tf_op jit(solution)/shard_map/arrange/pallas_call | solution.py:269
  269.4 3.9 concatenate.84
  274.2 8.8 %arrange.2.gate = bf16[2304,2304]{1,0:T(8,128)(2,1)} custom-call(s32[2]{0:T(128)} %pad_add_fusion.place, bf16[2,288,2304]{2,1,0:T(8,128)(2,1)} %copy-done.5, bf16[2,288,2304]{2,1,0:T(8,128)(2,1)} %collective-permute-done.9.rest_1_.two, bf16[2,288,2304]{2,1,0:T(8,128)(2,1)} %copy-done.18, bf16[2,288,2304]{2,1,0:T(8,128)(2,1)} %collective-permute-done.10.rest_3_.two_far), custom_call_target="tpu_custom_call" | custom-call | bytes 21233664 | tf_op jit(solution)/shard_map/arrange/pallas_call | solution.py:269
  304.7 33.8 %all-reduce.8.cloned.1.call-done.ffn_out = bf16[512,2304]{1,0:T(8,128)(2,1)} async-done(((bf16[512,2304]{1,0:T(8,128)(2,1)}), bf16[512,2304]{1,0:T(8,128)(2,1)}) %all-reduce.8.cloned.1.call-update) | async-done | bytes 2359312 | tf_op jit(solution)/shard_map/psum | solution.py:101
  338.5 26.1 %ffn_back.1 = (bf16[512,2304]{1,0:T(8,128)(2,1)}, bf16[512,2304]{1,0:T(8,128)(2,1)}, bf16[512,2304]{1,0:T(8,128)(2,1)}, f32[8,2304]{1,0:T(8,128)}, bf16[512,2304]{1,0:T(8,128)(2,1)}) custom-call(bf16[512,2304]{1,0:T(8,128)(2,1)} %all-reduce.8.cloned.1.call-done.ffn_out, bf16[512,2304]{1,0:T(8,128)(2,1)} %bitcast.225, f32[8,2304]{1,0:T(8,128)} %get-tuple-element.80.gains, ...), custom_call_target="tpu_custom_call" | custom-call | flops 16307453952 | bytes 55000000 | tf_op jit(solution)/shard_map/ffn_back/pallas_call | solution.py:615
  373.4 5.0 fusion.16
  378.5 14.7 %convolution_convert_fusion.2 = bf16[1152,2304]{1,0:T(8,128)(2,1)S(1)} fusion(bf16[1024,2304]{1,0:T(8,128)(2,1)} %constant_dynamic-update-slice_fusion.2.rest_3_, bf16[512,1152]{0,1:T(8,128)(2,1)} %collective-permute-done.17, bf16[512,288]{0,1:T(8,128)(2,1)S(1)} %copy-done.35, bf16[512,288]{0,1:T(8,128)(2,1)S(1)} %copy-done.36, ...), kind=kOutput, calls=%fused_computation.2 | convolution fusion | flops 5450268672 | bytes 12386304 | tf_op jit(solution)/shard_map/dot_general | solution.py:82
  396.2 8.2 %convolution_convert_fusion.1 = bf16[1152,2304]{1,0:T(8,128)(2,1)S(1)} fusion(bf16[512,2304]{1,0:T(8,128)(2,1)} %collective-permute-done.19, bf16[512,2304]{1,0:T(8,128)(2,1)S(1)} %copy-done.44, bf16[512,1152]{1,0:T(8,128)(2,1)} %collective-permute-done.15, bf16[512,1152]{1,0:T(8,128)(2,1)S(1)} %concatenate.86), kind=kOutput, calls=%fused_computation.1 | convolution fusion | flops 5452627968 | bytes 12386304 | tf_op jit(solution)/shard_map/dot_general | solution.py:82
  410.3 7.7 %convolution_convert_fusion = bf16[1152,2304]{1,0:T(8,128)(2,1)S(1)} fusion(bf16[512,2304]{1,0:T(8,128)(2,1)S(1)} %collective-permute-done.23, bf16[512,2304]{1,0:T(8,128)(2,1)S(1)} %copy-done.43, bf16[512,1152]{1,0:T(8,128)(2,1)} %collective-permute-done.15, bf16[512,1152]{1,0:T(8,128)(2,1)S(1)} %concatenate.86), kind=kOutput, calls=%fused_computation | convolution fusion | flops 5452627968 | bytes 12386304 | tf_op jit(solution)/shard_map/dot_general | solution.py:82
  430.6 34.5 %all-reduce.10.cloned.1.call-done.grad_in = bf16[512,2304]{1,0:T(8,128)(2,1)} async-done(((bf16[512,2304]{1,0:T(8,128)(2,1)}), bf16[512,2304]{1,0:T(8,128)(2,1)}) %all-reduce.10.cloned.1.call-update) | async-done | bytes 2359312 | tf_op jit(solution)/shard_map/psum | solution.py:101
  465.1 4.5 collective-permute-done.20.rest_1_
  469.6 11.5 %mid_back.1 = (f32[512,2304]{1,0:T(8,128)}, bf16[512,2304]{1,0:T(8,128)(2,1)}, bf16[512,512]{1,0:T(8,128)(2,1)}, f32[2,8,2304]{2,1,0:T(8,128)}) custom-call(s32[2]{0:T(128)} %pad_add_fusion.place, bf16[512,2304]{1,0:T(8,128)(2,1)} %all-reduce.10.cloned.1.call-done.grad_in, bf16[512,2304]{1,0:T(8,128)(2,1)} %bitcast.200, ...), custom_call_target="tpu_custom_call" | custom-call | flops 1207959552 | bytes 24000000 | tf_op jit(solution)/shard_map/mid_back/pallas_call | solution.py:686
  481.1 9.6 %attend_back.1 = (bf16[512,512]{1,0:T(8,128)(2,1)}, f32[2,512,256]{2,1,0:T(8,128)}, bf16[2,512,256]{2,1,0:T(8,128)(2,1)}) custom-call(s32[2]{0:T(128)} %pad_add_fusion.place, bf16[512,512]{1,0:T(8,128)(2,1)} %get-tuple-element.75.queries, bf16[2,512,256]{2,1,0:T(8,128)(2,1)} %get-tuple-element.76.pair, bf16[2,512,256]{2,1,0:T(8,128)(2,1)} %copy-done.46, ...), custom_call_target="tpu_custom_call" | custom-call | flops 5368709120 | bytes 5000000 | tf_op jit(solution)/shard_map/attend_back/pallas_call | solution.py:759
  500.5 10.8 %project_back.1 = (bf16[512,1024]{1,0:T(8,128)(2,1)}, bf16[512,2304]{1,0:T(8,128)(2,1)}, f32[8,2304]{1,0:T(8,128)}) custom-call(s32[2]{0:T(128)} %pad_add_fusion.place, bf16[512,512]{1,0:T(8,128)(2,1)} %get-tuple-element.93.grad_q, f32[2,512,256]{2,1,0:T(8,128)} %get-tuple-element.94.grad_own, bf16[2,512,256]{2,1,0:T(8,128)(2,1)} %copy-done.32, ...), custom_call_target="tpu_custom_call" | custom-call | flops 2415919104 | bytes 14000000 | tf_op jit(solution)/shard_map/project_back/pallas_call | solution.py:811
  526.0 4.2 convolution_convert_fusion.3
  532.3 9.0 %convolution_convert_fusion.4 = bf16[1152,512]{1,0:T(8,128)(2,1)S(1)} fusion(bf16[1024,512]{1,0:T(8,128)(2,1)} %constant_dynamic-update-slice_fusion.rest_0_, bf16[512,1152]{0,1:T(8,128)(2,1)S(1)} %collective-permute-done.28, bf16[512,288]{0,1:T(8,128)(2,1)S(1)} %get-tuple-element.190, bf16[512,288]{0,1:T(8,128)(2,1)S(1)} %get-tuple-element.191, ...), kind=kOutput, calls=%fused_computation.22 | convolution fusion | flops 1220345856 | bytes 4587520 | tf_op jit(solution)/shard_map/dot_general | solution.py:82
  545.2 10.3 %adam.7 = (f32[288,2304]{1,0:T(8,128)}, f32[288,2304]{1,0:T(8,128)}, f32[288,2304]{1,0:T(8,128)}, f32[288,2304]{1,0:T(8,128)}) custom-call(bf16[288,2304]{1,0:T(8,128)(2,1)} %get-tuple-element.107.refs_0_, bf16[288,2304]{1,0:T(8,128)(2,1)} %slice_bitcast_fusion.2.refs_1_, bf16[288,2304]{1,0:T(8,128)(2,1)} %collective-permute-done.22.rest_0_.refs_2_, ...), custom_call_target="tpu_custom_call" | custom-call | bytes 200000000 | tf_op jit(solution)/shard_map/adam/pallas_call | solution.py:919
  565.0 9.6 %join.1 = f32[288,2,2304]{2,1,0:T(2,128)} custom-call(bf16[288,2304]{1,0:T(8,128)(2,1)} %get-tuple-element.177.refs_0_, bf16[288,2304]{1,0:T(8,128)(2,1)} %slice_bitcast_fusion.1.refs_1_, bf16[288,2304]{1,0:T(8,128)(2,1)} %collective-permute-done.31.refs_2_, bf16[288,2304]{1,0:T(8,128)(2,1)} %get-tuple-element.174.refs_3_, ...), custom_call_target="tpu_custom_call" | custom-call | bytes 200000000 | tf_op jit(solution)/shard_map/join/pallas_call | solution.py:890
  574.6 14.4 %adam.6 = (f32[10368,128]{1,0:T(8,128)}, f32[10368,128]{1,0:T(8,128)}, f32[10368,128]{1,0:T(8,128)}) custom-call(f32[10368,128]{1,0:T(8,128)} %bitcast.203, f32[10368,128]{1,0:T(8,128)} %bitcast.204, f32[10368,128]{1,0:T(8,128)} %bitcast.212, f32[10368,128]{1,0:T(8,128)} %bitcast.213), custom_call_target="tpu_custom_call" | custom-call | bytes 200000000 | tf_op jit(solution)/shard_map/adam/pallas_call | solution.py:919
  591.5 4.5 adam.5
  600.9 5.2 adam.4
  608.0 7.5 %stream_back.1 = f32[512,2304]{1,0:T(8,128)} custom-call(bf16[512,2304]{1,0:T(8,128)(2,1)} %all-reduce.12.cloned.1.call-done.grad_in, bf16[512,2304]{1,0:T(8,128)(2,1)} %bitcast.202, f32[8,2304]{1,0:T(8,128)} %get-tuple-element.80.gains, f32[512,2304]{1,0:T(8,128)} %get-tuple-element.98.grad_mid, f32[288,1,1024]{2,1,0:T(1,128)} %bitcast.243, ...), custom_call_target="tpu_custom_call" | custom-call | flops 23592960 | bytes 14000000 | tf_op jit(solution)/shard_map/stream_back/pallas_call | solution.py:847
  (263 shorter events, 161.4 us)
Async XLA Ops:
  8.0 195.2 %all-reduce.6.cloned.1.call-start = ((), (), s32[]{:S(2)}) async-start(), calls=%async_computation | async-start | bytes 4718592 | tf_op jit(solution)/shard_map/psum | solution.py:101
  12.7 14.9 %collective-permute-start = (bf16[288,1664]{1,0:T(8,128)(2,1)S(1)}, bf16[288,1664]{1,0:T(8,128)(2,1)}, u32[]{:S(2)}, u32[]{:S(2)}) collective-permute-start(bf16[288,1664]{1,0:T(8,128)(2,1)S(1)} %pad_maximum_fusion.11), channel_id=1, source_target_pairs={{0,8},{4,20},{8,0},{12,28},{16,24},{20,4},{24,16},{28,12},{1,9},{5... | collective-permute-start | bytes 2875400 | tf_op jit(solution)/shard_map/ppermute | solution.py:118
  29.2 24.3 %collective-permute-start.1 = (bf16[2,288,1664]{2,1,0:T(8,128)(2,1)S(1)}, bf16[2,288,1664]{2,1,0:T(8,128)(2,1)}, u32[]{:S(2)}, u32[]{:S(2)}) collective-permute-start(bf16[2,288,1664]{2,1,0:T(8,128)(2,1)S(1)} %pad_maximum_fusion.7.one), channel_id=1, source_target_pairs={{0,16},{4,12},{8,24},{12,4},{16,0},{20,28},{24,8},{28,20},{1,17},{... | collective-permute-start | bytes 5750792 | tf_op jit(solution)/shard_map/ppermute | solution.py:118
  31.3 26.6 %collective-permute-start.2 = (bf16[2,288,1664]{2,1,0:T(8,128)(2,1)S(1)}, bf16[2,288,1664]{2,1,0:T(8,128)(2,1)}, u32[]{:S(2)}, u32[]{:S(2)}) collective-permute-start(bf16[2,288,1664]{2,1,0:T(8,128)(2,1)S(1)} %pad_maximum_fusion.7.one), channel_id=1, source_target_pairs={{0,4},{4,0},{1,5},{5,1},{2,6},{6,2},{3,7},{7,3},{8,12},{12,8},{9,1... | collective-permute-start | bytes 5750792 | tf_op jit(solution)/shard_map/ppermute | solution.py:106
  53.5 18.1 %collective-permute-start.5 = (bf16[288,2304]{1,0:T(8,128)(2,1)}, bf16[288,2304]{1,0:T(8,128)(2,1)}, u32[]{:S(2)}, u32[]{:S(2)}) collective-permute-start(bf16[288,2304]{1,0:T(8,128)(2,1)} %bitcast_convert_fusion), channel_id=1, source_target_pairs={{0,8},{4,20},{8,0},{12,28},{16,24},{20,4},{24,16},{28,12},{1,9},{5... | collective-permute-start | bytes 3981320 | tf_op jit(solution)/shard_map/ppermute | solution.py:118
  55.5 30.3 %collective-permute-start.6 = (bf16[288,2304]{1,0:T(8,128)(2,1)S(1)}, bf16[288,2304]{1,0:T(8,128)(2,1)}, u32[]{:S(2)}, u32[]{:S(2)}) collective-permute-start(bf16[288,2304]{1,0:T(8,128)(2,1)S(1)} %get-tuple-element.78), channel_id=1, source_target_pairs={{0,8},{4,20},{8,0},{12,28},{16,24},{20,4},{24,16},{28,12},{1,9},{5... | collective-permute-start | bytes 3981320 | tf_op jit(solution)/shard_map/ppermute | solution.py:118
  68.8 17.0 %collective-permute-start.4 = (bf16[2,512,256]{2,1,0:T(8,128)(2,1)}, bf16[2,512,256]{2,1,0:T(8,128)(2,1)S(1)}, u32[]{:S(2)}, u32[]{:S(2)}) collective-permute-start(bf16[2,512,256]{2,1,0:T(8,128)(2,1)} %get-tuple-element.76.pair), channel_id=1, source_target_pairs={{0,4},{1,5},{2,6},{3,7},{8,12},{9,13},{10,14},{11,15},{16,20},{17,... | collective-permute-start | bytes 1572872 | tf_op jit(solution)/shard_map/ppermute | solution.py:29
  94.3 114.2 %all-gather.2.cloned.1.call-start = ((), (), s32[]{:S(2)}) async-start(), calls=%async_computation.1 | async-start | bytes 11943936 | tf_op jit(solution)/shard_map/all_gather | solution.py:975
  94.9 243.6 %all-reduce.8.cloned.1.call-start = ((), (), s32[]{:S(2)}) async-start(), calls=%async_computation.2 | async-start | bytes 4718592 | tf_op jit(solution)/shard_map/psum | solution.py:101
  100.0 62.9 %collective-permute-start.11 = (bf16[2,288,2304]{2,1,0:T(8,128)(2,1)S(1)}, bf16[2,288,2304]{2,1,0:T(8,128)(2,1)S(1)}, u32[]{:S(2)}, u32[]{:S(2)}) collective-permute-start(bf16[2,288,2304]{2,1,0:T(8,128)(2,1)S(1)} %pad_maximum_fusion.1.rest_4_.one), channel_id=1, source_target_pairs={{0,16},{4,12},{8,24},{12,4},{16,0},{20,28},{24,8},{28,20},{1,17},{... | collective-permute-start | bytes 7962632 | tf_op jit(solution)/shard_map/ppermute | solution.py:118
  106.1 97.1 %collective-permute-start.9 = (bf16[2,288,2304]{2,1,0:T(8,128)(2,1)S(1)}, bf16[2,288,2304]{2,1,0:T(8,128)(2,1)}, u32[]{:S(2)}, u32[]{:S(2)}) collective-permute-start(bf16[2,288,2304]{2,1,0:T(8,128)(2,1)S(1)} %pad_maximum_fusion.rest_0_.one), channel_id=1, source_target_pairs={{0,16},{4,12},{8,24},{12,4},{16,0},{20,28},{24,8},{28,20},{1,17},{... | collective-permute-start | bytes 7962632 | tf_op jit(solution)/shard_map/ppermute | solution.py:118
  162.8 40.4 %collective-permute-start.12 = (bf16[2,288,2304]{2,1,0:T(8,128)(2,1)S(1)}, bf16[2,288,2304]{2,1,0:T(8,128)(2,1)}, u32[]{:S(2)}, u32[]{:S(2)}) collective-permute-start(bf16[2,288,2304]{2,1,0:T(8,128)(2,1)S(1)} %collective-permute-done.11.rest_5_.two), channel_id=1, source_target_pairs={{0,4},{4,0},{1,5},{5,1},{2,6},{6,2},{3,7},{7,3},{8,12},{12,8},{9,1... | collective-permute-start | bytes 7962632 | tf_op jit(solution)/shard_map/ppermute | solution.py:106
  233.3 68.2 %collective-permute-start.16 = (bf16[512,2304]{1,0:T(8,128)(2,1)}, bf16[512,2304]{1,0:T(8,128)(2,1)}, u32[]{:S(2)}, u32[]{:S(2)}) collective-permute-start(bf16[512,2304]{1,0:T(8,128)(2,1)} %get-tuple-element.88), channel_id=1, source_target_pairs={{0,4},{4,0},{1,5},{5,1},{2,6},{6,2},{3,7},{7,3},{8,12},{12,8},{9,1... | collective-permute-start | bytes 7077896 | tf_op jit(solution)/shard_map/ppermute | solution.py:106
  233.5 21.7 %collective-permute-start.13 = (bf16[512,512]{1,0:T(8,128)(2,1)}, bf16[512,512]{1,0:T(8,128)(2,1)}, u32[]{:S(2)}, u32[]{:S(2)}) collective-permute-start(bf16[512,512]{1,0:T(8,128)(2,1)} %get-tuple-element.83.attended), channel_id=1, source_target_pairs={{0,4},{4,0},{1,5},{5,1},{2,6},{6,2},{3,7},{7,3},{8,12},{12,8},{9,1... | collective-permute-start | bytes 1572872 | tf_op jit(solution)/shard_map/ppermute | solution.py:106
  241.0 224.2 %all-reduce.10.cloned.1.call-start = ((), (), s32[]{:S(2)}) async-start(), calls=%async_computation.3 | async-start | bytes 4718592 | tf_op jit(solution)/shard_map/psum | solution.py:101
  251.5 44.1 %collective-permute-start.15 = (bf16[512,1152]{1,0:T(8,128)(2,1)}, bf16[512,1152]{1,0:T(8,128)(2,1)}, u32[]{:S(2)}, u32[]{:S(2)}) collective-permute-start(bf16[512,1152]{1,0:T(8,128)(2,1)} %concatenate.87), channel_id=1, source_target_pairs={{0,4},{4,0},{1,5},{5,1},{2,6},{6,2},{3,7},{7,3},{8,12},{12,8},{9,1... | collective-permute-start | bytes 3538952 | tf_op jit(solution)/shard_map/ppermute | solution.py:106
  273.3 25.3 %collective-permute-start.14 = (bf16[512,1152]{1,0:T(8,128)(2,1)}, bf16[512,1152]{1,0:T(8,128)(2,1)}, u32[]{:S(2)}, u32[]{:S(2)}) collective-permute-start(bf16[512,1152]{1,0:T(8,128)(2,1)} %concatenate.84), channel_id=1, source_target_pairs={{0,4},{4,0},{1,5},{5,1},{2,6},{6,2},{3,7},{7,3},{8,12},{12,8},{9,1... | collective-permute-start | bytes 3538952 | tf_op jit(solution)/shard_map/ppermute | solution.py:106
  364.7 31.5 %collective-permute-start.19 = (bf16[512,2304]{1,0:T(8,128)(2,1)}, bf16[512,2304]{1,0:T(8,128)(2,1)}, u32[]{:S(2)}, u32[]{:S(2)}) collective-permute-start(bf16[512,2304]{1,0:T(8,128)(2,1)} %get-tuple-element.91), channel_id=1, source_target_pairs={{0,4},{4,0},{1,5},{5,1},{2,6},{6,2},{3,7},{7,3},{8,12},{12,8},{9,1... | collective-permute-start | bytes 7077896 | tf_op jit(solution)/shard_map/ppermute | solution.py:106
  370.3 237.6 %all-reduce.12.cloned.1.call-start = ((), (), s32[]{:S(2)}) async-start(), calls=%async_computation.4 | async-start | bytes 4718592 | tf_op jit(solution)/shard_map/psum | solution.py:101
  370.4 39.9 %collective-permute-start.23 = (bf16[512,2304]{1,0:T(8,128)(2,1)}, bf16[512,2304]{1,0:T(8,128)(2,1)S(1)}, u32[]{:S(2)}, u32[]{:S(2)}) collective-permute-start(bf16[512,2304]{1,0:T(8,128)(2,1)} %get-tuple-element.96), channel_id=1, source_target_pairs={{0,4},{4,0},{1,5},{5,1},{2,6},{6,2},{3,7},{7,3},{8,12},{12,8},{9,1... | collective-permute-start | bytes 7077896 | tf_op jit(solution)/shard_map/ppermute | solution.py:106
  394.8 32.1 %collective-permute-start.18 = (bf16[2,288,2304]{2,1,0:T(8,128)(2,1)S(1)}, bf16[2,288,2304]{2,1,0:T(8,128)(2,1)S(1)}, u32[]{:S(2)}, u32[]{:S(2)}) collective-permute-start(bf16[2,288,2304]{2,1,0:T(8,128)(2,1)S(1)} %pad_maximum_fusion.2), channel_id=1, source_target_pairs={{0,8},{4,20},{8,0},{12,28},{16,24},{20,4},{24,16},{28,12},{1,9},{5... | collective-permute-start | bytes 7962632 | tf_op jit(solution)/shard_map/ppermute | solution.py:118
  409.0 60.6 %collective-permute-start.20 = (bf16[2,288,2304]{2,1,0:T(8,128)(2,1)}, bf16[2,288,2304]{2,1,0:T(8,128)(2,1)}, u32[]{:S(2)}, u32[]{:S(2)}) collective-permute-start(bf16[2,288,2304]{2,1,0:T(8,128)(2,1)} %pad_maximum_fusion.3), channel_id=1, source_target_pairs={{0,8},{4,20},{8,0},{12,28},{16,24},{20,4},{24,16},{28,12},{1,9},{5... | collective-permute-start | bytes 7962632 | tf_op jit(solution)/shard_map/ppermute | solution.py:118
  422.5 76.3 %collective-permute-start.24 = (bf16[2,288,2304]{2,1,0:T(8,128)(2,1)}, bf16[2,288,2304]{2,1,0:T(8,128)(2,1)S(1)}, u32[]{:S(2)}, u32[]{:S(2)}) collective-permute-start(bf16[2,288,2304]{2,1,0:T(8,128)(2,1)} %pad_maximum_fusion.4), channel_id=1, source_target_pairs={{0,8},{4,20},{8,0},{12,28},{16,24},{20,4},{24,16},{28,12},{1,9},{5... | collective-permute-start | bytes 7962632 | tf_op jit(solution)/shard_map/ppermute | solution.py:118
  428.2 70.6 %collective-permute-start.22 = (bf16[288,2304]{1,0:T(8,128)(2,1)}, bf16[288,2304]{1,0:T(8,128)(2,1)}, u32[]{:S(2)}, u32[]{:S(2)}) collective-permute-start(bf16[288,2304]{1,0:T(8,128)(2,1)} %fusion.15.rest_0_), channel_id=1, source_target_pairs={{0,16},{4,12},{8,24},{12,4},{16,0},{20,28},{24,8},{28,20},{1,17},{... | collective-permute-start | bytes 3981320 | tf_op jit(solution)/shard_map/ppermute | solution.py:118
  495.1 68.8 %collective-permute-start.31 = (bf16[288,2304]{1,0:T(8,128)(2,1)}, bf16[288,2304]{1,0:T(8,128)(2,1)}, u32[]{:S(2)}, u32[]{:S(2)}) collective-permute-start(bf16[288,2304]{1,0:T(8,128)(2,1)} %fusion.14), channel_id=1, source_target_pairs={{0,16},{4,12},{8,24},{12,4},{16,0},{20,28},{24,8},{28,20},{1,17},{... | collective-permute-start | bytes 3981320 | tf_op jit(solution)/shard_map/ppermute | solution.py:118
  518.9 13.4 %collective-permute-start.28 = (bf16[512,1152]{0,1:T(8,128)(2,1)S(1)}, bf16[512,1152]{0,1:T(8,128)(2,1)S(1)}, u32[]{:S(2)}, u32[]{:S(2)}) collective-permute-start(bf16[512,1152]{0,1:T(8,128)(2,1)S(1)} %pad_maximum_fusion.10), channel_id=1, source_target_pairs={{0,4},{4,0},{1,5},{5,1},{2,6},{6,2},{3,7},{7,3},{8,12},{12,8},{9,1... | collective-permute-start | bytes 3538952 | tf_op jit(solution)/shard_map/ppermute | solution.py:106
  525.1 38.9 %collective-permute-start.32 = (bf16[288,2304]{1,0:T(8,128)(2,1)S(1)}, bf16[288,2304]{1,0:T(8,128)(2,1)S(1)}, u32[]{:S(2)}, u32[]{:S(2)}) collective-permute-start(bf16[288,2304]{1,0:T(8,128)(2,1)S(1)} %fusion.13), channel_id=1, source_target_pairs={{0,16},{4,12},{8,24},{12,4},{16,0},{20,28},{24,8},{28,20},{1,17},{... | collective-permute-start | bytes 3981320 | tf_op jit(solution)/shard_map/ppermute | solution.py:118
  525.9 29.7 %collective-permute-start.36 = (f32[4,2304]{1,0:T(4,128)S(1)}, f32[4,2304]{1,0:T(4,128)S(1)}, u32[]{:S(2)}, u32[]{:S(2)}) collective-permute-start(f32[4,2304]{1,0:T(4,128)S(1)} %add.247), channel_id=1, source_target_pairs={{0,1},{1,0},{2,3},{3,2},{4,5},{5,4},{6,7},{7,6},{8,9},{9,8},{10,11... | collective-permute-start | bytes 110600 | tf_op jit(solution)/shard_map/ppermute | solution.py:106
  531.4 25.9 %collective-permute-start.26 = (bf16[2,288,1024]{2,1,0:T(8,128)(2,1)}, bf16[2,288,1024]{2,1,0:T(8,128)(2,1)S(1)}, u32[]{:S(2)}, u32[]{:S(2)}) collective-permute-start(bf16[2,288,1024]{2,1,0:T(8,128)(2,1)} %pad_maximum_fusion.9), channel_id=1, source_target_pairs={{0,8},{4,20},{8,0},{12,28},{16,24},{20,4},{24,16},{28,12},{1,9},{5... | collective-permute-start | bytes 3538952 | tf_op jit(solution)/shard_map/ppermute | solution.py:118
  543.0 19.1 %collective-permute-start.29 = (bf16[2,288,512]{2,1,0:T(8,128)(2,1)}, bf16[2,288,512]{2,1,0:T(8,128)(2,1)}, u32[]{:S(2)}, u32[]{:S(2)}) collective-permute-start(bf16[2,288,512]{2,1,0:T(8,128)(2,1)} %pad_maximum_fusion.12), channel_id=1, source_target_pairs={{0,8},{4,20},{8,0},{12,28},{16,24},{20,4},{24,16},{28,12},{1,9},{5... | collective-permute-start | bytes 1769480 | tf_op jit(solution)/shard_map/ppermute | solution.py:118
  557.5 38.6 %collective-permute-start.27 = (bf16[288,1024]{1,0:T(8,128)(2,1)S(1)}, bf16[288,1024]{1,0:T(8,128)(2,1)}, u32[]{:S(2)}, u32[]{:S(2)}) collective-permute-start(bf16[288,1024]{1,0:T(8,128)(2,1)S(1)} %fusion.38), channel_id=1, source_target_pairs={{0,16},{4,12},{8,24},{12,4},{16,0},{20,28},{24,8},{28,20},{1,17},{... | collective-permute-start | bytes 1769480 | tf_op jit(solution)/shard_map/ppermute | solution.py:118
  563.1 27.6 %collective-permute-start.30 = (bf16[288,512]{1,0:T(8,128)(2,1)S(1)}, bf16[288,512]{1,0:T(8,128)(2,1)S(1)}, u32[]{:S(2)}, u32[]{:S(2)}) collective-permute-start(bf16[288,512]{1,0:T(8,128)(2,1)S(1)} %fusion.40), channel_id=1, source_target_pairs={{0,16},{4,12},{8,24},{12,4},{16,0},{20,28},{24,8},{28,20},{1,17},{... | collective-permute-start | bytes 884744 | tf_op jit(solution)/shard_map/ppermute | solution.py:118
  (58 other events, 658.8 us)
Sparse Core Ops, SparseCore 0:
  94.5 97.3 all-reduce.5
  241.1 97.3 all-reduce.7
  370.4 94.6 all-reduce.9
  512.5 95.4 all-reduce.11
Sparse Core Ops, SparseCore 1:
  97.3 86.9 all-gather.1

commit v5 on v4

--- a/solution.py
+++ b/solution.py
@@ -981,7 +981,7 @@
     )
     behind = from_behind(pair, "seq", 1)
     attended, attn_part = attend(
-        place, queries, pair, behind, near, far, stream.shape[1], down_one, gate_one
+        place, queries, pair, behind, near, far, stream.shape[1], down_one
     )
     attn_out = tensor_sum(attn_part)
     ffn_in, hidden, by_gate, by_up, ffn_part = ffn_forward(

time: 631 us -> 627 us (level)
  transfers between devices with their start and end apart: 43 -> 43, of which waited for: 17 -> 17; matrix products, arithmetic and copies ran while one was open for 25% -> 24% of each run, Pallas kernels for 17% -> 17%
where the time goes in v5:
time: 627 us; the launch traced here: 619 us
  waiting for transfers between devices  231 us (37%)
  Pallas kernels  170 us (27%)
  local copies, waits for them, and re-layouts  80.9 us (13%)
  matrix products  43.9 us (7%)
  other arithmetic  41.2 us (7%)
  starting transfers between devices  34.4 us (5%)
  between operations  16.7 us (3%)
    ppermute x16, waiting for transfers between devices, trade(): return lax.ppermute(value, ('batch', 'seq'), pairs)  148 us
    psum x4, waiting for transfers between devices, tensor_sum(): return lax.psum(part, 'tensor')  70 us
    dot_general x5, matrix products, rows_product(): lax.dot_general(left, right, (((0,), (0,)), ((), ())), preferred_element_...  43.9 us
    pallas_call x4, Pallas kernels, adam(): pl.pallas_call(functools.partial(adam_kernel, len(grads), decay), grid=(s...  34.5 us
    pallas_call x1, Pallas kernels, ffn_back(): pl.pallas_call(ffn_back_kernel, in_specs=[spec_vmem()] * 3 + [spec_any()]...  26.1 us
    pallas_call x1, Pallas kernels, ffn_forward(): pl.pallas_call(ffn_kernel, in_specs=[spec_smem()] + [spec_vmem()] * 3 + [...  24.7 us
    ppermute x16, starting transfers between devices, trade(): return lax.ppermute(value, ('batch', 'seq'), pairs)  21.4 us
    unnamed x100, local copies, waits for them, and re-layouts  20.3 us
  transfers between devices with their start and end apart: 43, of which 17 were waited for; matrix products, arithmetic and copies ran while one was open for 24% of the time, Pallas kernels for 17%

profile of v5, /device:TPU:0, one launch (start us, length us, event | category | flops | bytes accessed | tf_op | source)
XLA Modules:
  0.0 618.6 jit_solution(5371995426555535482)
XLA Ops:
  19.8 7.9 %collective-permute-done = bf16[288,1664]{1,0:T(8,128)(2,1)} collective-permute-done((bf16[288,1664]{1,0:T(8,128)(2,1)S(1)}, bf16[288,1664]{1,0:T(8,128)(2,1)}, u32[]{:S(2)}, u32[]{:S(2)}) %collective-permute-start) | collective-permute-done | bytes 958496 | tf_op jit(solution)/shard_map/ppermute | solution.py:118
  31.3 22.2 %collective-permute-done.1.two = bf16[2,288,1664]{2,1,0:T(8,128)(2,1)} collective-permute-done((bf16[2,288,1664]{2,1,0:T(8,128)(2,1)S(1)}, bf16[2,288,1664]{2,1,0:T(8,128)(2,1)}, u32[]{:S(2)}, u32[]{:S(2)}) %collective-permute-start.1) | collective-permute-done | bytes 1916960 | tf_op jit(solution)/shard_map/ppermute | solution.py:118
  57.9 10.8 %project.1 = (bf16[512,512]{1,0:T(8,128)(2,1)}, bf16[2,512,256]{2,1,0:T(8,128)(2,1)}, bf16[512,2304]{1,0:T(8,128)(2,1)}, f32[8,2304]{1,0:T(8,128)}) custom-call(s32[2]{0:T(128)} %pad_add_fusion.place, bf16[512,2304]{1,0:T(8,128)(2,1)} %bitcast.198, bf16[2,288,1664]{2,1,0:T(8,128)(2,1)} %copy-done.1, bf16[2,288,1664]{2,1,0:T(8,128)(2,1)} %collective-permute-done.1.two, ...), custom_call_target="tpu_custom_call" | custom-call | flops 2415919104 | bytes 12000000 | tf_op jit(solution)/shard_map/project/pallas_call | solution.py:314
  73.4 7.7 %attend.1 = (bf16[512,512]{1,0:T(8,128)(2,1)}, bf16[512,2304]{1,0:T(8,128)(2,1)}) custom-call(s32[2]{0:T(128)} %pad_add_fusion.place, bf16[512,512]{1,0:T(8,128)(2,1)} %get-tuple-element.75.queries, bf16[2,512,256]{2,1,0:T(8,128)(2,1)} %get-tuple-element.76.pair, bf16[2,512,256]{2,1,0:T(8,128)(2,1)} %copy-done.46, bf16[2,288,1664]{2,1,0:T(8,128)(2,1)} %copy-done.1, ...), custom_call_target="tpu_custom_call" | custom-call | flops 4831838208 | bytes 8000000 | tf_op jit(solution)/shard_map/attend/pallas_call | solution.py:379
  85.6 23.1 %collective-permute-done.6 = bf16[288,2304]{1,0:T(8,128)(2,1)S(1)} collective-permute-done((bf16[288,2304]{1,0:T(8,128)(2,1)S(1)}, bf16[288,2304]{1,0:T(8,128)(2,1)S(1)}, u32[]{:S(2)}, u32[]{:S(2)}) %collective-permute-start.6) | collective-permute-done | bytes 1327136 | tf_op jit(solution)/shard_map/ppermute | solution.py:118
  115.2 55.2 %collective-permute-done.11.rest_5_.two = bf16[2,288,2304]{2,1,0:T(8,128)(2,1)S(1)} collective-permute-done((bf16[2,288,2304]{2,1,0:T(8,128)(2,1)S(1)}, bf16[2,288,2304]{2,1,0:T(8,128)(2,1)S(1)}, u32[]{:S(2)}, u32[]{:S(2)}) %collective-permute-start.11) | collective-permute-done | bytes 2654240 | tf_op jit(solution)/shard_map/ppermute | solution.py:118
  171.2 27.7 %collective-permute-done.9.rest_1_.two = bf16[2,288,2304]{2,1,0:T(8,128)(2,1)} collective-permute-done((bf16[2,288,2304]{2,1,0:T(8,128)(2,1)S(1)}, bf16[2,288,2304]{2,1,0:T(8,128)(2,1)}, u32[]{:S(2)}, u32[]{:S(2)}) %collective-permute-start.9) | collective-permute-done | bytes 2654240 | tf_op jit(solution)/shard_map/ppermute | solution.py:118
  199.4 4.9 collective-permute-done.10.rest_3_.two_far
  204.2 24.7 %ffn_forward.1 = (bf16[512,2304]{1,0:T(8,128)(2,1)}, bf16[512,2304]{1,0:T(8,128)(2,1)}, bf16[512,2304]{1,0:T(8,128)(2,1)}, bf16[512,2304]{1,0:T(8,128)(2,1)}, bf16[512,2304]{1,0:T(8,128)(2,1)}) custom-call(s32[2]{0:T(128)} %pad_add_fusion.place, bf16[512,2304]{1,0:T(8,128)(2,1)} %all-reduce.6.cloned.1.call-done.attn_out, bf16[512,2304]{1,0:T(8,128)(2,1)} %bitcast.199, ...), custom_call_target="tpu_custom_call" | custom-call | flops 16307453952 | bytes 50000000 | tf_op jit(solution)/shard_map/ffn_forward/pallas_call | solution.py:492
  232.4 4.3 copy.73
  253.0 8.8 %arrange.3.down = bf16[2304,2304]{1,0:T(8,128)(2,1)} custom-call(s32[2]{0:T(128)} %pad_add_fusion.place, bf16[2,288,2304]{2,1,0:T(8,128)(2,1)} %copy-done.6, bf16[2,288,2304]{2,1,0:T(8,128)(2,1)} %copy-done.20, bf16[2,288,2304]{2,1,0:T(8,128)(2,1)} %copy-done.19, bf16[2,288,2304]{2,1,0:T(8,128)(2,1)} %collective-permute-done.12.rest_7_.two_far), custom_call_target="tpu_custom_call" | custom-call | bytes 21233664 | tf_op jit(solution)/shard_map/arrange/pallas_call | solution.py:269
  265.4 3.9 concatenate.84
  270.0 8.8 %arrange.2.gate = bf16[2304,2304]{1,0:T(8,128)(2,1)} custom-call(s32[2]{0:T(128)} %pad_add_fusion.place, bf16[2,288,2304]{2,1,0:T(8,128)(2,1)} %copy-done.5, bf16[2,288,2304]{2,1,0:T(8,128)(2,1)} %collective-permute-done.9.rest_1_.two, bf16[2,288,2304]{2,1,0:T(8,128)(2,1)} %copy-done.18, bf16[2,288,2304]{2,1,0:T(8,128)(2,1)} %collective-permute-done.10.rest_3_.two_far), custom_call_target="tpu_custom_call" | custom-call | bytes 21233664 | tf_op jit(solution)/shard_map/arrange/pallas_call | solution.py:269
  300.4 33.6 %all-reduce.8.cloned.1.call-done.ffn_out = bf16[512,2304]{1,0:T(8,128)(2,1)} async-done(((bf16[512,2304]{1,0:T(8,128)(2,1)}), bf16[512,2304]{1,0:T(8,128)(2,1)}) %all-reduce.8.cloned.1.call-update) | async-done | bytes 2359312 | tf_op jit(solution)/shard_map/psum | solution.py:101
  334.1 26.1 %ffn_back.1 = (bf16[512,2304]{1,0:T(8,128)(2,1)}, bf16[512,2304]{1,0:T(8,128)(2,1)}, bf16[512,2304]{1,0:T(8,128)(2,1)}, f32[8,2304]{1,0:T(8,128)}, bf16[512,2304]{1,0:T(8,128)(2,1)}) custom-call(bf16[512,2304]{1,0:T(8,128)(2,1)} %all-reduce.8.cloned.1.call-done.ffn_out, bf16[512,2304]{1,0:T(8,128)(2,1)} %bitcast.225, f32[8,2304]{1,0:T(8,128)} %get-tuple-element.79.gains, ...), custom_call_target="tpu_custom_call" | custom-call | flops 16307453952 | bytes 55000000 | tf_op jit(solution)/shard_map/ffn_back/pallas_call | solution.py:615
  369.0 5.0 fusion.16
  374.0 14.7 %convolution_convert_fusion.2 = bf16[1152,2304]{1,0:T(8,128)(2,1)S(1)} fusion(bf16[1024,2304]{1,0:T(8,128)(2,1)} %constant_dynamic-update-slice_fusion.2.rest_3_, bf16[512,1152]{0,1:T(8,128)(2,1)} %collective-permute-done.17, bf16[512,288]{0,1:T(8,128)(2,1)S(1)} %copy-done.35, bf16[512,288]{0,1:T(8,128)(2,1)S(1)} %copy-done.36, ...), kind=kOutput, calls=%fused_computation.2 | convolution fusion | flops 5450268672 | bytes 12386304 | tf_op jit(solution)/shard_map/dot_general | solution.py:82
  391.8 8.2 %convolution_convert_fusion.1 = bf16[1152,2304]{1,0:T(8,128)(2,1)S(1)} fusion(bf16[512,2304]{1,0:T(8,128)(2,1)} %collective-permute-done.19, bf16[512,2304]{1,0:T(8,128)(2,1)S(1)} %copy-done.44, bf16[512,1152]{1,0:T(8,128)(2,1)} %collective-permute-done.15, bf16[512,1152]{1,0:T(8,128)(2,1)S(1)} %concatenate.86), kind=kOutput, calls=%fused_computation.1 | convolution fusion | flops 5452627968 | bytes 12386304 | tf_op jit(solution)/shard_map/dot_general | solution.py:82
  405.8 7.7 %convolution_convert_fusion = bf16[1152,2304]{1,0:T(8,128)(2,1)S(1)} fusion(bf16[512,2304]{1,0:T(8,128)(2,1)S(1)} %collective-permute-done.23, bf16[512,2304]{1,0:T(8,128)(2,1)S(1)} %copy-done.43, bf16[512,1152]{1,0:T(8,128)(2,1)} %collective-permute-done.15, bf16[512,1152]{1,0:T(8,128)(2,1)S(1)} %concatenate.86), kind=kOutput, calls=%fused_computation | convolution fusion | flops 5452627968 | bytes 12386304 | tf_op jit(solution)/shard_map/dot_general | solution.py:82
  426.2 34.5 %all-reduce.10.cloned.1.call-done.grad_in = bf16[512,2304]{1,0:T(8,128)(2,1)} async-done(((bf16[512,2304]{1,0:T(8,128)(2,1)}), bf16[512,2304]{1,0:T(8,128)(2,1)}) %all-reduce.10.cloned.1.call-update) | async-done | bytes 2359312 | tf_op jit(solution)/shard_map/psum | solution.py:101
  460.7 4.5 collective-permute-done.20.rest_1_
  465.1 11.5 %mid_back.1 = (f32[512,2304]{1,0:T(8,128)}, bf16[512,2304]{1,0:T(8,128)(2,1)}, bf16[512,512]{1,0:T(8,128)(2,1)}, f32[2,8,2304]{2,1,0:T(8,128)}) custom-call(s32[2]{0:T(128)} %pad_add_fusion.place, bf16[512,2304]{1,0:T(8,128)(2,1)} %all-reduce.10.cloned.1.call-done.grad_in, bf16[512,2304]{1,0:T(8,128)(2,1)} %bitcast.200, ...), custom_call_target="tpu_custom_call" | custom-call | flops 1207959552 | bytes 24000000 | tf_op jit(solution)/shard_map/mid_back/pallas_call | solution.py:686
  476.6 9.6 %attend_back.1 = (bf16[512,512]{1,0:T(8,128)(2,1)}, f32[2,512,256]{2,1,0:T(8,128)}, bf16[2,512,256]{2,1,0:T(8,128)(2,1)}) custom-call(s32[2]{0:T(128)} %pad_add_fusion.place, bf16[512,512]{1,0:T(8,128)(2,1)} %get-tuple-element.75.queries, bf16[2,512,256]{2,1,0:T(8,128)(2,1)} %get-tuple-element.76.pair, bf16[2,512,256]{2,1,0:T(8,128)(2,1)} %copy-done.46, ...), custom_call_target="tpu_custom_call" | custom-call | flops 5368709120 | bytes 5000000 | tf_op jit(solution)/shard_map/attend_back/pallas_call | solution.py:759
  496.1 10.8 %project_back.1 = (bf16[512,1024]{1,0:T(8,128)(2,1)}, bf16[512,2304]{1,0:T(8,128)(2,1)}, f32[8,2304]{1,0:T(8,128)}) custom-call(s32[2]{0:T(128)} %pad_add_fusion.place, bf16[512,512]{1,0:T(8,128)(2,1)} %get-tuple-element.93.grad_q, f32[2,512,256]{2,1,0:T(8,128)} %get-tuple-element.94.grad_own, bf16[2,512,256]{2,1,0:T(8,128)(2,1)} %copy-done.32, ...), custom_call_target="tpu_custom_call" | custom-call | flops 2415919104 | bytes 14000000 | tf_op jit(solution)/shard_map/project_back/pallas_call | solution.py:811
  521.5 4.2 convolution_convert_fusion.3
  527.9 9.0 %convolution_convert_fusion.4 = bf16[1152,512]{1,0:T(8,128)(2,1)S(1)} fusion(bf16[1024,512]{1,0:T(8,128)(2,1)} %constant_dynamic-update-slice_fusion.rest_0_, bf16[512,1152]{0,1:T(8,128)(2,1)S(1)} %collective-permute-done.28, bf16[512,288]{0,1:T(8,128)(2,1)S(1)} %get-tuple-element.190, bf16[512,288]{0,1:T(8,128)(2,1)S(1)} %get-tuple-element.191, ...), kind=kOutput, calls=%fused_computation.22 | convolution fusion | flops 1220345856 | bytes 4587520 | tf_op jit(solution)/shard_map/dot_general | solution.py:82
  540.7 10.3 %adam.7 = (f32[288,2304]{1,0:T(8,128)}, f32[288,2304]{1,0:T(8,128)}, f32[288,2304]{1,0:T(8,128)}, f32[288,2304]{1,0:T(8,128)}) custom-call(bf16[288,2304]{1,0:T(8,128)(2,1)} %get-tuple-element.107.refs_0_, bf16[288,2304]{1,0:T(8,128)(2,1)} %slice_bitcast_fusion.2.refs_1_, bf16[288,2304]{1,0:T(8,128)(2,1)} %collective-permute-done.22.rest_0_.refs_2_, ...), custom_call_target="tpu_custom_call" | custom-call | bytes 200000000 | tf_op jit(solution)/shard_map/adam/pallas_call | solution.py:919
  560.6 9.6 %join.1 = f32[288,2,2304]{2,1,0:T(2,128)} custom-call(bf16[288,2304]{1,0:T(8,128)(2,1)} %get-tuple-element.177.refs_0_, bf16[288,2304]{1,0:T(8,128)(2,1)} %slice_bitcast_fusion.1.refs_1_, bf16[288,2304]{1,0:T(8,128)(2,1)} %collective-permute-done.31.refs_2_, bf16[288,2304]{1,0:T(8,128)(2,1)} %get-tuple-element.174.refs_3_, ...), custom_call_target="tpu_custom_call" | custom-call | bytes 200000000 | tf_op jit(solution)/shard_map/join/pallas_call | solution.py:890
  570.2 14.4 %adam.6 = (f32[10368,128]{1,0:T(8,128)}, f32[10368,128]{1,0:T(8,128)}, f32[10368,128]{1,0:T(8,128)}) custom-call(f32[10368,128]{1,0:T(8,128)} %bitcast.203, f32[10368,128]{1,0:T(8,128)} %bitcast.204, f32[10368,128]{1,0:T(8,128)} %bitcast.212, f32[10368,128]{1,0:T(8,128)} %bitcast.213), custom_call_target="tpu_custom_call" | custom-call | bytes 200000000 | tf_op jit(solution)/shard_map/adam/pallas_call | solution.py:919
  587.0 4.5 adam.5
  596.5 5.2 adam.4
  603.5 7.5 %stream_back.1 = f32[512,2304]{1,0:T(8,128)} custom-call(bf16[512,2304]{1,0:T(8,128)(2,1)} %all-reduce.12.cloned.1.call-done.grad_in, bf16[512,2304]{1,0:T(8,128)(2,1)} %bitcast.202, f32[8,2304]{1,0:T(8,128)} %get-tuple-element.79.gains, f32[512,2304]{1,0:T(8,128)} %get-tuple-element.98.grad_mid, f32[288,1,1024]{2,1,0:T(1,128)} %bitcast.244, ...), custom_call_target="tpu_custom_call" | custom-call | flops 23592960 | bytes 14000000 | tf_op jit(solution)/shard_map/stream_back/pallas_call | solution.py:847
  (263 shorter events, 160.8 us)
Async XLA Ops:
  8.0 191.3 %all-reduce.6.cloned.1.call-start = ((), (), s32[]{:S(2)}) async-start(), calls=%async_computation | async-start | bytes 4718592 | tf_op jit(solution)/shard_map/psum | solution.py:101
  12.7 14.9 %collective-permute-start = (bf16[288,1664]{1,0:T(8,128)(2,1)S(1)}, bf16[288,1664]{1,0:T(8,128)(2,1)}, u32[]{:S(2)}, u32[]{:S(2)}) collective-permute-start(bf16[288,1664]{1,0:T(8,128)(2,1)S(1)} %pad_maximum_fusion.11), channel_id=1, source_target_pairs={{0,8},{4,20},{8,0},{12,28},{16,24},{20,4},{24,16},{28,12},{1,9},{5... | collective-permute-start | bytes 2875400 | tf_op jit(solution)/shard_map/ppermute | solution.py:118
  29.2 24.3 %collective-permute-start.1 = (bf16[2,288,1664]{2,1,0:T(8,128)(2,1)S(1)}, bf16[2,288,1664]{2,1,0:T(8,128)(2,1)}, u32[]{:S(2)}, u32[]{:S(2)}) collective-permute-start(bf16[2,288,1664]{2,1,0:T(8,128)(2,1)S(1)} %pad_maximum_fusion.7.one), channel_id=1, source_target_pairs={{0,16},{4,12},{8,24},{12,4},{16,0},{20,28},{24,8},{28,20},{1,17},{... | collective-permute-start | bytes 5750792 | tf_op jit(solution)/shard_map/ppermute | solution.py:118
  31.3 26.6 %collective-permute-start.2 = (bf16[2,288,1664]{2,1,0:T(8,128)(2,1)S(1)}, bf16[2,288,1664]{2,1,0:T(8,128)(2,1)}, u32[]{:S(2)}, u32[]{:S(2)}) collective-permute-start(bf16[2,288,1664]{2,1,0:T(8,128)(2,1)S(1)} %pad_maximum_fusion.7.one), channel_id=1, source_target_pairs={{0,4},{4,0},{1,5},{5,1},{2,6},{6,2},{3,7},{7,3},{8,12},{12,8},{9,1... | collective-permute-start | bytes 5750792 | tf_op jit(solution)/shard_map/ppermute | solution.py:106
  53.5 18.1 %collective-permute-start.5 = (bf16[288,2304]{1,0:T(8,128)(2,1)}, bf16[288,2304]{1,0:T(8,128)(2,1)}, u32[]{:S(2)}, u32[]{:S(2)}) collective-permute-start(bf16[288,2304]{1,0:T(8,128)(2,1)} %bitcast_convert_fusion), channel_id=1, source_target_pairs={{0,8},{4,20},{8,0},{12,28},{16,24},{20,4},{24,16},{28,12},{1,9},{5... | collective-permute-start | bytes 3981320 | tf_op jit(solution)/shard_map/ppermute | solution.py:118
  81.1 123.1 %all-gather.2.cloned.1.call-start = ((), (), s32[]{:S(2)}) async-start(), calls=%async_computation.1 | async-start | bytes 11943936 | tf_op jit(solution)/shard_map/all_gather | solution.py:975
  81.7 252.3 %all-reduce.8.cloned.1.call-start = ((), (), s32[]{:S(2)}) async-start(), calls=%async_computation.2 | async-start | bytes 4718592 | tf_op jit(solution)/shard_map/psum | solution.py:101
  82.0 26.7 %collective-permute-start.6 = (bf16[288,2304]{1,0:T(8,128)(2,1)S(1)}, bf16[288,2304]{1,0:T(8,128)(2,1)S(1)}, u32[]{:S(2)}, u32[]{:S(2)}) collective-permute-start(bf16[288,2304]{1,0:T(8,128)(2,1)S(1)} %get-tuple-element.80), channel_id=1, source_target_pairs={{0,8},{4,20},{8,0},{12,28},{16,24},{20,4},{24,16},{28,12},{1,9},{5... | collective-permute-start | bytes 3981320 | tf_op jit(solution)/shard_map/ppermute | solution.py:118
  85.5 24.8 %collective-permute-start.7 = (bf16[2,288,2304]{2,1,0:T(8,128)(2,1)S(1)}, bf16[2,288,2304]{2,1,0:T(8,128)(2,1)S(1)}, u32[]{:S(2)}, u32[]{:S(2)}) collective-permute-start(bf16[2,288,2304]{2,1,0:T(8,128)(2,1)S(1)} %pad_maximum_fusion.1.rest_4_.one), channel_id=1, source_target_pairs={{0,4},{4,0},{1,5},{5,1},{2,6},{6,2},{3,7},{7,3},{8,12},{12,8},{9,1... | collective-permute-start | bytes 7962632 | tf_op jit(solution)/shard_map/ppermute | solution.py:106
  109.1 61.3 %collective-permute-start.11 = (bf16[2,288,2304]{2,1,0:T(8,128)(2,1)S(1)}, bf16[2,288,2304]{2,1,0:T(8,128)(2,1)S(1)}, u32[]{:S(2)}, u32[]{:S(2)}) collective-permute-start(bf16[2,288,2304]{2,1,0:T(8,128)(2,1)S(1)} %pad_maximum_fusion.1.rest_4_.one), channel_id=1, source_target_pairs={{0,16},{4,12},{8,24},{12,4},{16,0},{20,28},{24,8},{28,20},{1,17},{... | collective-permute-start | bytes 7962632 | tf_op jit(solution)/shard_map/ppermute | solution.py:118
  114.0 84.9 %collective-permute-start.9 = (bf16[2,288,2304]{2,1,0:T(8,128)(2,1)S(1)}, bf16[2,288,2304]{2,1,0:T(8,128)(2,1)}, u32[]{:S(2)}, u32[]{:S(2)}) collective-permute-start(bf16[2,288,2304]{2,1,0:T(8,128)(2,1)S(1)} %pad_maximum_fusion.rest_0_.one), channel_id=1, source_target_pairs={{0,16},{4,12},{8,24},{12,4},{16,0},{20,28},{24,8},{28,20},{1,17},{... | collective-permute-start | bytes 7962632 | tf_op jit(solution)/shard_map/ppermute | solution.py:118
  170.3 29.0 %collective-permute-start.12 = (bf16[2,288,2304]{2,1,0:T(8,128)(2,1)S(1)}, bf16[2,288,2304]{2,1,0:T(8,128)(2,1)}, u32[]{:S(2)}, u32[]{:S(2)}) collective-permute-start(bf16[2,288,2304]{2,1,0:T(8,128)(2,1)S(1)} %collective-permute-done.11.rest_5_.two), channel_id=1, source_target_pairs={{0,4},{4,0},{1,5},{5,1},{2,6},{6,2},{3,7},{7,3},{8,12},{12,8},{9,1... | collective-permute-start | bytes 7962632 | tf_op jit(solution)/shard_map/ppermute | solution.py:106
  229.0 68.2 %collective-permute-start.16 = (bf16[512,2304]{1,0:T(8,128)(2,1)}, bf16[512,2304]{1,0:T(8,128)(2,1)}, u32[]{:S(2)}, u32[]{:S(2)}) collective-permute-start(bf16[512,2304]{1,0:T(8,128)(2,1)} %get-tuple-element.88), channel_id=1, source_target_pairs={{0,4},{4,0},{1,5},{5,1},{2,6},{6,2},{3,7},{7,3},{8,12},{12,8},{9,1... | collective-permute-start | bytes 7077896 | tf_op jit(solution)/shard_map/ppermute | solution.py:106
  229.4 21.7 %collective-permute-start.13 = (bf16[512,512]{1,0:T(8,128)(2,1)}, bf16[512,512]{1,0:T(8,128)(2,1)}, u32[]{:S(2)}, u32[]{:S(2)}) collective-permute-start(bf16[512,512]{1,0:T(8,128)(2,1)} %get-tuple-element.83.attended), channel_id=1, source_target_pairs={{0,4},{4,0},{1,5},{5,1},{2,6},{6,2},{3,7},{7,3},{8,12},{12,8},{9,1... | collective-permute-start | bytes 1572872 | tf_op jit(solution)/shard_map/ppermute | solution.py:106
  236.7 224.0 %all-reduce.10.cloned.1.call-start = ((), (), s32[]{:S(2)}) async-start(), calls=%async_computation.3 | async-start | bytes 4718592 | tf_op jit(solution)/shard_map/psum | solution.py:101
  247.3 44.1 %collective-permute-start.15 = (bf16[512,1152]{1,0:T(8,128)(2,1)}, bf16[512,1152]{1,0:T(8,128)(2,1)}, u32[]{:S(2)}, u32[]{:S(2)}) collective-permute-start(bf16[512,1152]{1,0:T(8,128)(2,1)} %concatenate.87), channel_id=1, source_target_pairs={{0,4},{4,0},{1,5},{5,1},{2,6},{6,2},{3,7},{7,3},{8,12},{12,8},{9,1... | collective-permute-start | bytes 3538952 | tf_op jit(solution)/shard_map/ppermute | solution.py:106
  269.3 25.0 %collective-permute-start.14 = (bf16[512,1152]{1,0:T(8,128)(2,1)}, bf16[512,1152]{1,0:T(8,128)(2,1)}, u32[]{:S(2)}, u32[]{:S(2)}) collective-permute-start(bf16[512,1152]{1,0:T(8,128)(2,1)} %concatenate.84), channel_id=1, source_target_pairs={{0,4},{4,0},{1,5},{5,1},{2,6},{6,2},{3,7},{7,3},{8,12},{12,8},{9,1... | collective-permute-start | bytes 3538952 | tf_op jit(solution)/shard_map/ppermute | solution.py:106
  360.2 31.5 %collective-permute-start.19 = (bf16[512,2304]{1,0:T(8,128)(2,1)}, bf16[512,2304]{1,0:T(8,128)(2,1)}, u32[]{:S(2)}, u32[]{:S(2)}) collective-permute-start(bf16[512,2304]{1,0:T(8,128)(2,1)} %get-tuple-element.91), channel_id=1, source_target_pairs={{0,4},{4,0},{1,5},{5,1},{2,6},{6,2},{3,7},{7,3},{8,12},{12,8},{9,1... | collective-permute-start | bytes 7077896 | tf_op jit(solution)/shard_map/ppermute | solution.py:106
  365.9 237.6 %all-reduce.12.cloned.1.call-start = ((), (), s32[]{:S(2)}) async-start(), calls=%async_computation.4 | async-start | bytes 4718592 | tf_op jit(solution)/shard_map/psum | solution.py:101
  365.9 39.9 %collective-permute-start.23 = (bf16[512,2304]{1,0:T(8,128)(2,1)}, bf16[512,2304]{1,0:T(8,128)(2,1)S(1)}, u32[]{:S(2)}, u32[]{:S(2)}) collective-permute-start(bf16[512,2304]{1,0:T(8,128)(2,1)} %get-tuple-element.96), channel_id=1, source_target_pairs={{0,4},{4,0},{1,5},{5,1},{2,6},{6,2},{3,7},{7,3},{8,12},{12,8},{9,1... | collective-permute-start | bytes 7077896 | tf_op jit(solution)/shard_map/ppermute | solution.py:106
  390.3 32.1 %collective-permute-start.18 = (bf16[2,288,2304]{2,1,0:T(8,128)(2,1)S(1)}, bf16[2,288,2304]{2,1,0:T(8,128)(2,1)S(1)}, u32[]{:S(2)}, u32[]{:S(2)}) collective-permute-start(bf16[2,288,2304]{2,1,0:T(8,128)(2,1)S(1)} %pad_maximum_fusion.2), channel_id=1, source_target_pairs={{0,8},{4,20},{8,0},{12,28},{16,24},{20,4},{24,16},{28,12},{1,9},{5... | collective-permute-start | bytes 7962632 | tf_op jit(solution)/shard_map/ppermute | solution.py:118
  404.5 60.6 %collective-permute-start.20 = (bf16[2,288,2304]{2,1,0:T(8,128)(2,1)}, bf16[2,288,2304]{2,1,0:T(8,128)(2,1)}, u32[]{:S(2)}, u32[]{:S(2)}) collective-permute-start(bf16[2,288,2304]{2,1,0:T(8,128)(2,1)} %pad_maximum_fusion.3), channel_id=1, source_target_pairs={{0,8},{4,20},{8,0},{12,28},{16,24},{20,4},{24,16},{28,12},{1,9},{5... | collective-permute-start | bytes 7962632 | tf_op jit(solution)/shard_map/ppermute | solution.py:118
  418.0 76.3 %collective-permute-start.24 = (bf16[2,288,2304]{2,1,0:T(8,128)(2,1)}, bf16[2,288,2304]{2,1,0:T(8,128)(2,1)S(1)}, u32[]{:S(2)}, u32[]{:S(2)}) collective-permute-start(bf16[2,288,2304]{2,1,0:T(8,128)(2,1)} %pad_maximum_fusion.4), channel_id=1, source_target_pairs={{0,8},{4,20},{8,0},{12,28},{16,24},{20,4},{24,16},{28,12},{1,9},{5... | collective-permute-start | bytes 7962632 | tf_op jit(solution)/shard_map/ppermute | solution.py:118
  423.8 70.6 %collective-permute-start.22 = (bf16[288,2304]{1,0:T(8,128)(2,1)}, bf16[288,2304]{1,0:T(8,128)(2,1)}, u32[]{:S(2)}, u32[]{:S(2)}) collective-permute-start(bf16[288,2304]{1,0:T(8,128)(2,1)} %fusion.15.rest_0_), channel_id=1, source_target_pairs={{0,16},{4,12},{8,24},{12,4},{16,0},{20,28},{24,8},{28,20},{1,17},{... | collective-permute-start | bytes 3981320 | tf_op jit(solution)/shard_map/ppermute | solution.py:118
  490.7 68.8 %collective-permute-start.31 = (bf16[288,2304]{1,0:T(8,128)(2,1)}, bf16[288,2304]{1,0:T(8,128)(2,1)}, u32[]{:S(2)}, u32[]{:S(2)}) collective-permute-start(bf16[288,2304]{1,0:T(8,128)(2,1)} %fusion.14), channel_id=1, source_target_pairs={{0,16},{4,12},{8,24},{12,4},{16,0},{20,28},{24,8},{28,20},{1,17},{... | collective-permute-start | bytes 3981320 | tf_op jit(solution)/shard_map/ppermute | solution.py:118
  514.5 13.4 %collective-permute-start.28 = (bf16[512,1152]{0,1:T(8,128)(2,1)S(1)}, bf16[512,1152]{0,1:T(8,128)(2,1)S(1)}, u32[]{:S(2)}, u32[]{:S(2)}) collective-permute-start(bf16[512,1152]{0,1:T(8,128)(2,1)S(1)} %pad_maximum_fusion.10), channel_id=1, source_target_pairs={{0,4},{4,0},{1,5},{5,1},{2,6},{6,2},{3,7},{7,3},{8,12},{12,8},{9,1... | collective-permute-start | bytes 3538952 | tf_op jit(solution)/shard_map/ppermute | solution.py:106
  520.6 38.9 %collective-permute-start.32 = (bf16[288,2304]{1,0:T(8,128)(2,1)S(1)}, bf16[288,2304]{1,0:T(8,128)(2,1)S(1)}, u32[]{:S(2)}, u32[]{:S(2)}) collective-permute-start(bf16[288,2304]{1,0:T(8,128)(2,1)S(1)} %fusion.13), channel_id=1, source_target_pairs={{0,16},{4,12},{8,24},{12,4},{16,0},{20,28},{24,8},{28,20},{1,17},{... | collective-permute-start | bytes 3981320 | tf_op jit(solution)/shard_map/ppermute | solution.py:118
  521.4 29.7 %collective-permute-start.36 = (f32[4,2304]{1,0:T(4,128)S(1)}, f32[4,2304]{1,0:T(4,128)S(1)}, u32[]{:S(2)}, u32[]{:S(2)}) collective-permute-start(f32[4,2304]{1,0:T(4,128)S(1)} %add.247), channel_id=1, source_target_pairs={{0,1},{1,0},{2,3},{3,2},{4,5},{5,4},{6,7},{7,6},{8,9},{9,8},{10,11... | collective-permute-start | bytes 110600 | tf_op jit(solution)/shard_map/ppermute | solution.py:106
  526.9 25.9 %collective-permute-start.26 = (bf16[2,288,1024]{2,1,0:T(8,128)(2,1)}, bf16[2,288,1024]{2,1,0:T(8,128)(2,1)S(1)}, u32[]{:S(2)}, u32[]{:S(2)}) collective-permute-start(bf16[2,288,1024]{2,1,0:T(8,128)(2,1)} %pad_maximum_fusion.9), channel_id=1, source_target_pairs={{0,8},{4,20},{8,0},{12,28},{16,24},{20,4},{24,16},{28,12},{1,9},{5... | collective-permute-start | bytes 3538952 | tf_op jit(solution)/shard_map/ppermute | solution.py:118
  538.6 19.1 %collective-permute-start.29 = (bf16[2,288,512]{2,1,0:T(8,128)(2,1)}, bf16[2,288,512]{2,1,0:T(8,128)(2,1)}, u32[]{:S(2)}, u32[]{:S(2)}) collective-permute-start(bf16[2,288,512]{2,1,0:T(8,128)(2,1)} %pad_maximum_fusion.12), channel_id=1, source_target_pairs={{0,8},{4,20},{8,0},{12,28},{16,24},{20,4},{24,16},{28,12},{1,9},{5... | collective-permute-start | bytes 1769480 | tf_op jit(solution)/shard_map/ppermute | solution.py:118
  553.0 38.6 %collective-permute-start.27 = (bf16[288,1024]{1,0:T(8,128)(2,1)S(1)}, bf16[288,1024]{1,0:T(8,128)(2,1)}, u32[]{:S(2)}, u32[]{:S(2)}) collective-permute-start(bf16[288,1024]{1,0:T(8,128)(2,1)S(1)} %fusion.38), channel_id=1, source_target_pairs={{0,16},{4,12},{8,24},{12,4},{16,0},{20,28},{24,8},{28,20},{1,17},{... | collective-permute-start | bytes 1769480 | tf_op jit(solution)/shard_map/ppermute | solution.py:118
  558.7 27.6 %collective-permute-start.30 = (bf16[288,512]{1,0:T(8,128)(2,1)S(1)}, bf16[288,512]{1,0:T(8,128)(2,1)S(1)}, u32[]{:S(2)}, u32[]{:S(2)}) collective-permute-start(bf16[288,512]{1,0:T(8,128)(2,1)S(1)} %fusion.40), channel_id=1, source_target_pairs={{0,16},{4,12},{8,24},{12,4},{16,0},{20,28},{24,8},{28,20},{1,17},{... | collective-permute-start | bytes 884744 | tf_op jit(solution)/shard_map/ppermute | solution.py:118
  (58 other events, 666.0 us)
Sparse Core Ops, SparseCore 0:
  81.3 97.1 all-reduce.5
  236.8 97.2 all-reduce.7
  366.0 94.6 all-reduce.9
  508.0 95.4 all-reduce.11
Sparse Core Ops, SparseCore 1:
  84.1 84.5 all-gather.1

commit v6 on v5

--- a/solution.py
+++ b/solution.py
@@ -279,15 +279,18 @@
 
 
 def project_kernel(place, x, one, two, one_far, two_far, cosine, sine, *rest):
-    queries, pair, attn_in, gains, weight, sems = rest[-6:]
-    copies = fetch_rows(place, (one, two), (one_far, two_far), weight, sems, 0, weight.shape[1])
-    for copy in copies:
+    queries, pair, attn_in, gains, weight, tail, sems, tail_sems = rest[-8:]
+    parts = (one, two), (one_far, two_far)
+    width = (GROUP + 2) * HEAD_DIM
+    tail_copies = fetch_rows(
+        place, *parts, tail, tail_sems, width + GROUP * HEAD_DIM, tail.shape[1]
+    )
+    copies = fetch_rows(place, *parts, weight, sems, 0, width)
+    for copy in tail_copies + copies:
         copy.start()
-    for copy in copies:
+    for copy in tail_copies:
         copy.wait()
-    width = (GROUP + 2) * HEAD_DIM
-    tail = weight[:, width + GROUP * HEAD_DIM :].astype(jnp.float32)
-    gains[...] = jnp.transpose(tail)[:8]
+    gains[...] = jnp.transpose(tail[...].astype(jnp.float32))[:8]
     gain = 1.0 + gains[0:1, :]
     chunk = ROW_CHUNK
 
@@ -297,6 +300,8 @@
         stream = x[rows, :].astype(jnp.float32)
         attn_in[rows, :] = (stream * row_scale(stream) * gain).astype(jnp.bfloat16)
 
+    for copy in copies:
+        copy.wait()
     for member in range(GROUP + 2):
         columns = slice(member * HEAD_DIM, (member + 1) * HEAD_DIM)
         part = dot_nn(attn_in[...], weight[:, columns])
@@ -324,7 +329,12 @@
             shaped((tokens, width), bf16),
             shaped((8, width), jnp.float32),
         ],
-        scratch_shapes=[pltpu.VMEM((width, near[0].shape[2]), bf16), pltpu.SemaphoreType.DMA((8,))],
+        scratch_shapes=[
+            pltpu.VMEM((width, (GROUP + 2) * HEAD_DIM), bf16),
+            pltpu.VMEM((width, near[0].shape[2] - (2 * GROUP + 2) * HEAD_DIM), bf16),
+            pltpu.SemaphoreType.DMA((8,)),
+            pltpu.SemaphoreType.DMA((8,)),
+        ],
         compiler_params=kernel_params(),
         cost_estimate=cost(2 * tokens * width * 1024, 12_000_000),
         name="project",
@@ -665,7 +675,7 @@
         pulled, product = norm_pull(mid, row_scale(mid), gains[2:3, :], upstream)
         gain_out[1] += fold_rows(product)
         at_mid = top[rows, :].astype(jnp.float32) + pulled
-        grad_mid[rows, :] = at_mid
+        grad_mid[rows, :] = at_mid.astype(jnp.bfloat16)
         pulled, product = norm_pull(out, out_scale, gains[1:2, :], at_mid)
         gain_out[0] += fold_rows(product)
         grad_attn[rows, :] = pulled.astype(jnp.bfloat16)
@@ -697,7 +707,7 @@
             whole((2, 8, width)),
         ],
         out_shape=[
-            shaped((tokens, width), jnp.float32),
+            shaped((tokens, width), bf16),
             shaped((tokens, width), bf16),
             shaped((tokens, heads), bf16),
             shaped((2, 8, width), jnp.float32),
@@ -837,7 +847,7 @@
         stream = x[rows, :].astype(jnp.float32)
         upstream = grad_in[rows, :].astype(jnp.float32)
         pulled, _ = norm_pull(stream, row_scale(stream), gains[0:1, :], upstream)
-        result[rows, :] = grad_mid[rows, :] + pulled
+        result[rows, :] = grad_mid[rows, :].astype(jnp.float32) + pulled
 
 
 def stream_back(grad_in, x, gains, grad_mid, *earlier):

time: 627 us -> 625 us (level)
  no operation moved by 1% of the time
where the time goes in v6:
time: 625 us; the launch traced here: 617 us
  waiting for transfers between devices  231 us (37%)
  Pallas kernels  169 us (27%)
  local copies, waits for them, and re-layouts  80.8 us (13%)
  matrix products  43.9 us (7%)
  other arithmetic  41.2 us (7%)
  starting transfers between devices  34.3 us (5%)
  between operations  16.7 us (3%)
    ppermute x16, waiting for transfers between devices, trade(): return lax.ppermute(value, ('batch', 'seq'), pairs)  149 us
    psum x4, waiting for transfers between devices, tensor_sum(): return lax.psum(part, 'tensor')  70.2 us
    dot_general x5, matrix products, rows_product(): lax.dot_general(left, right, (((0,), (0,)), ((), ())), preferred_element_...  43.9 us
    pallas_call x4, Pallas kernels, adam(): pl.pallas_call(functools.partial(adam_kernel, len(grads), decay), grid=(s...  34.5 us
    pallas_call x1, Pallas kernels, ffn_back(): pl.pallas_call(ffn_back_kernel, in_specs=[spec_vmem()] * 3 + [spec_any()]...  26.1 us
    pallas_call x1, Pallas kernels, ffn_forward(): pl.pallas_call(ffn_kernel, in_specs=[spec_smem()] + [spec_vmem()] * 3 + [...  24.7 us
    ppermute x16, starting transfers between devices, trade(): return lax.ppermute(value, ('batch', 'seq'), pairs)  21.4 us
    unnamed x100, local copies, waits for them, and re-layouts  20.3 us
  transfers between devices with their start and end apart: 43, of which 17 were waited for; matrix products, arithmetic and copies ran while one was open for 24% of the time, Pallas kernels for 17%

profile of v6, /device:TPU:0, one launch (start us, length us, event | category | flops | bytes accessed | tf_op | source)
XLA Modules:
  0.0 617.1 jit_solution(681949140144151017)
XLA Ops:
  19.8 7.9 %collective-permute-done = bf16[288,1664]{1,0:T(8,128)(2,1)} collective-permute-done((bf16[288,1664]{1,0:T(8,128)(2,1)S(1)}, bf16[288,1664]{1,0:T(8,128)(2,1)}, u32[]{:S(2)}, u32[]{:S(2)}) %collective-permute-start) | collective-permute-done | bytes 958496 | tf_op jit(solution)/shard_map/ppermute | solution.py:118
  31.3 22.2 %collective-permute-done.1.two = bf16[2,288,1664]{2,1,0:T(8,128)(2,1)} collective-permute-done((bf16[2,288,1664]{2,1,0:T(8,128)(2,1)S(1)}, bf16[2,288,1664]{2,1,0:T(8,128)(2,1)}, u32[]{:S(2)}, u32[]{:S(2)}) %collective-permute-start.1) | collective-permute-done | bytes 1916960 | tf_op jit(solution)/shard_map/ppermute | solution.py:118
  57.9 10.0 %project.1 = (bf16[512,512]{1,0:T(8,128)(2,1)}, bf16[2,512,256]{2,1,0:T(8,128)(2,1)}, bf16[512,2304]{1,0:T(8,128)(2,1)}, f32[8,2304]{1,0:T(8,128)}) custom-call(s32[2]{0:T(128)} %pad_add_fusion.place, bf16[512,2304]{1,0:T(8,128)(2,1)} %bitcast.198, bf16[2,288,1664]{2,1,0:T(8,128)(2,1)} %copy-done.1, bf16[2,288,1664]{2,1,0:T(8,128)(2,1)} %collective-permute-done.1.two, ...), custom_call_target="tpu_custom_call" | custom-call | flops 2415919104 | bytes 12000000 | tf_op jit(solution)/shard_map/project/pallas_call | solution.py:319
  72.6 7.7 %attend.1 = (bf16[512,512]{1,0:T(8,128)(2,1)}, bf16[512,2304]{1,0:T(8,128)(2,1)}) custom-call(s32[2]{0:T(128)} %pad_add_fusion.place, bf16[512,512]{1,0:T(8,128)(2,1)} %get-tuple-element.75.queries, bf16[2,512,256]{2,1,0:T(8,128)(2,1)} %get-tuple-element.76.pair, bf16[2,512,256]{2,1,0:T(8,128)(2,1)} %copy-done.46, bf16[2,288,1664]{2,1,0:T(8,128)(2,1)} %copy-done.1, ...), custom_call_target="tpu_custom_call" | custom-call | flops 4831838208 | bytes 8000000 | tf_op jit(solution)/shard_map/attend/pallas_call | solution.py:389
  84.9 23.2 %collective-permute-done.6 = bf16[288,2304]{1,0:T(8,128)(2,1)S(1)} collective-permute-done((bf16[288,2304]{1,0:T(8,128)(2,1)S(1)}, bf16[288,2304]{1,0:T(8,128)(2,1)S(1)}, u32[]{:S(2)}, u32[]{:S(2)}) %collective-permute-start.6) | collective-permute-done | bytes 1327136 | tf_op jit(solution)/shard_map/ppermute | solution.py:118
  114.4 55.1 %collective-permute-done.11.rest_5_.two = bf16[2,288,2304]{2,1,0:T(8,128)(2,1)S(1)} collective-permute-done((bf16[2,288,2304]{2,1,0:T(8,128)(2,1)S(1)}, bf16[2,288,2304]{2,1,0:T(8,128)(2,1)S(1)}, u32[]{:S(2)}, u32[]{:S(2)}) %collective-permute-start.11) | collective-permute-done | bytes 2654240 | tf_op jit(solution)/shard_map/ppermute | solution.py:118
  170.4 27.7 %collective-permute-done.9.rest_1_.two = bf16[2,288,2304]{2,1,0:T(8,128)(2,1)} collective-permute-done((bf16[2,288,2304]{2,1,0:T(8,128)(2,1)S(1)}, bf16[2,288,2304]{2,1,0:T(8,128)(2,1)}, u32[]{:S(2)}, u32[]{:S(2)}) %collective-permute-start.9) | collective-permute-done | bytes 2654240 | tf_op jit(solution)/shard_map/ppermute | solution.py:118
  198.6 4.9 collective-permute-done.10.rest_3_.two_far
  203.5 24.7 %ffn_forward.1 = (bf16[512,2304]{1,0:T(8,128)(2,1)}, bf16[512,2304]{1,0:T(8,128)(2,1)}, bf16[512,2304]{1,0:T(8,128)(2,1)}, bf16[512,2304]{1,0:T(8,128)(2,1)}, bf16[512,2304]{1,0:T(8,128)(2,1)}) custom-call(s32[2]{0:T(128)} %pad_add_fusion.place, bf16[512,2304]{1,0:T(8,128)(2,1)} %all-reduce.6.cloned.1.call-done.attn_out, bf16[512,2304]{1,0:T(8,128)(2,1)} %bitcast.199, ...), custom_call_target="tpu_custom_call" | custom-call | flops 16307453952 | bytes 50000000 | tf_op jit(solution)/shard_map/ffn_forward/pallas_call | solution.py:502
  231.6 4.3 copy.73
  252.2 8.8 %arrange.3.down = bf16[2304,2304]{1,0:T(8,128)(2,1)} custom-call(s32[2]{0:T(128)} %pad_add_fusion.place, bf16[2,288,2304]{2,1,0:T(8,128)(2,1)} %copy-done.6, bf16[2,288,2304]{2,1,0:T(8,128)(2,1)} %copy-done.20, bf16[2,288,2304]{2,1,0:T(8,128)(2,1)} %copy-done.19, bf16[2,288,2304]{2,1,0:T(8,128)(2,1)} %collective-permute-done.12.rest_7_.two_far), custom_call_target="tpu_custom_call" | custom-call | bytes 21233664 | tf_op jit(solution)/shard_map/arrange/pallas_call | solution.py:269
  264.6 3.9 concatenate.84
  269.2 8.8 %arrange.2.gate = bf16[2304,2304]{1,0:T(8,128)(2,1)} custom-call(s32[2]{0:T(128)} %pad_add_fusion.place, bf16[2,288,2304]{2,1,0:T(8,128)(2,1)} %copy-done.5, bf16[2,288,2304]{2,1,0:T(8,128)(2,1)} %collective-permute-done.9.rest_1_.two, bf16[2,288,2304]{2,1,0:T(8,128)(2,1)} %copy-done.18, bf16[2,288,2304]{2,1,0:T(8,128)(2,1)} %collective-permute-done.10.rest_3_.two_far), custom_call_target="tpu_custom_call" | custom-call | bytes 21233664 | tf_op jit(solution)/shard_map/arrange/pallas_call | solution.py:269
  299.6 33.7 %all-reduce.8.cloned.1.call-done.ffn_out = bf16[512,2304]{1,0:T(8,128)(2,1)} async-done(((bf16[512,2304]{1,0:T(8,128)(2,1)}), bf16[512,2304]{1,0:T(8,128)(2,1)}) %all-reduce.8.cloned.1.call-update) | async-done | bytes 2359312 | tf_op jit(solution)/shard_map/psum | solution.py:101
  333.4 26.1 %ffn_back.1 = (bf16[512,2304]{1,0:T(8,128)(2,1)}, bf16[512,2304]{1,0:T(8,128)(2,1)}, bf16[512,2304]{1,0:T(8,128)(2,1)}, f32[8,2304]{1,0:T(8,128)}, bf16[512,2304]{1,0:T(8,128)(2,1)}) custom-call(bf16[512,2304]{1,0:T(8,128)(2,1)} %all-reduce.8.cloned.1.call-done.ffn_out, bf16[512,2304]{1,0:T(8,128)(2,1)} %bitcast.225, f32[8,2304]{1,0:T(8,128)} %get-tuple-element.79.gains, ...), custom_call_target="tpu_custom_call" | custom-call | flops 16307453952 | bytes 55000000 | tf_op jit(solution)/shard_map/ffn_back/pallas_call | solution.py:625
  368.3 5.0 fusion.16
  373.3 14.7 %convolution_convert_fusion.2 = bf16[1152,2304]{1,0:T(8,128)(2,1)S(1)} fusion(bf16[1024,2304]{1,0:T(8,128)(2,1)} %constant_dynamic-update-slice_fusion.2.rest_3_, bf16[512,1152]{0,1:T(8,128)(2,1)} %collective-permute-done.17, bf16[512,288]{0,1:T(8,128)(2,1)S(1)} %copy-done.35, bf16[512,288]{0,1:T(8,128)(2,1)S(1)} %copy-done.36, ...), kind=kOutput, calls=%fused_computation.2 | convolution fusion | flops 5450268672 | bytes 12386304 | tf_op jit(solution)/shard_map/dot_general | solution.py:82
  391.1 8.2 %convolution_convert_fusion.1 = bf16[1152,2304]{1,0:T(8,128)(2,1)S(1)} fusion(bf16[512,2304]{1,0:T(8,128)(2,1)} %collective-permute-done.19, bf16[512,2304]{1,0:T(8,128)(2,1)S(1)} %copy-done.44, bf16[512,1152]{1,0:T(8,128)(2,1)} %collective-permute-done.15, bf16[512,1152]{1,0:T(8,128)(2,1)S(1)} %concatenate.86), kind=kOutput, calls=%fused_computation.1 | convolution fusion | flops 5452627968 | bytes 12386304 | tf_op jit(solution)/shard_map/dot_general | solution.py:82
  405.1 7.7 %convolution_convert_fusion = bf16[1152,2304]{1,0:T(8,128)(2,1)S(1)} fusion(bf16[512,2304]{1,0:T(8,128)(2,1)S(1)} %collective-permute-done.23, bf16[512,2304]{1,0:T(8,128)(2,1)S(1)} %copy-done.43, bf16[512,1152]{1,0:T(8,128)(2,1)} %collective-permute-done.15, bf16[512,1152]{1,0:T(8,128)(2,1)S(1)} %concatenate.86), kind=kOutput, calls=%fused_computation | convolution fusion | flops 5452627968 | bytes 12386304 | tf_op jit(solution)/shard_map/dot_general | solution.py:82
  425.5 34.5 %all-reduce.10.cloned.1.call-done.grad_in = bf16[512,2304]{1,0:T(8,128)(2,1)} async-done(((bf16[512,2304]{1,0:T(8,128)(2,1)}), bf16[512,2304]{1,0:T(8,128)(2,1)}) %all-reduce.10.cloned.1.call-update) | async-done | bytes 2359312 | tf_op jit(solution)/shard_map/psum | solution.py:101
  460.0 4.5 collective-permute-done.20.rest_1_
  464.5 11.1 %mid_back.1 = (bf16[512,2304]{1,0:T(8,128)(2,1)}, bf16[512,2304]{1,0:T(8,128)(2,1)}, bf16[512,512]{1,0:T(8,128)(2,1)}, f32[2,8,2304]{2,1,0:T(8,128)}) custom-call(s32[2]{0:T(128)} %pad_add_fusion.place, bf16[512,2304]{1,0:T(8,128)(2,1)} %all-reduce.10.cloned.1.call-done.grad_in, bf16[512,2304]{1,0:T(8,128)(2,1)} %bitcast.200, ...), custom_call_target="tpu_custom_call" | custom-call | flops 1207959552 | bytes 24000000 | tf_op jit(solution)/shard_map/mid_back/pallas_call | solution.py:696
  475.6 9.6 %attend_back.1 = (bf16[512,512]{1,0:T(8,128)(2,1)}, f32[2,512,256]{2,1,0:T(8,128)}, bf16[2,512,256]{2,1,0:T(8,128)(2,1)}) custom-call(s32[2]{0:T(128)} %pad_add_fusion.place, bf16[512,512]{1,0:T(8,128)(2,1)} %get-tuple-element.75.queries, bf16[2,512,256]{2,1,0:T(8,128)(2,1)} %get-tuple-element.76.pair, bf16[2,512,256]{2,1,0:T(8,128)(2,1)} %copy-done.46, ...), custom_call_target="tpu_custom_call" | custom-call | flops 5368709120 | bytes 5000000 | tf_op jit(solution)/shard_map/attend_back/pallas_call | solution.py:769
  495.0 10.8 %project_back.1 = (bf16[512,1024]{1,0:T(8,128)(2,1)}, bf16[512,2304]{1,0:T(8,128)(2,1)}, f32[8,2304]{1,0:T(8,128)}) custom-call(s32[2]{0:T(128)} %pad_add_fusion.place, bf16[512,512]{1,0:T(8,128)(2,1)} %get-tuple-element.93.grad_q, f32[2,512,256]{2,1,0:T(8,128)} %get-tuple-element.94.grad_own, bf16[2,512,256]{2,1,0:T(8,128)(2,1)} %copy-done.32, ...), custom_call_target="tpu_custom_call" | custom-call | flops 2415919104 | bytes 14000000 | tf_op jit(solution)/shard_map/project_back/pallas_call | solution.py:821
  520.5 4.2 convolution_convert_fusion.3
  526.8 9.0 %convolution_convert_fusion.4 = bf16[1152,512]{1,0:T(8,128)(2,1)S(1)} fusion(bf16[1024,512]{1,0:T(8,128)(2,1)} %constant_dynamic-update-slice_fusion.rest_0_, bf16[512,1152]{0,1:T(8,128)(2,1)S(1)} %collective-permute-done.28, bf16[512,288]{0,1:T(8,128)(2,1)S(1)} %get-tuple-element.190, bf16[512,288]{0,1:T(8,128)(2,1)S(1)} %get-tuple-element.191, ...), kind=kOutput, calls=%fused_computation.22 | convolution fusion | flops 1220345856 | bytes 4587520 | tf_op jit(solution)/shard_map/dot_general | solution.py:82
  539.7 10.3 %adam.7 = (f32[288,2304]{1,0:T(8,128)}, f32[288,2304]{1,0:T(8,128)}, f32[288,2304]{1,0:T(8,128)}, f32[288,2304]{1,0:T(8,128)}) custom-call(bf16[288,2304]{1,0:T(8,128)(2,1)} %get-tuple-element.107.refs_0_, bf16[288,2304]{1,0:T(8,128)(2,1)} %slice_bitcast_fusion.2.refs_1_, bf16[288,2304]{1,0:T(8,128)(2,1)} %collective-permute-done.22.rest_0_.refs_2_, ...), custom_call_target="tpu_custom_call" | custom-call | bytes 200000000 | tf_op jit(solution)/shard_map/adam/pallas_call | solution.py:929
  559.5 9.6 %join.1 = f32[288,2,2304]{2,1,0:T(2,128)} custom-call(bf16[288,2304]{1,0:T(8,128)(2,1)} %get-tuple-element.177.refs_0_, bf16[288,2304]{1,0:T(8,128)(2,1)} %slice_bitcast_fusion.1.refs_1_, bf16[288,2304]{1,0:T(8,128)(2,1)} %collective-permute-done.31.refs_2_, bf16[288,2304]{1,0:T(8,128)(2,1)} %get-tuple-element.174.refs_3_, ...), custom_call_target="tpu_custom_call" | custom-call | bytes 200000000 | tf_op jit(solution)/shard_map/join/pallas_call | solution.py:900
  569.1 14.4 %adam.6 = (f32[10368,128]{1,0:T(8,128)}, f32[10368,128]{1,0:T(8,128)}, f32[10368,128]{1,0:T(8,128)}) custom-call(f32[10368,128]{1,0:T(8,128)} %bitcast.203, f32[10368,128]{1,0:T(8,128)} %bitcast.204, f32[10368,128]{1,0:T(8,128)} %bitcast.212, f32[10368,128]{1,0:T(8,128)} %bitcast.213), custom_call_target="tpu_custom_call" | custom-call | bytes 200000000 | tf_op jit(solution)/shard_map/adam/pallas_call | solution.py:929
  585.9 4.5 adam.5
  595.3 5.2 adam.4
  602.4 7.0 %stream_back.1 = f32[512,2304]{1,0:T(8,128)} custom-call(bf16[512,2304]{1,0:T(8,128)(2,1)} %all-reduce.12.cloned.1.call-done.grad_in, bf16[512,2304]{1,0:T(8,128)(2,1)} %bitcast.202, f32[8,2304]{1,0:T(8,128)} %get-tuple-element.79.gains, bf16[512,2304]{1,0:T(8,128)(2,1)} %get-tuple-element.98.grad_mid, f32[288,1,1024]{2,1,0:T(1,128)} %bitcast.244, ...), custom_call_target="tpu_custom_call" | custom-call | flops 23592960 | bytes 14000000 | tf_op jit(solution)/shard_map/stream_back/pallas_call | solution.py:857
  (263 shorter events, 160.7 us)
Async XLA Ops:
  8.0 190.5 %all-reduce.6.cloned.1.call-start = ((), (), s32[]{:S(2)}) async-start(), calls=%async_computation | async-start | bytes 4718592 | tf_op jit(solution)/shard_map/psum | solution.py:101
  12.7 14.9 %collective-permute-start = (bf16[288,1664]{1,0:T(8,128)(2,1)S(1)}, bf16[288,1664]{1,0:T(8,128)(2,1)}, u32[]{:S(2)}, u32[]{:S(2)}) collective-permute-start(bf16[288,1664]{1,0:T(8,128)(2,1)S(1)} %pad_maximum_fusion.11), channel_id=1, source_target_pairs={{0,8},{4,20},{8,0},{12,28},{16,24},{20,4},{24,16},{28,12},{1,9},{5... | collective-permute-start | bytes 2875400 | tf_op jit(solution)/shard_map/ppermute | solution.py:118
  29.2 24.3 %collective-permute-start.1 = (bf16[2,288,1664]{2,1,0:T(8,128)(2,1)S(1)}, bf16[2,288,1664]{2,1,0:T(8,128)(2,1)}, u32[]{:S(2)}, u32[]{:S(2)}) collective-permute-start(bf16[2,288,1664]{2,1,0:T(8,128)(2,1)S(1)} %pad_maximum_fusion.7.one), channel_id=1, source_target_pairs={{0,16},{4,12},{8,24},{12,4},{16,0},{20,28},{24,8},{28,20},{1,17},{... | collective-permute-start | bytes 5750792 | tf_op jit(solution)/shard_map/ppermute | solution.py:118
  31.3 26.6 %collective-permute-start.2 = (bf16[2,288,1664]{2,1,0:T(8,128)(2,1)S(1)}, bf16[2,288,1664]{2,1,0:T(8,128)(2,1)}, u32[]{:S(2)}, u32[]{:S(2)}) collective-permute-start(bf16[2,288,1664]{2,1,0:T(8,128)(2,1)S(1)} %pad_maximum_fusion.7.one), channel_id=1, source_target_pairs={{0,4},{4,0},{1,5},{5,1},{2,6},{6,2},{3,7},{7,3},{8,12},{12,8},{9,1... | collective-permute-start | bytes 5750792 | tf_op jit(solution)/shard_map/ppermute | solution.py:106
  53.5 18.1 %collective-permute-start.5 = (bf16[288,2304]{1,0:T(8,128)(2,1)}, bf16[288,2304]{1,0:T(8,128)(2,1)}, u32[]{:S(2)}, u32[]{:S(2)}) collective-permute-start(bf16[288,2304]{1,0:T(8,128)(2,1)} %bitcast_convert_fusion), channel_id=1, source_target_pairs={{0,8},{4,20},{8,0},{12,28},{16,24},{20,4},{24,16},{28,12},{1,9},{5... | collective-permute-start | bytes 3981320 | tf_op jit(solution)/shard_map/ppermute | solution.py:118
  80.4 123.1 %all-gather.2.cloned.1.call-start = ((), (), s32[]{:S(2)}) async-start(), calls=%async_computation.1 | async-start | bytes 11943936 | tf_op jit(solution)/shard_map/all_gather | solution.py:985
  80.9 252.4 %all-reduce.8.cloned.1.call-start = ((), (), s32[]{:S(2)}) async-start(), calls=%async_computation.2 | async-start | bytes 4718592 | tf_op jit(solution)/shard_map/psum | solution.py:101
  81.2 26.8 %collective-permute-start.6 = (bf16[288,2304]{1,0:T(8,128)(2,1)S(1)}, bf16[288,2304]{1,0:T(8,128)(2,1)S(1)}, u32[]{:S(2)}, u32[]{:S(2)}) collective-permute-start(bf16[288,2304]{1,0:T(8,128)(2,1)S(1)} %get-tuple-element.80), channel_id=1, source_target_pairs={{0,8},{4,20},{8,0},{12,28},{16,24},{20,4},{24,16},{28,12},{1,9},{5... | collective-permute-start | bytes 3981320 | tf_op jit(solution)/shard_map/ppermute | solution.py:118
  84.7 24.8 %collective-permute-start.7 = (bf16[2,288,2304]{2,1,0:T(8,128)(2,1)S(1)}, bf16[2,288,2304]{2,1,0:T(8,128)(2,1)S(1)}, u32[]{:S(2)}, u32[]{:S(2)}) collective-permute-start(bf16[2,288,2304]{2,1,0:T(8,128)(2,1)S(1)} %pad_maximum_fusion.1.rest_4_.one), channel_id=1, source_target_pairs={{0,4},{4,0},{1,5},{5,1},{2,6},{6,2},{3,7},{7,3},{8,12},{12,8},{9,1... | collective-permute-start | bytes 7962632 | tf_op jit(solution)/shard_map/ppermute | solution.py:106
  108.4 61.2 %collective-permute-start.11 = (bf16[2,288,2304]{2,1,0:T(8,128)(2,1)S(1)}, bf16[2,288,2304]{2,1,0:T(8,128)(2,1)S(1)}, u32[]{:S(2)}, u32[]{:S(2)}) collective-permute-start(bf16[2,288,2304]{2,1,0:T(8,128)(2,1)S(1)} %pad_maximum_fusion.1.rest_4_.one), channel_id=1, source_target_pairs={{0,16},{4,12},{8,24},{12,4},{16,0},{20,28},{24,8},{28,20},{1,17},{... | collective-permute-start | bytes 7962632 | tf_op jit(solution)/shard_map/ppermute | solution.py:118
  113.3 84.8 %collective-permute-start.9 = (bf16[2,288,2304]{2,1,0:T(8,128)(2,1)S(1)}, bf16[2,288,2304]{2,1,0:T(8,128)(2,1)}, u32[]{:S(2)}, u32[]{:S(2)}) collective-permute-start(bf16[2,288,2304]{2,1,0:T(8,128)(2,1)S(1)} %pad_maximum_fusion.rest_0_.one), channel_id=1, source_target_pairs={{0,16},{4,12},{8,24},{12,4},{16,0},{20,28},{24,8},{28,20},{1,17},{... | collective-permute-start | bytes 7962632 | tf_op jit(solution)/shard_map/ppermute | solution.py:118
  169.6 29.0 %collective-permute-start.12 = (bf16[2,288,2304]{2,1,0:T(8,128)(2,1)S(1)}, bf16[2,288,2304]{2,1,0:T(8,128)(2,1)}, u32[]{:S(2)}, u32[]{:S(2)}) collective-permute-start(bf16[2,288,2304]{2,1,0:T(8,128)(2,1)S(1)} %collective-permute-done.11.rest_5_.two), channel_id=1, source_target_pairs={{0,4},{4,0},{1,5},{5,1},{2,6},{6,2},{3,7},{7,3},{8,12},{12,8},{9,1... | collective-permute-start | bytes 7962632 | tf_op jit(solution)/shard_map/ppermute | solution.py:106
  228.2 68.2 %collective-permute-start.16 = (bf16[512,2304]{1,0:T(8,128)(2,1)}, bf16[512,2304]{1,0:T(8,128)(2,1)}, u32[]{:S(2)}, u32[]{:S(2)}) collective-permute-start(bf16[512,2304]{1,0:T(8,128)(2,1)} %get-tuple-element.88), channel_id=1, source_target_pairs={{0,4},{4,0},{1,5},{5,1},{2,6},{6,2},{3,7},{7,3},{8,12},{12,8},{9,1... | collective-permute-start | bytes 7077896 | tf_op jit(solution)/shard_map/ppermute | solution.py:106
  228.6 21.7 %collective-permute-start.13 = (bf16[512,512]{1,0:T(8,128)(2,1)}, bf16[512,512]{1,0:T(8,128)(2,1)}, u32[]{:S(2)}, u32[]{:S(2)}) collective-permute-start(bf16[512,512]{1,0:T(8,128)(2,1)} %get-tuple-element.83.attended), channel_id=1, source_target_pairs={{0,4},{4,0},{1,5},{5,1},{2,6},{6,2},{3,7},{7,3},{8,12},{12,8},{9,1... | collective-permute-start | bytes 1572872 | tf_op jit(solution)/shard_map/ppermute | solution.py:106
  235.9 224.1 %all-reduce.10.cloned.1.call-start = ((), (), s32[]{:S(2)}) async-start(), calls=%async_computation.3 | async-start | bytes 4718592 | tf_op jit(solution)/shard_map/psum | solution.py:101
  246.5 44.1 %collective-permute-start.15 = (bf16[512,1152]{1,0:T(8,128)(2,1)}, bf16[512,1152]{1,0:T(8,128)(2,1)}, u32[]{:S(2)}, u32[]{:S(2)}) collective-permute-start(bf16[512,1152]{1,0:T(8,128)(2,1)} %concatenate.87), channel_id=1, source_target_pairs={{0,4},{4,0},{1,5},{5,1},{2,6},{6,2},{3,7},{7,3},{8,12},{12,8},{9,1... | collective-permute-start | bytes 3538952 | tf_op jit(solution)/shard_map/ppermute | solution.py:106
  268.5 25.0 %collective-permute-start.14 = (bf16[512,1152]{1,0:T(8,128)(2,1)}, bf16[512,1152]{1,0:T(8,128)(2,1)}, u32[]{:S(2)}, u32[]{:S(2)}) collective-permute-start(bf16[512,1152]{1,0:T(8,128)(2,1)} %concatenate.84), channel_id=1, source_target_pairs={{0,4},{4,0},{1,5},{5,1},{2,6},{6,2},{3,7},{7,3},{8,12},{12,8},{9,1... | collective-permute-start | bytes 3538952 | tf_op jit(solution)/shard_map/ppermute | solution.py:106
  359.5 31.5 %collective-permute-start.19 = (bf16[512,2304]{1,0:T(8,128)(2,1)}, bf16[512,2304]{1,0:T(8,128)(2,1)}, u32[]{:S(2)}, u32[]{:S(2)}) collective-permute-start(bf16[512,2304]{1,0:T(8,128)(2,1)} %get-tuple-element.91), channel_id=1, source_target_pairs={{0,4},{4,0},{1,5},{5,1},{2,6},{6,2},{3,7},{7,3},{8,12},{12,8},{9,1... | collective-permute-start | bytes 7077896 | tf_op jit(solution)/shard_map/ppermute | solution.py:106
  365.2 237.3 %all-reduce.12.cloned.1.call-start = ((), (), s32[]{:S(2)}) async-start(), calls=%async_computation.4 | async-start | bytes 4718592 | tf_op jit(solution)/shard_map/psum | solution.py:101
  365.2 39.9 %collective-permute-start.23 = (bf16[512,2304]{1,0:T(8,128)(2,1)}, bf16[512,2304]{1,0:T(8,128)(2,1)S(1)}, u32[]{:S(2)}, u32[]{:S(2)}) collective-permute-start(bf16[512,2304]{1,0:T(8,128)(2,1)} %get-tuple-element.96), channel_id=1, source_target_pairs={{0,4},{4,0},{1,5},{5,1},{2,6},{6,2},{3,7},{7,3},{8,12},{12,8},{9,1... | collective-permute-start | bytes 7077896 | tf_op jit(solution)/shard_map/ppermute | solution.py:106
  389.6 32.1 %collective-permute-start.18 = (bf16[2,288,2304]{2,1,0:T(8,128)(2,1)S(1)}, bf16[2,288,2304]{2,1,0:T(8,128)(2,1)S(1)}, u32[]{:S(2)}, u32[]{:S(2)}) collective-permute-start(bf16[2,288,2304]{2,1,0:T(8,128)(2,1)S(1)} %pad_maximum_fusion.2), channel_id=1, source_target_pairs={{0,8},{4,20},{8,0},{12,28},{16,24},{20,4},{24,16},{28,12},{1,9},{5... | collective-permute-start | bytes 7962632 | tf_op jit(solution)/shard_map/ppermute | solution.py:118
  403.8 60.6 %collective-permute-start.20 = (bf16[2,288,2304]{2,1,0:T(8,128)(2,1)}, bf16[2,288,2304]{2,1,0:T(8,128)(2,1)}, u32[]{:S(2)}, u32[]{:S(2)}) collective-permute-start(bf16[2,288,2304]{2,1,0:T(8,128)(2,1)} %pad_maximum_fusion.3), channel_id=1, source_target_pairs={{0,8},{4,20},{8,0},{12,28},{16,24},{20,4},{24,16},{28,12},{1,9},{5... | collective-permute-start | bytes 7962632 | tf_op jit(solution)/shard_map/ppermute | solution.py:118
  417.4 76.0 %collective-permute-start.24 = (bf16[2,288,2304]{2,1,0:T(8,128)(2,1)}, bf16[2,288,2304]{2,1,0:T(8,128)(2,1)S(1)}, u32[]{:S(2)}, u32[]{:S(2)}) collective-permute-start(bf16[2,288,2304]{2,1,0:T(8,128)(2,1)} %pad_maximum_fusion.4), channel_id=1, source_target_pairs={{0,8},{4,20},{8,0},{12,28},{16,24},{20,4},{24,16},{28,12},{1,9},{5... | collective-permute-start | bytes 7962632 | tf_op jit(solution)/shard_map/ppermute | solution.py:118
  423.1 70.3 %collective-permute-start.22 = (bf16[288,2304]{1,0:T(8,128)(2,1)}, bf16[288,2304]{1,0:T(8,128)(2,1)}, u32[]{:S(2)}, u32[]{:S(2)}) collective-permute-start(bf16[288,2304]{1,0:T(8,128)(2,1)} %fusion.15.rest_0_), channel_id=1, source_target_pairs={{0,16},{4,12},{8,24},{12,4},{16,0},{20,28},{24,8},{28,20},{1,17},{... | collective-permute-start | bytes 3981320 | tf_op jit(solution)/shard_map/ppermute | solution.py:118
  489.6 68.8 %collective-permute-start.31 = (bf16[288,2304]{1,0:T(8,128)(2,1)}, bf16[288,2304]{1,0:T(8,128)(2,1)}, u32[]{:S(2)}, u32[]{:S(2)}) collective-permute-start(bf16[288,2304]{1,0:T(8,128)(2,1)} %fusion.14), channel_id=1, source_target_pairs={{0,16},{4,12},{8,24},{12,4},{16,0},{20,28},{24,8},{28,20},{1,17},{... | collective-permute-start | bytes 3981320 | tf_op jit(solution)/shard_map/ppermute | solution.py:118
  513.4 13.4 %collective-permute-start.28 = (bf16[512,1152]{0,1:T(8,128)(2,1)S(1)}, bf16[512,1152]{0,1:T(8,128)(2,1)S(1)}, u32[]{:S(2)}, u32[]{:S(2)}) collective-permute-start(bf16[512,1152]{0,1:T(8,128)(2,1)S(1)} %pad_maximum_fusion.10), channel_id=1, source_target_pairs={{0,4},{4,0},{1,5},{5,1},{2,6},{6,2},{3,7},{7,3},{8,12},{12,8},{9,1... | collective-permute-start | bytes 3538952 | tf_op jit(solution)/shard_map/ppermute | solution.py:106
  519.5 38.9 %collective-permute-start.32 = (bf16[288,2304]{1,0:T(8,128)(2,1)S(1)}, bf16[288,2304]{1,0:T(8,128)(2,1)S(1)}, u32[]{:S(2)}, u32[]{:S(2)}) collective-permute-start(bf16[288,2304]{1,0:T(8,128)(2,1)S(1)} %fusion.13), channel_id=1, source_target_pairs={{0,16},{4,12},{8,24},{12,4},{16,0},{20,28},{24,8},{28,20},{1,17},{... | collective-permute-start | bytes 3981320 | tf_op jit(solution)/shard_map/ppermute | solution.py:118
  520.4 29.7 %collective-permute-start.36 = (f32[4,2304]{1,0:T(4,128)S(1)}, f32[4,2304]{1,0:T(4,128)S(1)}, u32[]{:S(2)}, u32[]{:S(2)}) collective-permute-start(f32[4,2304]{1,0:T(4,128)S(1)} %add.247), channel_id=1, source_target_pairs={{0,1},{1,0},{2,3},{3,2},{4,5},{5,4},{6,7},{7,6},{8,9},{9,8},{10,11... | collective-permute-start | bytes 110600 | tf_op jit(solution)/shard_map/ppermute | solution.py:106
  525.9 25.9 %collective-permute-start.26 = (bf16[2,288,1024]{2,1,0:T(8,128)(2,1)}, bf16[2,288,1024]{2,1,0:T(8,128)(2,1)S(1)}, u32[]{:S(2)}, u32[]{:S(2)}) collective-permute-start(bf16[2,288,1024]{2,1,0:T(8,128)(2,1)} %pad_maximum_fusion.9), channel_id=1, source_target_pairs={{0,8},{4,20},{8,0},{12,28},{16,24},{20,4},{24,16},{28,12},{1,9},{5... | collective-permute-start | bytes 3538952 | tf_op jit(solution)/shard_map/ppermute | solution.py:118
  537.5 19.1 %collective-permute-start.29 = (bf16[2,288,512]{2,1,0:T(8,128)(2,1)}, bf16[2,288,512]{2,1,0:T(8,128)(2,1)}, u32[]{:S(2)}, u32[]{:S(2)}) collective-permute-start(bf16[2,288,512]{2,1,0:T(8,128)(2,1)} %pad_maximum_fusion.12), channel_id=1, source_target_pairs={{0,8},{4,20},{8,0},{12,28},{16,24},{20,4},{24,16},{28,12},{1,9},{5... | collective-permute-start | bytes 1769480 | tf_op jit(solution)/shard_map/ppermute | solution.py:118
  552.0 38.5 %collective-permute-start.27 = (bf16[288,1024]{1,0:T(8,128)(2,1)S(1)}, bf16[288,1024]{1,0:T(8,128)(2,1)}, u32[]{:S(2)}, u32[]{:S(2)}) collective-permute-start(bf16[288,1024]{1,0:T(8,128)(2,1)S(1)} %fusion.38), channel_id=1, source_target_pairs={{0,16},{4,12},{8,24},{12,4},{16,0},{20,28},{24,8},{28,20},{1,17},{... | collective-permute-start | bytes 1769480 | tf_op jit(solution)/shard_map/ppermute | solution.py:118
  557.6 27.6 %collective-permute-start.30 = (bf16[288,512]{1,0:T(8,128)(2,1)S(1)}, bf16[288,512]{1,0:T(8,128)(2,1)S(1)}, u32[]{:S(2)}, u32[]{:S(2)}) collective-permute-start(bf16[288,512]{1,0:T(8,128)(2,1)S(1)} %fusion.40), channel_id=1, source_target_pairs={{0,16},{4,12},{8,24},{12,4},{16,0},{20,28},{24,8},{28,20},{1,17},{... | collective-permute-start | bytes 884744 | tf_op jit(solution)/shard_map/ppermute | solution.py:118
  (58 other events, 665.0 us)
Sparse Core Ops, SparseCore 0:
  80.5 97.1 all-reduce.5
  236.0 97.2 all-reduce.7
  365.3 94.6 all-reduce.9
  507.0 95.4 all-reduce.11
Sparse Core Ops, SparseCore 1:
  83.3 84.5 all-gather.1
